TPU v7x, 32 devices: a whole 2x2x4 slice. The times are simulated.
32 devices in a mesh: dp: 16 (over z, y, core), fsdp: 2 (over x).
Axes of the slice: x: 2, y: 2, z: 4, core: 2. Of those that a mesh axis runs over, the one named last changes fastest.
Arguments:
- tokens: float32 [64, 1088, 1024], P(('dp', 'fsdp')), may hold values from -6 to 6
- cotangent: float32 [64, 1088, 1024], P(('dp', 'fsdp')), may hold values from -6 to 6
- group_ids: int32 [64], P(('dp', 'fsdp')), may hold values from 0 to 7
- counts: int32 [32], P(('dp', 'fsdp')), may hold values from 1 to 2, as said below
- w_qkv: float32 [1024, 3072], P('fsdp'), may hold values from -0.1875 to 0.1875
- w_proj: float32 [1024, 1024], P('fsdp'), may hold values from -0.75 to 0.75
- w_up: float32 [1024, 4096], P('fsdp'), may hold values from -0.1875 to 0.1875
- w_down: float32 [4096, 1024], P('fsdp'), may hold values from -0.09375 to 0.09375
- gains: float32 [4, 1024], P(None, 'fsdp'), may hold values from 0.25 to 1.75
- table: float32 [8, 1024], P(None, 'fsdp'), may hold values from -3 to 3
Outputs:
- output: float32 [64, 1088, 1024], P(('dp', 'fsdp'))
- grad_tokens: float32 [64, 1088, 1024], P(('dp', 'fsdp'))
- grad_qkv: float32 [1024, 3072], P('fsdp')
- grad_proj: float32 [1024, 1024], P('fsdp')
- grad_up: float32 [1024, 4096], P('fsdp')
- grad_down: float32 [4096, 1024], P('fsdp')
- grad_gains: float32 [4, 1024], P(None, 'fsdp')
- grad_table: float32 [8, 1024], P(None, 'fsdp')
Inputs may be any that keep to these rules, and one draw needn't show every extreme that they name: `counts`: the number of live slots of each device, which are its first ones; some device holds 2 and some holds 1.
All inputs are finite; a program needn't handle non-finite values.
Results may differ from a plain program's by a relative error of at most 0.012.
Values may be sent and summed in bfloat16 or wider, within the bound.
No kernel may reach another device: no remote copies, remote signals or barrier semaphores. Data moves between devices by JAX's collectives and lax.ppermute only.
A program may use at most 704 MiB of HBM per device.

v0:
```python
import math

import jax
import jax.numpy as jnp
from jax import lax
from jax.sharding import PartitionSpec as P

HEADS = 16
HEAD_DIM = 64


EPSILON = 1e-05
RELAX_ALPHA = 32.0


def norm_parts(hidden_rows):
    centered = hidden_rows - jnp.mean(hidden_rows, axis=-1, keepdims=True)
    variance = jnp.mean(centered * centered, axis=-1, keepdims=True)
    inv_std = lax.rsqrt(variance + EPSILON)
    return (centered * inv_std, inv_std)


def norm_back(gradient, hidden_rows, gain_vec):
    normed, inv_std = norm_parts(hidden_rows)
    grad_norm = gradient * gain_vec
    first_mean = jnp.mean(grad_norm, axis=-1, keepdims=True)
    second_mean = jnp.mean(grad_norm * normed, axis=-1, keepdims=True)
    grad_rows = inv_std * (grad_norm - first_mean - normed * second_mean)
    return (grad_rows, jnp.sum(gradient * normed, axis=0))


def block_plan(length):
    block_count = max(1, length // 512)
    return (block_count, length // block_count)


def causal_scores(queries, key_rows, start, head_dim):
    scores = jnp.einsum("qhd,khd->hqk", queries, key_rows, preferred_element_type=jnp.float32)
    row_index = start + lax.broadcasted_iota(jnp.int32, (1, scores.shape[1], scores.shape[2]), 1)
    col_index = lax.broadcasted_iota(jnp.int32, (1, scores.shape[1], scores.shape[2]), 2)
    return (scores * (1.0 / (RELAX_ALPHA * math.sqrt(head_dim))), row_index >= col_index)


def split_heads(packed, head_count, head_dim):
    length = packed.shape[0]
    width = head_count * head_dim
    queries = packed[:, :width].reshape(length, head_count, head_dim)
    key_rows = packed[:, width : 2 * width].reshape(length, head_count, head_dim)
    value_rows = packed[:, 2 * width :].reshape(length, head_count, head_dim)
    return (queries, key_rows, value_rows)


def attend_forward(packed, head_count, head_dim):
    length = packed.shape[0]
    queries, key_rows, value_rows = split_heads(packed, head_count, head_dim)
    block_count, block_rows = block_plan(length)

    def one_block(block_index):
        start = block_index * block_rows
        query_part = lax.dynamic_slice_in_dim(queries, start, block_rows, 0)
        relaxed, causal = causal_scores(query_part, key_rows, start, head_dim)
        relaxed = jnp.where(causal, relaxed, -1e30)
        maximum = jnp.max(relaxed, axis=-1, keepdims=True)
        expanded = jnp.exp((relaxed - maximum) * RELAX_ALPHA)
        row_totals = jnp.sum(expanded, axis=-1, keepdims=True)
        attn_probs = (expanded / row_totals).astype(jnp.bfloat16)
        mixture = jnp.einsum(
            "hqk,khd->qhd", attn_probs, value_rows, preferred_element_type=jnp.float32
        )
        return (mixture.astype(jnp.bfloat16), (maximum * RELAX_ALPHA + jnp.log(row_totals))[..., 0])

    mixture, log_totals = lax.map(one_block, jnp.arange(block_count))
    return (mixture.reshape(length, head_count * head_dim), log_totals)


def attend_back(packed, log_totals, grad_mix, head_count, head_dim):
    length = packed.shape[0]
    width = head_count * head_dim
    queries, key_rows, value_rows = split_heads(packed, head_count, head_dim)
    grad_heads = grad_mix.reshape(length, head_count, head_dim)
    block_count, block_rows = block_plan(length)
    score_scale = 1.0 / math.sqrt(head_dim)

    def one_block(carry, block_index):
        grad_keys, grad_values = carry
        start = block_index * block_rows
        query_part = lax.dynamic_slice_in_dim(queries, start, block_rows, 0)
        grad_part = lax.dynamic_slice_in_dim(grad_heads, start, block_rows, 0)
        relaxed, causal = causal_scores(query_part, key_rows, start, head_dim)
        logits = jnp.where(causal, relaxed * RELAX_ALPHA, -1e30)
        attn_probs = jnp.exp(logits - log_totals[block_index][..., None])
        grad_values = grad_values + jnp.einsum(
            "hqk,qhd->khd",
            attn_probs.astype(jnp.bfloat16),
            grad_part,
            preferred_element_type=jnp.float32,
        )
        grad_probs = jnp.einsum(
            "qhd,khd->hqk", grad_part, value_rows, preferred_element_type=jnp.float32
        )
        row_delta = jnp.sum(attn_probs * grad_probs, axis=-1, keepdims=True)
        grad_scores = (attn_probs * (grad_probs - row_delta) * score_scale).astype(jnp.bfloat16)
        grad_queries = jnp.einsum(
            "hqk,khd->qhd", grad_scores, key_rows, preferred_element_type=jnp.float32
        )
        grad_keys = grad_keys + jnp.einsum(
            "hqk,qhd->khd", grad_scores, query_part, preferred_element_type=jnp.float32
        )
        return ((grad_keys, grad_values), grad_queries)

    blank = jnp.zeros((length, head_count, head_dim), jnp.float32)
    (grad_keys, grad_values), grad_queries = lax.scan(
        one_block, (blank, blank), jnp.arange(block_count)
    )
    return jnp.concatenate(
        [
            grad_queries.reshape(length, width),
            grad_keys.reshape(length, width),
            grad_values.reshape(length, width),
        ],
        axis=1,
    )


def group_onehot(group_id, group_total):
    return (jnp.arange(group_total) == group_id).astype(jnp.float32)


def forward_slot(token_rows, group_id, weight_set):
    w_qkv, w_proj, w_up, w_down, gain_rows, table_rows = weight_set
    gain_vals = gain_rows.astype(jnp.float32)
    onehot = group_onehot(group_id, table_rows.shape[0])
    added = jnp.dot(onehot[None, :], table_rows.astype(jnp.float32))
    start_rows = token_rows + added
    normed_one = (norm_parts(start_rows)[0] * gain_vals[0]).astype(jnp.bfloat16)
    packed = jnp.dot(normed_one, w_qkv, preferred_element_type=jnp.float32).astype(jnp.bfloat16)
    mixture, log_totals = attend_forward(packed, HEADS, HEAD_DIM)
    projected = jnp.dot(mixture, w_proj, preferred_element_type=jnp.float32)
    middle = start_rows + norm_parts(projected)[0] * gain_vals[1]
    normed_two = (norm_parts(middle)[0] * gain_vals[2]).astype(jnp.bfloat16)
    up_rows = jnp.dot(normed_two, w_up, preferred_element_type=jnp.float32)
    activated = jax.nn.gelu(up_rows, approximate=False).astype(jnp.bfloat16)
    down_rows = jnp.dot(activated, w_down, preferred_element_type=jnp.float32)
    result = middle + norm_parts(down_rows)[0] * gain_vals[3]
    kept = (
        start_rows,
        normed_one,
        packed,
        log_totals,
        mixture,
        projected,
        middle,
        normed_two,
        up_rows,
        activated,
        down_rows,
    )
    return (result, kept)


def blank_slot(length, width, hidden_width):
    block_count, block_rows = block_plan(length)
    float_rows = jnp.zeros((length, width), jnp.float32)
    half_rows = jnp.zeros((length, width), jnp.bfloat16)
    kept = (
        float_rows,
        half_rows,
        jnp.zeros((length, 3 * width), jnp.bfloat16),
        jnp.zeros((block_count, HEADS, block_rows), jnp.float32),
        half_rows,
        float_rows,
        float_rows,
        half_rows,
        jnp.zeros((length, hidden_width), jnp.float32),
        jnp.zeros((length, hidden_width), jnp.bfloat16),
        float_rows,
    )
    return (float_rows, kept)


def backward_slot(grad_rows, group_id, kept, weight_set):
    w_qkv, w_proj, w_up, w_down, gain_rows, table_rows = weight_set
    gain_vals = gain_rows.astype(jnp.float32)
    (
        start_rows,
        normed_one,
        packed,
        log_totals,
        mixture,
        projected,
        middle,
        normed_two,
        up_rows,
        activated,
        down_rows,
    ) = kept
    grad_down_rows, grad_gain_four = norm_back(grad_rows, down_rows, gain_vals[3])
    grad_down_low = grad_down_rows.astype(jnp.bfloat16)
    grad_w_down = jnp.einsum(
        "ti,td->id", activated, grad_down_low, preferred_element_type=jnp.float32
    )
    grad_active = jnp.einsum("td,id->ti", grad_down_low, w_down, preferred_element_type=jnp.float32)
    normal_cdf = 0.5 * (1.0 + lax.erf(up_rows * (1.0 / math.sqrt(2.0))))
    normal_pdf = jnp.exp(-0.5 * up_rows * up_rows) * (1.0 / math.sqrt(2.0 * math.pi))
    grad_up_low = (grad_active * (normal_cdf + up_rows * normal_pdf)).astype(jnp.bfloat16)
    grad_w_up = jnp.einsum("td,ti->di", normed_two, grad_up_low, preferred_element_type=jnp.float32)
    grad_normed_two = jnp.einsum("ti,di->td", grad_up_low, w_up, preferred_element_type=jnp.float32)
    grad_middle_extra, grad_gain_three = norm_back(grad_normed_two, middle, gain_vals[2])
    grad_middle = grad_rows + grad_middle_extra
    grad_projected, grad_gain_two = norm_back(grad_middle, projected, gain_vals[1])
    grad_proj_low = grad_projected.astype(jnp.bfloat16)
    grad_w_proj = jnp.einsum(
        "ti,to->io", mixture, grad_proj_low, preferred_element_type=jnp.float32
    )
    grad_mixture = jnp.einsum(
        "to,io->ti", grad_proj_low, w_proj, preferred_element_type=jnp.float32
    ).astype(jnp.bfloat16)
    grad_packed = attend_back(packed, log_totals, grad_mixture, HEADS, HEAD_DIM).astype(
        jnp.bfloat16
    )
    grad_w_qkv = jnp.einsum(
        "td,tj->dj", normed_one, grad_packed, preferred_element_type=jnp.float32
    )
    grad_normed_one = jnp.einsum(
        "tj,dj->td", grad_packed, w_qkv, preferred_element_type=jnp.float32
    )
    grad_start_extra, grad_gain_one = norm_back(grad_normed_one, start_rows, gain_vals[0])
    grad_start = grad_middle + grad_start_extra
    onehot = group_onehot(group_id, table_rows.shape[0])
    grad_table = onehot[:, None] * jnp.sum(grad_start, axis=0)[None, :]
    grad_gain_rows = jnp.stack([grad_gain_one, grad_gain_two, grad_gain_three, grad_gain_four])
    return (
        grad_start,
        (grad_w_qkv, grad_w_proj, grad_w_up, grad_w_down, grad_gain_rows, grad_table),
    )


def to_spans(gradient, split_axis, span_count):
    shape_now = gradient.shape
    shaped = gradient.reshape(
        shape_now[:split_axis]
        + (span_count, shape_now[split_axis] // span_count)
        + shape_now[split_axis + 1 :]
    )
    return jnp.moveaxis(shaped, split_axis, 0).reshape(span_count, -1)


def local(tokens, cotangent, group_ids, counts, w_qkv, w_proj, w_up, w_down, gains, table):
    length = tokens.shape[1]
    width = tokens.shape[2]
    hidden_width = w_up.shape[1]
    weight_set = (
        lax.all_gather(w_qkv.astype(jnp.bfloat16), "fsdp", axis=0, tiled=True),
        lax.all_gather(w_proj.astype(jnp.bfloat16), "fsdp", axis=0, tiled=True),
        lax.all_gather(w_up.astype(jnp.bfloat16), "fsdp", axis=0, tiled=True),
        lax.all_gather(w_down.astype(jnp.bfloat16), "fsdp", axis=0, tiled=True),
        lax.all_gather(gains.astype(jnp.bfloat16), "fsdp", axis=1, tiled=True),
        lax.all_gather(table.astype(jnp.bfloat16), "fsdp", axis=1, tiled=True),
    )
    slot_live = jnp.arange(tokens.shape[0]) < counts[0]

    def run_forward(slot_item):
        token_rows, group_id, is_live = slot_item
        return lax.cond(
            is_live,
            lambda: forward_slot(token_rows, group_id, weight_set),
            lambda: blank_slot(length, width, hidden_width),
        )

    output, kept_all = lax.map(run_forward, (tokens, group_ids, slot_live))
    back_set = (
        lax.all_gather(w_qkv.astype(jnp.bfloat16), "fsdp", axis=0, tiled=True),
        lax.all_gather(w_proj.astype(jnp.bfloat16), "fsdp", axis=0, tiled=True),
        lax.all_gather(w_up.astype(jnp.bfloat16), "fsdp", axis=0, tiled=True),
        lax.all_gather(w_down.astype(jnp.bfloat16), "fsdp", axis=0, tiled=True),
        lax.all_gather(gains.astype(jnp.bfloat16), "fsdp", axis=1, tiled=True),
        lax.all_gather(table.astype(jnp.bfloat16), "fsdp", axis=1, tiled=True),
    )

    def run_back(running, slot_item):
        grad_rows, group_id, is_live, kept = slot_item

        def live_branch():
            grad_start, slot_grads = backward_slot(grad_rows, group_id, kept, back_set)
            return (jax.tree.map(jnp.add, running, slot_grads), grad_start)

        def empty_branch():
            return (running, jnp.zeros_like(grad_rows))

        return lax.cond(is_live, live_branch, empty_branch)

    start_sums = tuple((jnp.zeros(weight.shape, jnp.float32) for weight in back_set))
    summed, grad_tokens = lax.scan(
        run_back, start_sums, (cotangent, group_ids, slot_live, kept_all)
    )
    fsdp_count = lax.axis_size("fsdp")
    split_axes = (0, 0, 0, 0, 1, 1)
    spanned = tuple(
        (
            to_spans(gradient, split_axis, fsdp_count)
            for gradient, split_axis in zip(summed, split_axes)
        )
    )
    mine = (
        lax.psum_scatter(spanned[0], "fsdp", scatter_dimension=0, tiled=True),
        lax.psum_scatter(spanned[1], "fsdp", scatter_dimension=0, tiled=True),
        lax.psum_scatter(spanned[2], "fsdp", scatter_dimension=0, tiled=True),
        lax.psum_scatter(spanned[3], "fsdp", scatter_dimension=0, tiled=True),
        lax.psum_scatter(spanned[4], "fsdp", scatter_dimension=0, tiled=True),
        lax.psum_scatter(spanned[5], "fsdp", scatter_dimension=0, tiled=True),
    )
    reduced = lax.psum((mine[0], mine[1], mine[2], mine[3], mine[4], mine[5]), "dp")
    shard_shapes = (w_qkv.shape, w_proj.shape, w_up.shape, w_down.shape, gains.shape, table.shape)
    finals = tuple(
        (piece.reshape(shard_shape) for piece, shard_shape in zip(reduced, shard_shapes))
    )
    return (output, grad_tokens, finals[0], finals[1], finals[2], finals[3], finals[4], finals[5])


def solution(mesh):
    placed = (
        P(("dp", "fsdp"), None, None),
        P(("dp", "fsdp"), None, None),
        P(("dp", "fsdp")),
        P(("dp", "fsdp")),
        P("fsdp", None),
        P("fsdp", None),
        P("fsdp", None),
        P("fsdp", None),
        P(None, "fsdp"),
        P(None, "fsdp"),
    )
    return jax.shard_map(
        local,
        mesh=mesh,
        in_specs=placed,
        out_specs=(
            P(("dp", "fsdp"), None, None),
            P(("dp", "fsdp"), None, None),
            P("fsdp", None),
            P("fsdp", None),
            P("fsdp", None),
            P("fsdp", None),
            P(None, "fsdp"),
            P(None, "fsdp"),
        ),
        check_vma=False,
    )
```

profile of v0, /device:TPU:0, one launch (start us, length us, event | category | flops | bytes accessed | tf_op | source)
XLA Modules:
  0.0 3724.0 jit_solution(16134357578124365683)
XLA Ops:
  46.2 82.5 %all-gather.5.cloned.1.call-done = bf16[1024,3072]{1,0:T(8,128)(2,1)} async-done(((bf16[512,3072]{1,0:T(8,128)(2,1)}), bf16[1024,3072]{1,0:T(8,128)(2,1)}) %all-gather.5.cloned.1.call-update) | async-done | bytes 6291472 | tf_op jit(solution)/shard_map/all_gather | solution.py:253
  128.8 106.2 %all-gather.11.cloned.1.call-done = bf16[4096,1024]{1,0:T(8,128)(2,1)} async-done(((bf16[2048,1024]{1,0:T(8,128)(2,1)}), bf16[4096,1024]{1,0:T(8,128)(2,1)}) %all-gather.11.cloned.1.call-update) | async-done | bytes 8388624 | tf_op jit(solution)/shard_map/all_gather | solution.py:256
  234.9 106.0 %all-gather.9.cloned.1.call-done = bf16[1024,4096]{1,0:T(8,128)(2,1)} async-done(((bf16[512,4096]{1,0:T(8,128)(2,1)}), bf16[1024,4096]{1,0:T(8,128)(2,1)}) %all-gather.9.cloned.1.call-update) | async-done | bytes 8388624 | tf_op jit(solution)/shard_map/all_gather | solution.py:255
  364.0 657.7 %while.99 = (s32[]{:T(128)}, f32[2,1088,1024]{2,1,0:T(8,128)}, f32[2,1088,1024]{2,1,0:T(8,128)}, bf16[2,1088,1024]{2,1,0:T(8,128)(2,1)}, bf16[2,1088,3072]{2,1,0...) while((s32[]{:T(128)}, f32[2,1088,1024]{2,1,0:T(8,128)}, ...), condition=%wide.region_15.16_spmd, body=%wide.region_0.15_spmd.sunk | while | flops 30243739648 | bytes 664615040 | solution.py:270
  366.1 260.5 %conditional.4 = (f32[1,1088,1024]{2,1,0:T(8,128)}, f32[1,1088,1024]{2,1,0:T(8,128)}, bf16[1,1088,1024]{2,1,0:T(8,128)(2,1)}, bf16[1,1088,3072]{2,1,0:T(8,128)(2...) conditional(s32[]{:T(128)} %bitcast.235, () %tuple.176, ...), branch_computations={%region_1.1_spmd, %region_2.14_spmd} | conditional | flops 30243739648 | bytes 462804800 | solution.py:264
  406.3 110.6 %while.97 = (s32[]{:T(128)}, bf16[2,544,16,64]{1,3,2,0:T(8,128)(2,1)}, f32[2,16,544]{2,1,0:T(8,128)}, s32[2]{0:T(128)S(1)}, bf16[1088,16,64]{0,2,1:T(8,128)(2,1)...) while((s32[]{:T(128)}, ...), condition=%wide.region_8.7_spmd, body=%wide.region_5.6_spmd.sunk | while | flops 2520156672 | bytes 133332424 | solution.py:72
  543.3 51.5 %fusion.10 = (bf16[1088,4096]{1,0:T(8,128)(2,1)}, f32[1088,4096]{1,0:T(8,128)}) fusion(bf16[1024,4096]{1,0:T(8,128)(2,1)S(1)} %bitcast.304, f32[1088,1024]{1,0:T(8,128)} %get-tuple-element.1197, f32[1024]{0:T(1024)S(1)} %bitcast.294, f32[1088]{0:T(1024)S(1)} %add_rsqrt_fusion.1, f32[1088]{0:T(1024)S(1)} %broadcast_multiply_fusion.1), kind=kOutput, calls=%fused_computation.17 | convolution fusion | flops 9420931072 | bytes 39596544 | tf_op jit(solution)/shard_map/while/body/eval_jaxpr/cond/branch_1_fun/dot_general | solution.py:141
  692.9 260.5 %conditional.4 = (f32[1,1088,1024]{2,1,0:T(8,128)}, f32[1,1088,1024]{2,1,0:T(8,128)}, bf16[1,1088,1024]{2,1,0:T(8,128)(2,1)}, bf16[1,1088,3072]{2,1,0:T(8,128)(2...) conditional(s32[]{:T(128)} %bitcast.235, () %tuple.176, ...), branch_computations={%region_1.1_spmd, %region_2.14_spmd} | conditional | flops 30243739648 | bytes 462804800 | solution.py:264
  733.2 110.8 %while.97 = (s32[]{:T(128)}, bf16[2,544,16,64]{1,3,2,0:T(8,128)(2,1)}, f32[2,16,544]{2,1,0:T(8,128)}, s32[2]{0:T(128)S(1)}, bf16[1088,16,64]{0,2,1:T(8,128)(2,1)...) while((s32[]{:T(128)}, ...), condition=%wide.region_8.7_spmd, body=%wide.region_5.6_spmd.sunk | while | flops 2520156672 | bytes 133332424 | solution.py:72
  870.4 51.1 %fusion.10 = (bf16[1088,4096]{1,0:T(8,128)(2,1)}, f32[1088,4096]{1,0:T(8,128)}) fusion(bf16[1024,4096]{1,0:T(8,128)(2,1)S(1)} %bitcast.304, f32[1088,1024]{1,0:T(8,128)} %get-tuple-element.1197, f32[1024]{0:T(1024)S(1)} %bitcast.294, f32[1088]{0:T(1024)S(1)} %add_rsqrt_fusion.1, f32[1088]{0:T(1024)S(1)} %broadcast_multiply_fusion.1), kind=kOutput, calls=%fused_computation.17 | convolution fusion | flops 9420931072 | bytes 39596544 | tf_op jit(solution)/shard_map/while/body/eval_jaxpr/cond/branch_1_fun/dot_general | solution.py:141
  1069.3 905.1 %while.100 = (s32[]{:T(128)}, f32[1024,3072]{1,0:T(8,128)}, f32[1024,1024]{1,0:T(8,128)}, f32[1024,4096]{1,0:T(8,128)}, f32[4096,1024]{1,0:T(8,128)}, /*index=5*...) while((s32[]{:T(128)}, f32[1024,3072]{1,0:T(8,128)}, ...), condition=%wide.region_43.44_spmd, body=%wide.region_16.43_spmd.sunk | while | flops 64795500544 | bytes 883403776 | solution.py:293
  1071.4 437.6 %conditional.5 = (f32[1024,3072]{1,0:T(8,128)}, f32[1024,1024]{1,0:T(8,128)}, f32[1024,4096]{1,0:T(8,128)}, f32[4096,1024]{1,0:T(8,128)}, f32[4,1024]{1,0:T(4,12...) conditional(s32[]{:T(128)} %bitcast.236, (f32[1024,3072]{1,0:T(8,128)}, f32[1024,1024]{1,0:T(8,128)}, ...), branch_computations={%region_17.17_spmd, %region_18.42_spmd} | conditional | flops 64795500544 | bytes 874489920 | solution.py:290
  1164.1 243.0 %while.98 = (s32[]{:T(128)}, f32[1088,16,64]{0,2,1:T(8,128)}, f32[1088,16,64]{0,2,1:T(8,128)}, bf16[2,544,16,64]{1,3,2,0:T(8,128)(2,1)}, s32[2]{0:T(128)S(1)}, /...) while((s32[]{:T(128)}, f32[1088,16,64]{0,2,1:T(8,128)}, ...), condition=%wide.region_33.32_spmd.clone, body=%wide.region_31.31_spmd.clone.sunk | while | flops 9834878976 | bytes 281135104 | solution.py:112
  1326.6 41.1 %bitcast_add_fusion.7 = f32[1088,16,64]{0,2,1:T(8,128)} fusion(f32[1088,16,64]{0,2,1:T(8,128)} %get-tuple-element.1763, f32[16,544,1088]{2,1,0:T(8,128)} %subtract_exponential_fusion.2, bf16[1088,16,64]{0,2,1:T(8,128)(2,1)} %get-tuple-element.1786, pred[]{:T(512)S(6)} %compare.3, bf16[1088,16,64]{0,2,1:T(8,128)(2,1)} %get-tuple-element.1782, ...), kind=kOutput, calls=%fused_computation.87.clone.1 | convolution fusion | flops 3686049280 | bytes 98043904 | tf_op jit(solution)/shard_map/while/body/eval_jaxpr/cond/branch_1_fun/while/body/eval_jaxpr/hqk,qhd->khd/dot_general | solution.py:106
  1519.7 437.5 %conditional.5 = (f32[1024,3072]{1,0:T(8,128)}, f32[1024,1024]{1,0:T(8,128)}, f32[1024,4096]{1,0:T(8,128)}, f32[4096,1024]{1,0:T(8,128)}, f32[4,1024]{1,0:T(4,12...) conditional(s32[]{:T(128)} %bitcast.236, (f32[1024,3072]{1,0:T(8,128)}, f32[1024,1024]{1,0:T(8,128)}, ...), branch_computations={%region_17.17_spmd, %region_18.42_spmd} | conditional | flops 64795500544 | bytes 874489920 | solution.py:290
  1612.4 243.0 %while.98 = (s32[]{:T(128)}, f32[1088,16,64]{0,2,1:T(8,128)}, f32[1088,16,64]{0,2,1:T(8,128)}, bf16[2,544,16,64]{1,3,2,0:T(8,128)(2,1)}, s32[2]{0:T(128)S(1)}, /...) while((s32[]{:T(128)}, f32[1088,16,64]{0,2,1:T(8,128)}, ...), condition=%wide.region_33.32_spmd.clone, body=%wide.region_31.31_spmd.clone.sunk | while | flops 9834878976 | bytes 281135104 | solution.py:112
  2072.2 318.0 %all-reduce.15.cloned.1.call-done = f32[2,2097152]{1,0:T(2,128)} async-done(((f32[2,2097152]{1,0:T(2,128)}), f32[2,2097152]{1,0:T(2,128)}) %all-reduce.15.cloned.1.call-update) | async-done | bytes 16777232
  2390.2 91.9 %dynamic-slice_reduce_fusion.5 = f32[2097152]{0:T(1024)} fusion(f32[2,2097152]{1,0:T(2,128)} %all-reduce.15.cloned.1.call-done, u32[]{:T(128)} %bitcast.67), kind=kLoop, calls=%fused_computation.212 | loop fusion | bytes 16777220
  2491.6 279.4 %all-reduce.17.cloned.1.call-done = f32[2,2097152]{1,0:T(2,128)} async-done(((f32[2,2097152]{1,0:T(2,128)}), f32[2,2097152]{1,0:T(2,128)}) %all-reduce.17.cloned.1.call-update) | async-done | bytes 16777232
  2771.0 91.9 %dynamic-slice_reduce_fusion.4 = f32[2097152]{0:T(1024)} fusion(f32[2,2097152]{1,0:T(2,128)} %all-reduce.17.cloned.1.call-done, u32[]{:T(128)} %bitcast.67), kind=kLoop, calls=%fused_computation.211 | loop fusion | bytes 16777220
  2872.3 281.1 %all-reduce.21.cloned.1.call-done = (f32[2,1572864]{1,0:T(2,128)}, f32[2,524288]{1,0:T(2,128)}) async-done(((f32[2,1572864]{1,0:T(2,128)}, f32[2,524288]{1,0:T(2,128)}), (f32[2,1572864]{1,0:T(2,128)}, f32[2,524288]{1,0:T(2,128)})) %all-reduce.21.cloned.1.call-update) | async-done | bytes 16777232
  3153.4 69.7 %dynamic-slice_reduce_fusion.6 = f32[1572864]{0:T(1024)} fusion(f32[2,1572864]{1,0:T(2,128)} %get-tuple-element.1192, u32[]{:T(128)} %bitcast.67), kind=kLoop, calls=%fused_computation.213 | loop fusion | bytes 12582916
  3265.2 63.0 %all-reduce.6 = (f32[4,512]{1,0:T(4,128)}, f32[8,512]{1,0:T(8,128)}) all-reduce(f32[4,512]{1,0:T(4,128)S(1)} %reshape.393, f32[8,512]{1,0:T(8,128)S(1)} %reshape.396), channel_id=1, replica_groups=mesh['dp'=16,'fsdp'=2] {'dp'}, use_global_device_ids=true, to_apply=%region_53.54 | all-reduce | flops 6144 | bytes 49152 | tf_op jit(solution)/shard_map/psum | solution.py:312
  3328.3 370.9 %all-reduce.19.cloned.1.call-done = (f32[512,3072]{1,0:T(8,128)}, f32[512,1024]{1,0:T(8,128)}, f32[512,4096]{1,0:T(8,128)}, f32[2048,1024]{1,0:T(8,128)}) async-done(((f32[512,3072]{1,0:T(8,128)}, f32[512,1024]{1,0:T(8,128)}, f32[512,4096]{1,0:T(8,128)}, f32[2048,1024]{1,0:T(8,128)}), (f32[512,3072]{1,0:T(8,128)}, f32[512,1024]{1,0:T(8,128)}, f32[512,4096]{1,0:T(8,128)}, ...) | async-done | bytes 25165840 | tf_op jit(solution)/shard_map/psum | solution.py:312
  (607 shorter events, 1664.3 us)
Async XLA Ops:
  7.2 39.1 %all-gather.7.cloned.1.call-start = ((), (), s32[]{:S(2)}) async-start(), calls=%async_computation.1 | async-start | bytes 3145728 | tf_op jit(solution)/shard_map/all_gather | solution.py:254
  10.0 118.8 %all-gather.5.cloned.1.call-start = ((), (), s32[]{:S(2)}) async-start(), calls=%async_computation | async-start | bytes 9437184 | tf_op jit(solution)/shard_map/all_gather | solution.py:253
  15.0 220.0 %all-gather.11.cloned.1.call-start = ((), (), s32[]{:S(2)}) async-start(), calls=%async_computation.3 | async-start | bytes 12582912 | tf_op jit(solution)/shard_map/all_gather | solution.py:256
  21.1 319.8 %all-gather.9.cloned.1.call-start = ((), (), s32[]{:S(2)}) async-start(), calls=%async_computation.2 | async-start | bytes 12582912 | tf_op jit(solution)/shard_map/all_gather | solution.py:255
  27.5 2362.7 %all-reduce.15.cloned.1.call-start = ((), (), s32[]{:S(2)}) async-start(), calls=%async_computation.4 | async-start | bytes 33554432
  543.3 51.5 %copy-start.55 = (bf16[4096,1024]{1,0:T(8,128)(2,1)S(1)}, bf16[4096,1024]{1,0:T(8,128)(2,1)}, u32[]{:S(2)}) copy-start(bf16[4096,1024]{1,0:T(8,128)(2,1)} %get-tuple-element.678) | copy-start | bytes 25165828 | tf_op jit(solution)/shard_map/while/body/eval_jaxpr/cond
  870.4 51.1 %copy-start.55 = (bf16[4096,1024]{1,0:T(8,128)(2,1)S(1)}, bf16[4096,1024]{1,0:T(8,128)(2,1)}, u32[]{:S(2)}) copy-start(bf16[4096,1024]{1,0:T(8,128)(2,1)} %get-tuple-element.678) | copy-start | bytes 25165828 | tf_op jit(solution)/shard_map/while/body/eval_jaxpr/cond
  1085.4 22.2 copy-start.48
  1085.4 22.2 copy-start.50
  1112.8 26.5 slice-start
  1112.8 26.5 slice-start.8
  1118.8 20.5 slice-start.2
  1118.8 20.5 slice-start.9
  1118.8 20.5 slice-start.10
  1533.7 22.2 copy-start.48
  1533.7 22.2 copy-start.50
  1561.1 26.5 slice-start
  1561.1 26.5 slice-start.8
  1567.1 20.5 slice-start.2
  1567.1 20.5 slice-start.9
  1567.1 20.5 slice-start.10
  2013.0 758.0 %all-reduce.17.cloned.1.call-start = ((), (), s32[]{:S(2)}) async-start(), calls=%async_computation.5 | async-start | bytes 33554432
  2041.2 1112.2 %all-reduce.21.cloned.1.call-start = ((), (), s32[]{:S(2)}) async-start(), calls=%async_computation.7 | async-start | bytes 33554432
  2071.0 1628.2 %all-reduce.19.cloned.1.call-start = ((), (), s32[]{:S(2)}) async-start(), calls=%async_computation.6 | async-start | bytes 50331648 | tf_op jit(solution)/shard_map/psum | solution.py:312
  (123 other events, 1081.1 us)
Sparse Core Ops, SparseCore 0:
  10.1 36.0 all-gather.6
  48.3 80.3 all-gather.4
  130.9 103.9 all-gather.10
  236.9 103.9 all-gather.8
  2013.1 377.0 all-reduce.14
  2392.7 378.3 all-reduce.16
  2774.1 379.1 all-reduce.20
  3255.4 443.7 all-reduce.18
where the time goes:
time: 3730 us; the launch traced here: 3720 us
  waiting for transfers between devices  1550 us (42%)
  matrix products  1030 us (28%)
  local copies, waits for them, and re-layouts  751 us (20%)
  other arithmetic  257 us (7%)
  blocking collectives  80.8 us (2%)
  loops' own time  40.2 us (1%)
    unnamed x11, waiting for transfers between devices  879 us
    psum x1, waiting for transfers between devices, local(): lax.psum((mine[0], mine[1], mine[2], mine[3], mine[4], mine[5]), 'dp')  371 us
    unnamed x31, local copies, waits for them, and re-layouts  298 us
    dot_general x4, matrix products, one_block(): jnp.einsum('hqk,qhd->khd', grad_scores, query_part, preferred_element_typ...  161 us
    dot_general x4, matrix products, one_block(): jnp.einsum('hqk,khd->qhd', grad_scores, key_rows, preferred_element_type=...  157 us
    dot_general x8, matrix products, causal_scores(): jnp.einsum('qhd,khd->hqk', queries, key_rows, preferred_element_type=jnp....  152 us
    dynamic_update_slice x22, local copies, waits for them, and re-layouts, local(): output, kept_all = lax.map(run_forward, (tokens, group_ids, slot_live))  135 us
    all_gather x1, waiting for transfers between devices, local(): lax.all_gather(w_down.astype(jnp.bfloat16), 'fsdp', axis=0, tiled=True)  106 us
  transfers between devices with their start and end apart: 8, of which 8 were waited for; matrix products, arithmetic and copies ran while one was open for 8% of the time, Pallas kernels for 0%

commit v1 on v0

v1 whole, which is shorter than its diff:
```python
import math

import jax
import jax.numpy as jnp
from jax import lax
from jax.experimental import pallas as pl
from jax.experimental.pallas import tpu as pltpu
from jax.sharding import PartitionSpec as P

HEAD_DIM = 64
LANES = 128
EPSILON = 1e-05
NEG = -1e30
ATTN_ROWS = 256
VMEM_BYTES = 60 * 1024 * 1024


def dot(a, b, a_dim, b_dim):
    return lax.dot_general(a, b, (((a_dim,), (b_dim,)), ((), ())), preferred_element_type=jnp.float32)


def params(*semantics):
    return pltpu.CompilerParams(vmem_limit_bytes=VMEM_BYTES)


def cost(micros):
    return pl.CostEstimate(flops=int(micros * 1e9), bytes_accessed=int(micros * 1e6), transcendentals=0)


def row_block(length, most):
    return max(b for b in range(16, most + 1, 16) if length % b == 0)


def normed(rows):
    centered = rows - jnp.mean(rows, axis=-1, keepdims=True)
    inv_std = lax.rsqrt(jnp.mean(centered * centered, axis=-1, keepdims=True) + EPSILON)
    return centered * inv_std, inv_std


def norm_back(gradient, unit, inv_std, gain):
    grad_unit = gradient * gain
    first = jnp.mean(grad_unit, axis=-1, keepdims=True)
    second = jnp.mean(grad_unit * unit, axis=-1, keepdims=True)
    return inv_std * (grad_unit - first - unit * second)


def gelu_parts(u):
    cdf = 0.5 + 0.5 * lax.erf(u * math.sqrt(0.5))
    return u * cdf, cdf + u * jnp.exp(-0.5 * u * u) * (1.0 / math.sqrt(2.0 * math.pi))


def staged(jobs, one, two, three):
    n, firsts, seconds = len(jobs), {}, {}
    for i in range(n + 2):
        if i < n:
            firsts[i] = one(jobs[i])
        if i >= 2:
            three(jobs[i - 2], seconds.pop(i - 2))
        if 1 <= i <= n:
            seconds[i - 1] = two(jobs[i - 1], firsts.pop(i - 1))


def spans(length):
    return [(s, min(s + ATTN_ROWS, length)) for s in range(0, length, ATTN_ROWS)]


class Weights:
    def __init__(self, matrices):
        self.refs = [part[0] for parts, _ in matrices for part in parts]
        self.parts = [[part[1:] for part in parts] for parts, _ in matrices]
        self.shapes = [shape for _, shape in matrices]
        self.starts = jnp.stack([jnp.asarray(part[1], jnp.int32) for parts, _ in matrices for part in parts])
        self.in_specs = [pl.BlockSpec(memory_space=pl.ANY)] * len(self.refs)
        self.scratch = [pltpu.VMEM(shape, jnp.bfloat16) for shape in self.shapes]
        n_copies = sum(len(part[1]) if len(part) > 1 else 1 for parts in self.parts for part in parts)
        self.scratch.append(pltpu.SemaphoreType.DMA((n_copies,)))

    def copies(self, starts_ref, refs, scratch):
        lists, at, n = [], 0, 0
        for parts, whole in zip(self.parts, scratch[:-1]):
            mine = []
            for part in parts:
                rows = pl.ds(pl.multiple_of(starts_ref[at], 16), refs[at].shape[-2])
                pairs = [(refs[at], whole.at[..., rows, :])]
                if len(part) > 1:
                    pairs = [(refs[at].at[:, lo:hi], whole.at[i, rows, :]) for i, (lo, hi) in enumerate(part[1])]
                for source, target in pairs:
                    mine.append(pltpu.make_async_copy(source, target, scratch[-1].at[n]))
                    n += 1
                at += 1
            lists.append(mine)
        return lists


def run_all(copies, method):
    for copy in copies:
        getattr(copy, method)()


def project_in(tokens, added, gain, weight):
    slots, length, width = tokens.shape
    part = weight[1][2]
    block = row_block(length, 544)
    held = Weights([weight])
    n_held = len(held.refs)

    def kernel(starts_ref, x_ref, e_ref, g_ref, *rest):
        refs, (a_ref, out_ref), scratch = rest[:n_held], rest[n_held : n_held + 2], rest[n_held + 2 :]
        first = (pl.program_id(0) == 0) & (pl.program_id(1) == 0)
        copies = held.copies(starts_ref, refs, scratch)[0]

        @pl.when(first)
        def _():
            run_all(copies, "start")

        a = (normed(x_ref[0] + e_ref[0])[0] * g_ref[...]).astype(jnp.bfloat16)
        a_ref[0] = a

        @pl.when(first)
        def _():
            run_all(copies, "wait")

        for i in range(3):
            out_ref[i, 0] = dot(a, scratch[0][i], 1, 0).astype(jnp.bfloat16)

    rows = pl.BlockSpec((1, block, width), lambda s, i, _: (s, i, 0))
    return pl.pallas_call(
        kernel,
        grid_spec=pltpu.PrefetchScalarGridSpec(
            num_scalar_prefetch=1,
            grid=(slots, length // block),
            in_specs=[
                rows,
                pl.BlockSpec((1, 1, width), lambda s, i, _: (s, 0, 0)),
                pl.BlockSpec((1, width), lambda s, i, _: (0, 0)),
            ]
            + held.in_specs,
            out_specs=[rows, pl.BlockSpec((3, 1, block, part), lambda s, i, _: (0, s, i, 0))],
            scratch_shapes=held.scratch,
        ),
        out_shape=[
            jax.ShapeDtypeStruct(tokens.shape, jnp.bfloat16),
            jax.ShapeDtypeStruct((3, slots, length, part), jnp.bfloat16),
        ],
        compiler_params=params(),
        cost_estimate=cost(14),
        name="project_in",
    )(held.starts, tokens, added, gain, *held.refs)


def causal(scores, keys_first):
    q = lax.broadcasted_iota(jnp.int32, scores.shape, 1 if keys_first else 0)
    k = lax.broadcasted_iota(jnp.int32, scores.shape, 0 if keys_first else 1)
    return q >= k


def attn_fwd_kernel(x_ref, o_ref, l_ref):
    length = x_ref.shape[2]
    first = lax.broadcasted_iota(jnp.int32, (1, LANES), 1) < HEAD_DIM
    jobs = [(lo, hi, h) for lo, hi in spans(length) for h in range(2)]
    outs = {}

    def scores(job):
        lo, hi, h = job
        q = x_ref[0, 0, lo:hi, :] * (1.0 / math.sqrt(HEAD_DIM))
        q = jnp.where(first if h == 0 else ~first, q, 0).astype(jnp.bfloat16)
        near = dot(q, x_ref[1, 0, lo:hi, :], 1, 1)
        near = jnp.where(causal(near, False), near, NEG)
        return near, dot(q, x_ref[1, 0, 0:lo, :], 1, 1) if lo else None

    def weights(job, both):
        near, far = both
        top = jnp.max(near, axis=1, keepdims=True)
        if far is not None:
            top = jnp.maximum(top, jnp.max(far, axis=1, keepdims=True))
        near = jnp.exp(near - top)
        total = jnp.sum(near, axis=1, keepdims=True)
        if far is not None:
            far = jnp.exp(far - top)
            total = total + jnp.sum(far, axis=1, keepdims=True)
            far = far.astype(jnp.bfloat16)
        return near.astype(jnp.bfloat16), far, top, total

    def mix(job, parts):
        lo, hi, h = job
        near, far, top, total = parts
        o = dot(near, x_ref[2, 0, lo:hi, :], 1, 0)
        if far is not None:
            o = o + dot(far, x_ref[2, 0, 0:lo, :], 1, 0)
        outs[h] = o / total
        log_total = jnp.broadcast_to(top + jnp.log(total), (hi - lo, LANES))
        l_ref[0, 0, h : h + 1, lo:hi] = jnp.transpose(log_total)[0:1, :]
        if h == 1:
            o_ref[0, lo:hi, :] = jnp.where(first, outs[0], outs[1]).astype(jnp.bfloat16)

    staged(jobs, scores, weights, mix)


def attn_fwd(qkv, start, count, first_pair, width, before=None):
    _, slots, length, _ = qkv.shape
    place = first_pair + start
    n_before = 0 if before is None else 2

    def kernel(x_ref, *rest):
        attn_fwd_kernel(x_ref, *rest[n_before:])

    return pl.pallas_call(
        kernel,
        grid=(slots, count),
        in_specs=[pl.BlockSpec((3, 1, length, LANES), lambda s, p: (0, s, 0, start + p))]
        + [pl.BlockSpec(memory_space=pl.ANY)] * n_before,
        out_specs=[
            pl.BlockSpec((1, length, LANES), lambda s, p: (s, 0, place + p)),
            pl.BlockSpec((1, 1, 2, length), lambda s, p: (s, place + p, 0, 0)),
        ],
        out_shape=[
            jax.ShapeDtypeStruct((slots, length, width), jnp.bfloat16),
            jax.ShapeDtypeStruct((slots, width // LANES, 2, length), jnp.float32),
        ],
        input_output_aliases={1 + i: i for i in range(n_before)},
        compiler_params=params(),
        cost_estimate=cost(8 * count),
        name="attn_fwd",
    )(qkv, *(before or ()))


def attn_bwd_kernel(x_ref, o_ref, do_ref, l_ref, d_ref, dqt_ref):
    length = x_ref.shape[2]
    scale = 1.0 / math.sqrt(HEAD_DIM)
    first = lax.broadcasted_iota(jnp.int32, (1, LANES), 1) < HEAD_DIM
    q = x_ref[0, 0] * scale
    do = do_ref[0]
    prod = jnp.transpose(do.astype(jnp.float32) * o_ref[0].astype(jnp.float32))
    deltas = [jnp.sum(prod[:HEAD_DIM], axis=0, keepdims=True), jnp.sum(prod[HEAD_DIM:], axis=0, keepdims=True)]
    dqt_ref[...] = jnp.zeros_like(dqt_ref)
    jobs = []
    for lo, hi in spans(length):
        for h in range(2):
            jobs.append((lo, hi, h, lo, hi))
            if hi < length:
                jobs.append((lo, hi, h, hi, length))
    sums = {}

    def scores(job):
        lo, hi, h, a, b = job
        mine = lambda v: jnp.where(first if h == 0 else ~first, v, 0).astype(jnp.bfloat16)
        return dot(mine(x_ref[1, 0, lo:hi, :]), q[a:b], 1, 1), dot(mine(x_ref[2, 0, lo:hi, :]), do[a:b], 1, 1)

    def weights(job, both):
        lo, hi, h, a, b = job
        p = jnp.exp(both[0] - l_ref[0, 0, h : h + 1, a:b])
        if a == lo:
            p = jnp.where(causal(p, True), p, 0.0)
        return p.astype(jnp.bfloat16), (p * (both[1] - deltas[h][:, a:b])).astype(jnp.bfloat16)

    def collect(job, parts):
        lo, hi, h, a, b = job
        p, ds = parts
        dv, dk = dot(p, do[a:b], 1, 0), dot(ds, q[a:b], 1, 0)
        sums[h] = (dk, dv) if a == lo else (sums[h][0] + dk, sums[h][1] + dv)
        lanes = slice(h * HEAD_DIM, (h + 1) * HEAD_DIM)
        kt = jnp.transpose(x_ref[1, 0, lo:hi, :].astype(jnp.float32)).astype(jnp.bfloat16)
        dqt_ref[lanes, a:b] += dot(kt[lanes], ds, 1, 0)
        if h == 1 and b == length:
            for i in range(2):
                d_ref[1 + i, 0, lo:hi, :] = jnp.where(first, sums[0][i], sums[1][i]).astype(jnp.bfloat16)

    staged(jobs, scores, weights, collect)
    d_ref[0, 0] = (jnp.transpose(dqt_ref[...]) * scale).astype(jnp.bfloat16)


def attn_bwd(qkv, mixture, grad_mix, log_totals, start, count, first_pair):
    _, slots, length, _ = qkv.shape
    place = first_pair + start
    triple = pl.BlockSpec((3, 1, length, LANES), lambda s, p: (0, s, 0, start + p))
    single = pl.BlockSpec((1, length, LANES), lambda s, p: (s, 0, place + p))
    return pl.pallas_call(
        attn_bwd_kernel,
        grid=(slots, count),
        in_specs=[triple, single, single, pl.BlockSpec((1, 1, 2, length), lambda s, p: (s, place + p, 0, 0))],
        out_specs=pl.BlockSpec((3, 1, length, LANES), lambda s, p: (0, s, 0, p)),
        out_shape=jax.ShapeDtypeStruct((3, slots, length, count * LANES), jnp.bfloat16),
        scratch_shapes=[pltpu.VMEM((LANES, length), jnp.float32)],
        compiler_params=params(),
        cost_estimate=cost(6 * count),
        name="attn_bwd",
    )(qkv, mixture, grad_mix, log_totals)


def token_specs(shape, block):
    slots, length, width = shape
    rows = pl.BlockSpec((1, block, width), lambda s, i, *_: (s, i, 0))
    per_slot = lambda n: pl.BlockSpec((1, n, width), lambda s, i, *_: (s, 0, 0))
    whole = lambda v: pl.BlockSpec(v.shape, lambda s, i, *_: (0,) * v.ndim)
    return rows, per_slot, whole


def up_and_down(live, mixture, tokens, cotangent, added, gains, w_proj, w_up, w_down):
    slots, length, width = tokens.shape
    hidden = w_up[1][1]
    block = row_block(length, 272)
    chunk = min(512, hidden)
    held = Weights([w_proj, w_up, w_down])
    n_held = len(held.refs)

    def kernel(starts_ref, live_ref, o_ref, x_ref, c_ref, e_ref, g_ref, *rest):
        refs = rest[:n_held]
        a_ref, f_ref, slope_ref, dm_ref, z_ref, h_ref, out_ref, sum_ref = rest[n_held : n_held + 8]
        wp, wu, wd = rest[n_held + 8 : n_held + 11]

        @pl.when((pl.program_id(0) == 0) & (pl.program_id(1) == 0))
        def _():
            copies = held.copies(starts_ref, refs, rest[n_held + 8 : n_held + 12])
            for some in copies:
                run_all(some, "start")
            for some in copies:
                run_all(some, "wait")

        @pl.when(pl.program_id(1) == 0)
        def _():
            sum_ref[...] = jnp.zeros_like(sum_ref)

        alive = live_ref[pl.program_id(0)].astype(jnp.float32)
        z = dot(o_ref[0], wp[...], 1, 0)
        z_ref[0] = z
        h1 = x_ref[0] + e_ref[0] + normed(z)[0] * g_ref[1:2]
        h_ref[0] = h1
        a = (normed(h1)[0] * g_ref[2:3]).astype(jnp.bfloat16)
        a_ref[0] = a
        m = []

        def activate(cols, u):
            f, slope = gelu_parts(u)
            f_ref[0, :, cols] = f.astype(jnp.bfloat16)
            slope_ref[0, :, cols] = slope.astype(jnp.bfloat16)
            return f.astype(jnp.bfloat16)

        def lower(cols, f):
            more = dot(f, wd[cols, :], 1, 0)
            m[:] = [m[0] + more] if m else [more]

        cols = [slice(j, j + chunk) for j in range(0, hidden, chunk)]
        staged(cols, lambda c: dot(a, wu[:, c], 1, 0), activate, lower)
        unit_m, inv_m = normed(m[0])
        out_ref[0] = alive * (h1 + unit_m * g_ref[3:4])
        dy = alive * c_ref[0]
        dm_ref[0] = norm_back(dy, unit_m, inv_m, g_ref[3:4]).astype(jnp.bfloat16)
        sum_ref[0, 0:1] += jnp.sum(dy * unit_m, axis=0, keepdims=True)

    rows, per_slot, whole = token_specs(tokens.shape, block)
    wide = pl.BlockSpec((1, block, hidden), lambda s, i, *_: (s, i, 0))
    low = jax.ShapeDtypeStruct(tokens.shape, jnp.bfloat16)
    low_wide = jax.ShapeDtypeStruct((slots, length, hidden), jnp.bfloat16)
    full = jax.ShapeDtypeStruct(tokens.shape, jnp.float32)
    return pl.pallas_call(
        kernel,
        grid_spec=pltpu.PrefetchScalarGridSpec(
            num_scalar_prefetch=2,
            grid=(slots, length // block),
            in_specs=[rows, rows, rows, per_slot(1), whole(gains)] + held.in_specs,
            out_specs=[rows, wide, wide, rows, rows, rows, rows, per_slot(8)],
            scratch_shapes=held.scratch,
        ),
        out_shape=[low, low_wide, low_wide, low, full, full, full, jax.ShapeDtypeStruct((slots, 8, width), jnp.float32)],
        compiler_params=params(),
        cost_estimate=cost(80),
        name="up_and_down",
    )(held.starts, live, mixture, tokens, cotangent, added, gains, *held.refs)


def back_to_hidden(dm, slope, w_down):
    slots, length, width = dm.shape
    hidden = slope.shape[-1]
    block = row_block(length, 544)
    chunk = min(512, hidden)
    held = Weights([w_down])
    n_held = len(held.refs)

    def kernel(starts_ref, dm_ref, slope_ref, *rest):
        refs, du_ref, scratch = rest[:n_held], rest[n_held], rest[n_held + 1 :]

        @pl.when((pl.program_id(0) == 0) & (pl.program_id(1) == 0))
        def _():
            copies = held.copies(starts_ref, refs, scratch)[0]
            run_all(copies, "start")
            run_all(copies, "wait")

        dm_block = dm_ref[0]
        for j in range(0, hidden, chunk):
            df = dot(dm_block, scratch[0][j : j + chunk, :], 1, 1)
            du_ref[0, :, j : j + chunk] = (df * slope_ref[0, :, j : j + chunk].astype(jnp.float32)).astype(jnp.bfloat16)

    rows, _, _ = token_specs(dm.shape, block)
    wide = pl.BlockSpec((1, block, hidden), lambda s, i, *_: (s, i, 0))
    return pl.pallas_call(
        kernel,
        grid_spec=pltpu.PrefetchScalarGridSpec(
            num_scalar_prefetch=1,
            grid=(slots, length // block),
            in_specs=[rows, wide] + held.in_specs,
            out_specs=wide,
            scratch_shapes=held.scratch,
        ),
        out_shape=jax.ShapeDtypeStruct(slope.shape, jnp.bfloat16),
        compiler_params=params(),
        cost_estimate=cost(25),
        name="back_to_hidden",
    )(held.starts, dm, slope, *held.refs)


def back_to_mixture(live, du, h1, z, cotangent, gains, w_proj, w_up):
    slots, length, width = h1.shape
    hidden = du.shape[-1]
    block = row_block(length, 272)
    held = Weights([w_up, w_proj])
    n_held = len(held.refs)

    def kernel(starts_ref, live_ref, du_ref, h_ref, z_ref, c_ref, g_ref, *rest):
        refs = rest[:n_held]
        dz_ref, do_ref, dh_ref, sum_ref = rest[n_held : n_held + 4]
        wu, wp = rest[n_held + 4 : n_held + 6]

        @pl.when((pl.program_id(0) == 0) & (pl.program_id(1) == 0))
        def _():
            copies = held.copies(starts_ref, refs, rest[n_held + 4 : n_held + 7])
            for some in copies:
                run_all(some, "start")
            for some in copies:
                run_all(some, "wait")

        @pl.when(pl.program_id(1) == 0)
        def _():
            sum_ref[...] = jnp.zeros_like(sum_ref)

        alive = live_ref[pl.program_id(0)].astype(jnp.float32)
        da = dot(du_ref[0], wu[...], 1, 1)
        unit_h, inv_h = normed(h_ref[0])
        unit_z, inv_z = normed(z_ref[0])
        dh1 = alive * c_ref[0] + norm_back(da, unit_h, inv_h, g_ref[2:3])
        dh_ref[0] = dh1
        dz = norm_back(dh1, unit_z, inv_z, g_ref[1:2]).astype(jnp.bfloat16)
        dz_ref[0] = dz
        do_ref[0] = dot(dz, wp[...], 1, 1).astype(jnp.bfloat16)
        sum_ref[0, 0:1] += jnp.sum(dh1 * unit_z, axis=0, keepdims=True)
        sum_ref[0, 1:2] += jnp.sum(da * unit_h, axis=0, keepdims=True)

    rows, per_slot, whole = token_specs(h1.shape, block)
    wide = pl.BlockSpec((1, block, hidden), lambda s, i, *_: (s, i, 0))
    low = jax.ShapeDtypeStruct(h1.shape, jnp.bfloat16)
    return pl.pallas_call(
        kernel,
        grid_spec=pltpu.PrefetchScalarGridSpec(
            num_scalar_prefetch=2,
            grid=(slots, length // block),
            in_specs=[wide, rows, rows, rows, whole(gains)] + held.in_specs,
            out_specs=[rows, rows, rows, per_slot(8)],
            scratch_shapes=held.scratch,
        ),
        out_shape=[
            low,
            low,
            jax.ShapeDtypeStruct(h1.shape, jnp.float32),
            jax.ShapeDtypeStruct((slots, 8, width), jnp.float32),
        ],
        compiler_params=params(),
        cost_estimate=cost(40),
        name="back_to_mixture",
    )(held.starts, live, du, h1, z, cotangent, gains, *held.refs)


def project_back(slot, groups, tokens, grad_middle, added, gain, weights):
    _, length, width = tokens.shape
    block = row_block(length, 272)
    held = Weights(weights)
    per_weight = len(groups) // len(weights)
    n_held = len(held.refs)

    n_groups, part = len(groups), groups[0].shape[-1]

    def kernel(starts_ref, *refs_in):
        d_refs, (x_ref, h_ref, e_ref, g_ref), rest = refs_in[:n_groups], refs_in[n_groups : n_groups + 4], refs_in[n_groups + 4 :]
        refs, (out_ref, sum_ref), scratch = rest[:n_held], rest[n_held : n_held + 2], rest[n_held + 2 :]
        first = pl.program_id(0) == 0
        copies = sum(held.copies(starts_ref, refs, scratch), [])

        @pl.when(first)
        def _():
            run_all(copies, "start")

        unit, inv_std = normed(x_ref[0] + e_ref[0])

        @pl.when(first)
        def _():
            run_all(copies, "wait")

        da = None
        for w in range(len(weights)):
            mine = d_refs[w * per_weight : (w + 1) * per_weight]
            for i in range(3):
                more = dot(jnp.concatenate([ref[i, 0] for ref in mine], axis=1), scratch[w][i], 1, 1)
                da = more if da is None else da + more
        dh = h_ref[0] + norm_back(da, unit, inv_std, g_ref[...])
        out_ref[0] = dh

        @pl.when(pl.program_id(0) == 0)
        def _():
            sum_ref[...] = jnp.zeros_like(sum_ref)

        sum_ref[0, 0:1] += jnp.sum(da * unit, axis=0, keepdims=True)
        sum_ref[0, 1:2] += jnp.sum(dh, axis=0, keepdims=True)

    rows = pl.BlockSpec((1, block, width), lambda i, _: (slot, i, 0))
    return pl.pallas_call(
        kernel,
        grid_spec=pltpu.PrefetchScalarGridSpec(
            num_scalar_prefetch=1,
            grid=(length // block,),
            in_specs=[pl.BlockSpec((3, 1, block, part), lambda i, _: (0, slot, i, 0))] * n_groups
            + [
                rows,
                rows,
                pl.BlockSpec((1, 1, width), lambda i, _: (slot, 0, 0)),
                pl.BlockSpec((1, width), lambda i, _: (0, 0)),
            ]
            + held.in_specs,
            out_specs=[
                pl.BlockSpec((1, block, width), lambda i, _: (0, i, 0)),
                pl.BlockSpec((1, 8, width), lambda i, _: (0, 0, 0)),
            ],
            scratch_shapes=held.scratch,
        ),
        out_shape=[
            jax.ShapeDtypeStruct((1,) + tokens.shape[1:], jnp.float32),
            jax.ShapeDtypeStruct((1, 8, width), jnp.float32),
        ],
        compiler_params=params(),
        cost_estimate=cost(15),
        name="project_back",
    )(held.starts, *groups, tokens, grad_middle, added, gain, *held.refs)


def grad_blocks(order, left, right, received=None):
    rows, depth = left.shape[0], left.shape[1] // 4
    tall = min(depth, 512)
    per_block = depth // tall
    stacked = isinstance(right, list)
    if stacked:
        count, slab = right[0].shape[0], sum(r.shape[-1] for r in right)
        right_specs = [pl.BlockSpec((1, rows, r.shape[-1]), lambda r, k, j, order: (j, 0, 0)) for r in right]
    else:
        slab = min(1024, right.shape[1])
        count = right.shape[1] // slab
        right_specs = [pl.BlockSpec((rows, slab), lambda r, k, j, order: (0, j))]
        right = [right]
    n_right = len(right)

    def kernel(order_ref, a_ref, *rest):
        if stacked:
            right_block = jnp.concatenate([ref[0] for ref in rest[:n_right]], axis=1)
        else:
            right_block = rest[0][...]
        outs = rest[n_right:]
        total = dot(a_ref[...], right_block, 0, 0)
        if received is None:
            outs[0][0, 0] = total.astype(jnp.bfloat16)
            return
        total = (total + outs[0][0, 0].astype(jnp.float32)).astype(jnp.bfloat16)

        @pl.when(pl.program_id(0) == 0)
        def _():
            outs[1][0] = total

        @pl.when(pl.program_id(0) == 1)
        def _():
            outs[2][0] = total

    both = pl.BlockSpec((1, 1, tall, slab), lambda r, k, j, order: (r, j, k, 0))
    sent = pl.BlockSpec((1, tall, slab), lambda r, k, j, order: (jnp.where(r == 0, j, count - 1), jnp.where(r == 0, k, per_block - 1), 0))
    kept = pl.BlockSpec((1, tall, slab), lambda r, k, j, order: (jnp.where(r == 0, 0, j), jnp.where(r == 0, 0, k), 0))
    more = [] if received is None else [received]
    shape = (count, depth, slab)
    return pl.pallas_call(
        kernel,
        grid_spec=pltpu.PrefetchScalarGridSpec(
            num_scalar_prefetch=1,
            grid=(2, per_block, count),
            in_specs=[pl.BlockSpec((rows, tall), lambda r, k, j, order: (0, order[r] * per_block + k))]
            + right_specs
            + [both] * len(more),
            out_specs=[sent, kept] if more else both,
        ),
        out_shape=[jax.ShapeDtypeStruct(shape, jnp.bfloat16)] * 2 if more else jax.ShapeDtypeStruct((2,) + shape, jnp.bfloat16),
        compiler_params=params(),
        cost_estimate=cost(rows * left.shape[1] * slab * count // 10**9),
        name="grad_blocks",
    )(order, left, *right, *more)


def after(value, *earlier):
    return lax.optimization_barrier((value,) + earlier)[0]


def swap(value, axis, bit):
    size = lax.axis_size(axis)
    return lax.ppermute(value, axis, [(i, i ^ (1 << bit)) for i in range(size)])


def bit_of(axis, bit):
    return (lax.axis_index(axis) >> bit) & 1


def bits_of(axis):
    return range(lax.axis_size(axis).bit_length() - 1)


def pick(value, index):
    return lax.dynamic_index_in_dim(value, index, 0, keepdims=False)


def paired():
    return lax.axis_size("fsdp") == 2 and lax.axis_size("dp") % 2 == 0


def slot(before, ends=(), starts=()):
    before = tuple(before)
    if not paired():
        for e in ends:
            e.take()
        return before
    if ends:
        arrived = lax.optimization_barrier(tuple(e.received for e in ends) + before)
        for e, value in zip(ends, arrived):
            e.received = value
            e.take()
        before = arrived[len(ends) :]
    if starts:
        leaving = lax.optimization_barrier(tuple(e.sent for e in starts) + before)
        for e, value in zip(starts, leaving):
            e.send(value)
        before = leaving
    return before


class Gather:
    def __init__(self, low, ranges=None):
        self.low, self.ranges = low, ranges
        self.size, wide = low.shape
        whole = self.size * lax.axis_size("fsdp")
        self.shape = (whole, wide) if ranges is None else (len(ranges), whole, ranges[0][1] - ranges[0][0])
        self.crossed = None
        if paired():
            half = self.size // 2
            mine = lambda lo, hi: lax.dynamic_slice(low, (bit_of("dp", 0) * half, lo), (half, hi - lo))
            self.sent = mine(0, wide) if ranges is None else jnp.stack([mine(lo, hi) for lo, hi in ranges])
        else:
            self.sent = low

    def send(self, value):
        self.received = swap(value, "fsdp" if self.crossed is None else "dp", 0)

    def take(self):
        if not paired():
            return
        if self.crossed is None:
            self.crossed = self.sent = self.received
        else:
            self.beside = self.received

    def parts(self):
        ranges = () if self.ranges is None else (self.ranges,)
        if not paired():
            return [(lax.all_gather(self.low, "fsdp", axis=0, tiled=True), 0) + ranges], self.shape
        size, c, x = self.size, bit_of("dp", 0), lax.axis_index("fsdp")
        base = (1 - x) * size
        own = (self.low, x * size) + ranges
        return [own, (self.crossed, base + c * (size // 2)), (self.beside, base + (1 - c) * (size // 2))], self.shape


class WideGather:
    def __init__(self, low):
        self.low = low
        self.shape = (low.shape[0] * lax.axis_size("fsdp"), low.shape[1])
        self.crossed = None
        self.sent = low
        if paired():
            n_dp = lax.axis_size("dp")
            self.sent = pick(low.reshape(n_dp, low.shape[0] // n_dp, low.shape[1]), lax.axis_index("dp"))

    def send(self, value):
        if self.crossed is None:
            self.received = swap(value, "fsdp", 0)
        else:
            self.other = lax.all_gather(value, "dp", axis=0, tiled=True)

    def take(self):
        if paired():
            self.crossed = self.sent = self.received

    def parts(self):
        if not paired():
            return [(lax.all_gather(self.low, "fsdp", axis=0, tiled=True), 0)], self.shape
        size, x = self.low.shape[0], lax.axis_index("fsdp")
        return [(self.low, x * size), (self.other, (1 - x) * size)], self.shape


class Columns:
    def __init__(self, low):
        self.low = self.sent = low

    def send(self, value):
        self.received = swap(value, "fsdp", 0)

    def take(self):
        if not paired():
            self.whole = lax.all_gather(self.low, "fsdp", axis=1, tiled=True)
            return
        first = lax.axis_index("fsdp") == 0
        self.whole = jnp.concatenate(
            [jnp.where(first, self.low, self.received), jnp.where(first, self.received, self.low)], axis=1
        )


class SmallSum:
    def __init__(self, value):
        self.value, self.bits = value, None
        if paired():
            halves = value.reshape(value.shape[0], 2, -1)
            x = lax.axis_index("fsdp")
            self.value = lax.dynamic_index_in_dim(halves, x, 1, keepdims=False)
            self.sent = lax.dynamic_index_in_dim(halves, 1 - x, 1, keepdims=False)

    def send(self, value):
        if self.bits is None:
            self.bits = list(bits_of("dp"))
            self.received = swap(value, "fsdp", 0)
        else:
            self.received = swap(value, "dp", self.bits.pop(0))

    def take(self):
        if paired():
            self.value = self.sent = self.value + self.received

    def result(self):
        if paired():
            return self.value
        return lax.psum(lax.psum_scatter(self.value, "fsdp", scatter_dimension=1, tiled=True), "dp")


def assemble(pieces):
    count, rows, wide = pieces[0][0].shape
    n_pieces = len(pieces)

    def kernel(c_ref, *refs):
        out_ref = refs[-1]
        for p in range(n_pieces):

            @pl.when(pl.program_id(1) == p)
            def _():
                for i, ref in enumerate(refs[2 * p : 2 * p + 2]):
                    half = c_ref[0] if i == 0 else 1 - c_ref[0]
                    out_ref[pl.ds(pl.multiple_of(half * rows, rows), rows), :] = ref[0].astype(jnp.float32)

    return pl.pallas_call(
        kernel,
        grid_spec=pltpu.PrefetchScalarGridSpec(
            num_scalar_prefetch=1,
            grid=(count, n_pieces),
            in_specs=[pl.BlockSpec((1, rows, wide), lambda i, p, c: (i, 0, 0))] * (2 * n_pieces),
            out_specs=pl.BlockSpec((2 * rows, wide), lambda i, p, c: (0, i * n_pieces + p)),
        ),
        out_shape=jax.ShapeDtypeStruct((2 * rows, count * n_pieces * wide), jnp.float32),
        compiler_params=params(),
        cost_estimate=cost(4),
        name="assemble",
    )(bit_of("dp", 0).astype(jnp.int32).reshape(1), *[v for piece in pieces for v in piece])


def in_rows(whole):
    n, count, rows, wide = whole.shape
    n_bits = n.bit_length() - 1
    step = min(wide, 512)

    def place(i):
        return sum(((i >> (n_bits - 1 - b)) & 1) << b for b in range(n_bits))

    def kernel(in_ref, out_ref):
        for i in range(n):
            out_ref[place(i) * rows : (place(i) + 1) * rows, :] = in_ref[i, 0].astype(jnp.float32)

    return pl.pallas_call(
        kernel,
        grid=(count, wide // step),
        in_specs=[pl.BlockSpec((n, 1, rows, step), lambda s, j: (0, s, 0, j))],
        out_specs=pl.BlockSpec((n * rows, step), lambda s, j: (0, s * (wide // step) + j)),
        out_shape=jax.ShapeDtypeStruct((n * rows, count * wide), jnp.float32),
        compiler_params=params(),
        name="in_rows",
    )(whole)


class GradSum:
    def __init__(self, left, right, spread=False):
        self.left, self.right, self.spread = left, right, spread
        self.state = "send"
        if paired():
            self.bits = list(bits_of("dp"))[1:]

    def part(self, before):
        if not paired():
            if self.state == "send":
                right = self.right
                if isinstance(right, list):
                    right = jnp.concatenate([r[i] for i in range(3) for r in right], axis=1)
                low = dot(self.left, right, 0, 0).astype(jnp.bfloat16)
                piece = lax.psum_scatter(low, ("fsdp", "dp"), scatter_dimension=0, tiled=True)
                self.total = lax.all_gather(piece, "dp", axis=0, tiled=True).astype(jnp.float32)
                self.state = "keep"
            return before
        c, x = bit_of("dp", 0), lax.axis_index("fsdp")
        left = after(self.left, *before)
        if self.state == "send":
            order = jnp.stack([(1 - x) * 2 + 1 - c, x * 2 + 1 - c]).astype(jnp.int32)
            self.sent = grad_blocks(order, left, self.right)
        else:
            order = jnp.stack([(1 - x) * 2 + c, x * 2 + c]).astype(jnp.int32)
            self.sent, self.kept = grad_blocks(order, left, self.right, self.received)
        return (self.sent,)

    def send(self, value):
        if self.state == "send":
            self.received = swap(value, "dp", 0)
        elif self.state == "keep":
            self.received = swap(value, "fsdp", 0)
        elif self.state == "halve":
            self.received = swap(value, "dp", self.bit)
        elif self.spread:
            self.whole = lax.all_gather(value, "dp", axis=0, tiled=False)
        else:
            self.received = swap(value, "dp", self.bit)

    def take(self):
        if not paired():
            return
        if self.state == "send":
            self.state = "keep"
        elif self.state in ("keep", "halve"):
            if self.bits:
                self.state, self.bit = "halve", self.bits.pop(0)
                b = bit_of("dp", self.bit)
                slabs, rows, wide = self.kept.shape
                kept, received = (v.reshape(slabs, 2, rows // 2, wide) for v in (self.kept, self.received))
                part = lambda v, i: lax.dynamic_index_in_dim(v, i, 1, keepdims=False).astype(jnp.float32)
                self.sent = (part(kept, 1 - b) + part(received, 1 - b)).astype(jnp.bfloat16)
                self.kept = (part(kept, b) + part(received, b)).astype(jnp.bfloat16)
            else:
                self.kept = self.sent = (self.kept.astype(jnp.float32) + self.received.astype(jnp.float32)).astype(jnp.bfloat16)
                self.state, self.bits = "join", list(bits_of("dp"))
                self.bit = self.bits.pop()
        elif self.bits:
            self.kept = self.sent = in_order(self.kept, self.received, bit_of("dp", self.bit))
            self.bit = self.bits.pop()
        else:
            self.state = "done"

    def result(self, *earlier):
        if not paired():
            return self.total
        if self.spread:
            return in_rows(after(self.whole, *earlier))
        return assemble([(self.kept, self.received)])


def in_order(mine, other, bit):
    return jnp.where(bit == 0, jnp.concatenate([mine, other], axis=1), jnp.concatenate([other, mine], axis=1))


def local(tokens, cotangent, group_ids, counts, w_qkv, w_proj, w_up, w_down, gains, table):
    slots, length, width = tokens.shape
    rows = slots * length
    flat = lambda v: v.reshape(v.shape[:-3] + (rows, v.shape[-1]))
    pairs = width // LANES
    n_groups = 2
    group_pairs = pairs // n_groups
    half = group_pairs // 2
    part = width // n_groups
    small = Columns(jnp.concatenate([gains, table], axis=0).astype(jnp.bfloat16))
    low_qkv = w_qkv.astype(jnp.bfloat16)
    get_qkv = [
        Gather(low_qkv, [(i * width + j * part, i * width + (j + 1) * part) for i in range(3)]) for j in range(n_groups)
    ]
    t = slot((), starts=[small, get_qkv[0]])
    get_down = WideGather(after(w_down, *t).astype(jnp.bfloat16))
    get_proj = Gather(after(w_proj, *t).astype(jnp.bfloat16))
    get_up = Gather(after(w_up, *t).astype(jnp.bfloat16))
    t = (get_down.sent, get_proj.sent, get_up.sent)
    t = slot(t, [small, get_qkv[0]], [get_qkv[0], get_down, get_qkv[1]])
    t = slot(t, [get_qkv[0]])
    small = small.whole.astype(jnp.float32)
    g = small[: gains.shape[0]]
    embed = small[gains.shape[0] :]
    onehot = (group_ids[:, None] == jnp.arange(table.shape[0])[None, :]).astype(jnp.float32)
    added = jnp.sum(onehot[:, :, None] * embed[None], axis=1)[:, None, :]
    live = (jnp.arange(slots) < counts[0]).astype(jnp.int32)

    qkv = []
    a1, group = project_in(after(tokens, *t), added, g[0:1], get_qkv[0].parts())
    qkv.append(group)
    t = slot((group,), [get_down], [get_down, get_proj])
    attended = attn_fwd(after(group, *t), 0, half, 0, width)
    t = slot((attended[0],), [get_qkv[1], get_proj], [get_qkv[1], get_proj, get_up])
    attended = attn_fwd(after(group, *t), half, group_pairs - half, 0, width, attended)
    t = slot((attended[0],), [get_qkv[1], get_proj])
    _, group = project_in(after(tokens, *t), added, g[0:1], get_qkv[1].parts())
    qkv.append(group)
    attended = attn_fwd(group, 0, half, group_pairs, width, attended)
    t = slot((attended[0],), [get_up], [get_up])
    attended = attn_fwd(after(group, *t), half, group_pairs - half, group_pairs, width, attended)
    mixture, log_totals = attended
    t = slot((mixture,), [get_up])
    p_qkv = [w.parts() for w in get_qkv]
    p_proj, p_up, p_down = get_proj.parts(), get_up.parts(), get_down.parts()
    a3, f, slope, dm, z, h1, output, sums_out = up_and_down(
        live, after(mixture, *t), tokens, cotangent, added, g, p_proj, p_up, p_down
    )

    down = GradSum(flat(f), flat(dm), spread=True)
    t = down.part((dm,))
    t = slot(t, [], [down])
    t = slot(t, [down])
    t = slot(down.part(t), [], [down])
    du = back_to_hidden(after(dm, *t), slope, p_down)
    up = GradSum(flat(a3), flat(du), spread=True)
    t = up.part((du,))
    t = slot(t, [down], [down, up])
    t = slot(t, [up])
    t = slot(up.part(t), [], [up])
    dz, do, dh1, sums_mid = back_to_mixture(live, after(du, *t), h1, z, cotangent, g, p_proj, p_up)
    t = slot((dz,), [down], [down])
    proj = GradSum(flat(mixture), flat(dz))
    t = slot(proj.part(t), [], [proj])
    chunks = []

    def attend(i, t):
        group = i // 2
        chunks.append(attn_bwd(qkv[group], mixture, after(do, *t), log_totals, (i % 2) * half, half, group * group_pairs))
        return (chunks[-1],)

    t = attend(0, t)
    t = slot(t, [up, down, proj], [up, down])
    t = slot(proj.part(t), [], [proj])
    t = attend(1, t)
    t = slot(t, [up, down, proj], [up, down, proj])
    first = GradSum(flat(a1), [flat(d) for d in chunks])
    t = slot(first.part(t), [proj], [first, proj])
    t = attend(2, t)
    t = slot(t, [up, proj, first], [up, proj])
    t = slot(first.part(t), [proj], [first, proj])
    t = attend(3, t)
    t = slot(t, [up, first, proj], [up, first, proj])
    last = GradSum(flat(a1), [flat(d) for d in chunks[2:]])
    t = slot(last.part(t), [proj], [last, proj])
    t = slot(t, [last, first, proj], [first, proj])
    t = slot(last.part(t), [first], [last, first])

    backs = []
    for i in range(slots):
        backs.append(project_back(i, chunks, tokens, after(dh1, *t), added, g[0:1], p_qkv))
        t = (backs[-1][0],)
        if i == 0:
            t = slot(t, [last, first, proj], [last, first])
    grad_tokens, more = (jnp.concatenate(v, axis=0) for v in zip(*backs))
    grad_embed = jnp.sum(onehot[:, :, None] * more[:, None, 1, :], axis=0)
    grad_gains = jnp.concatenate([more[:, 0:1], sums_mid[:, 0:2], sums_out[:, 0:1]], axis=1).sum(axis=0)
    little = SmallSum(jnp.concatenate([grad_gains, grad_embed], axis=0))
    t = slot(t + (little.sent,) if paired() else t, [last, first], [last, first, little])
    grad_down = down.result(*t)
    t = slot((grad_down,), [last, first, little], [last, first, little])
    grad_proj = proj.result()
    t = slot((grad_proj,), [last, first, little], [last, first, little])
    while paired() and last.state != "done":
        moving = [e for e in (last, first) if e.state != "done"] + ([little] if little.bits else [])
        ending = [e for e in (last, first) if e.state != "done"] + ([little] if little.received is not None else [])
        t = slot(t, ending, [])
        moving = [e for e in (last, first) if e.state != "done"] + ([little] if little.bits else [])
        little.received = None
        if moving:
            t = slot(t, [], moving)
    if paired():
        grad_qkv = assemble([(e.kept, e.received) for e in (first, last)])
    else:
        part = first.total.shape[1] // 3
        grad_qkv = jnp.concatenate([e.total[:, i * part : (i + 1) * part] for i in range(3) for e in (first, last)], axis=1)
    small_sum = little.result()
    return (
        output,
        grad_tokens,
        grad_qkv,
        grad_proj,
        up.result(*t),
        grad_down,
        small_sum[: gains.shape[0]],
        small_sum[gains.shape[0] :],
    )


def solution(mesh):
    by_seq = P(("dp", "fsdp"), None, None)
    by_slot = P(("dp", "fsdp"))
    by_row = P("fsdp", None)
    by_col = P(None, "fsdp")
    return jax.shard_map(
        local,
        mesh=mesh,
        in_specs=(by_seq, by_seq, by_slot, by_slot) + (by_row,) * 4 + (by_col,) * 2,
        out_specs=(by_seq, by_seq) + (by_row,) * 4 + (by_col,) * 2,
        check_vma=False,
    )
```

time: 3730 us -> 701 us (0.19)
  waiting for transfers between devices: 1550 us -> 80.8 us
  matrix products: 1030 us -> 0 us
  local copies, waits for them, and re-layouts: 751 us -> 14.7 us
  Pallas kernels: 0 us -> 485 us
  other arithmetic: 257 us -> 50 us
  blocking collectives: 80.8 us -> 0 us
  starting transfers between devices: 0.33 us -> 48.6 us
  loops' own time: 40.2 us -> 0 us
    dot_general x50 -> x0, matrix products: 1030 us -> none  [the longest x4 161 us: one_block(): jnp.einsum('hqk,qhd->khd', grad_scores, query_part, preferred_element_typ...]
    unnamed x11 -> x3, waiting for transfers between devices: 879 us -> 0.05 us
    pallas_call x0 -> x29, Pallas kernels: none -> 485 us  [the longest x10 130 us: grad_blocks(): pl.pallas_call(kernel, grid_spec=pltpu.PrefetchScalarGridSpec(num_scalar_...]
    psum x1 -> x0, waiting for transfers between devices: 371 us -> none  [local(): lax.psum((mine[0], mine[1], mine[2], mine[3], mine[4], mine[5]), 'dp')]
    all_gather x4 -> x3, waiting for transfers between devices: 302 us -> 0.02 us  [the longest x1 0.02 us: send(): self.other = lax.all_gather(value, 'dp', axis=0, tiled=True)]
    unnamed x31 -> x59, local copies, waits for them, and re-layouts: 298 us -> 6.93 us
    reduce_sum x34 -> x3, other arithmetic: 184 us -> 0.21 us  [the longest x1 0.1 us: local(): added = jnp.sum(onehot[:, :, None] * embed[None], axis=1)[:, None, :]]
    dynamic_update_slice x22 -> x0, local copies, waits for them, and re-layouts: 135 us -> none  [local(): output, kept_all = lax.map(run_forward, (tokens, group_ids, slot_live))]
  transfers between devices with their start and end apart: 8 -> 55, of which waited for: 8 -> 19; matrix products, arithmetic and copies ran while one was open for 8% -> 6% of each run, Pallas kernels for 0% -> 54%
where the time goes in v1:
time: 701 us; the launch traced here: 695 us
  Pallas kernels  485 us (69%)
  waiting for transfers between devices  80.8 us (12%)
  other arithmetic  50 us (7%)
  starting transfers between devices  48.6 us (7%)
  between operations  15.6 us (2%)
  local copies, waits for them, and re-layouts  14.7 us (2%)
    pallas_call x10, Pallas kernels, grad_blocks(): pl.pallas_call(kernel, grid_spec=pltpu.PrefetchScalarGridSpec(num_scalar_...  130 us
    ppermute x52, waiting for transfers between devices, swap(): return lax.ppermute(value, axis, [(i, i ^ 1 << bit) for i in range(size)])  80.7 us
    pallas_call x4, Pallas kernels, attn_bwd(): pl.pallas_call(attn_bwd_kernel, grid=(slots, count), in_specs=[triple, si...  78 us
    pallas_call x1, Pallas kernels, up_and_down(): pl.pallas_call(kernel, grid_spec=pltpu.PrefetchScalarGridSpec(num_scalar_...  69.8 us
    ppermute x52, starting transfers between devices, swap(): return lax.ppermute(value, axis, [(i, i ^ 1 << bit) for i in range(size)])  48.3 us
    pallas_call x4, Pallas kernels, attn_fwd(): pl.pallas_call(kernel, grid=(slots, count), in_specs=[pl.BlockSpec((3, 1,...  46 us
    pallas_call x1, Pallas kernels, back_to_mixture(): pl.pallas_call(kernel, grid_spec=pltpu.PrefetchScalarGridSpec(num_scalar_...  43.5 us
    pallas_call x2, Pallas kernels, project_back(): pl.pallas_call(kernel, grid_spec=pltpu.PrefetchScalarGridSpec(num_scalar_...  35.6 us
  transfers between devices with their start and end apart: 55, of which 19 were waited for; matrix products, arithmetic and copies ran while one was open for 6% of the time, Pallas kernels for 54%

profile of v1, /device:TPU:0, one launch (start us, length us, event | category | flops | bytes accessed | tf_op | source)
XLA Modules:
  0.0 695.0 jit_solution(9357759338984812960)
XLA Ops:
  39.4 15.6 %project_in.2 = (bf16[2,1088,1024]{2,1,0:T(8,128)(2,1)}, bf16[3,2,1088,512]{3,2,1,0:T(8,128)(2,1)}) custom-call(s32[3]{0:T(128)} %pad_add_fusion.starts_ref, f32[2,1088,1024]{2,1,0:T(8,128)} %refs_in_4_.3, f32[2,1,1024]{2,1,0:T(1,128)} %broadcast_in_dim.2.e_ref.refs_in_6_, f32[1,1024]{1,0:T(1,128)} %maximum_convert_fusion.2.g_ref.refs_in_7_, ...), custom_call_target="tpu_custom_call" | custom-call | flops 14000000000 | bytes 14000000 | tf_op jit(solution)/shard_map/project_in/pallas_call | solution.py:127
  55.7 11.4 %attn_fwd.4 = (bf16[2,1088,1024]{2,1,0:T(8,128)(2,1)}, f32[2,8,2,1088]{3,2,1,0:T(2,128)}) custom-call(bf16[3,2,1088,512]{3,2,1,0:T(8,128)(2,1)} %get-tuple-element.190.x_ref), custom_call_target="tpu_custom_call" | custom-call | flops 16000000000 | bytes 16000000 | tf_op jit(solution)/shard_map/attn_fwd/pallas_call | solution.py:207
  74.7 11.4 %attn_fwd.5 = (bf16[2,1088,1024]{2,1,0:T(8,128)(2,1)}, f32[2,8,2,1088]{3,2,1,0:T(2,128)}) custom-call(bf16[3,2,1088,512]{3,2,1,0:T(8,128)(2,1)} %get-tuple-element.190.x_ref, bf16[2,1088,1024]{2,1,0:T(8,128)(2,1)} %get-tuple-element.184.rest_0_, f32[2,8,2,1088]{3,2,1,0:T(2,128)} %get-tuple-element.191.rest_1_), custom_call_target="tpu_custom_call", output_to_operand_aliasing={{0}: (1, {}), {1}: (2, {})} | custom-call | flops 16000000000 | bytes 16000000 | tf_op jit(solution)/shard_map/attn_fwd/pallas_call | solution.py:207
  87.2 15.6 %project_in.3 = (bf16[2,1088,1024]{2,1,0:T(8,128)(2,1)}, bf16[3,2,1088,512]{3,2,1,0:T(8,128)(2,1)}) custom-call(s32[3]{0:T(128)} %pad_add_fusion.starts_ref, f32[2,1088,1024]{2,1,0:T(8,128)} %refs_in_4_.3, f32[2,1,1024]{2,1,0:T(1,128)} %broadcast_in_dim.2.e_ref.refs_in_6_, f32[1,1024]{1,0:T(1,128)} %maximum_convert_fusion.2.g_ref.refs_in_7_, ...), custom_call_target="tpu_custom_call" | custom-call | flops 14000000000 | bytes 14000000 | tf_op jit(solution)/shard_map/project_in/pallas_call | solution.py:127
  102.8 11.6 %attn_fwd.6 = (bf16[2,1088,1024]{2,1,0:T(8,128)(2,1)}, f32[2,8,2,1088]{3,2,1,0:T(2,128)}) custom-call(bf16[3,2,1088,512]{3,2,1,0:T(8,128)(2,1)} %get-tuple-element.198.x_ref, bf16[2,1088,1024]{2,1,0:T(8,128)(2,1)} %get-tuple-element.192.rest_0_, f32[2,8,2,1088]{3,2,1,0:T(2,128)} %get-tuple-element.195.rest_1_), custom_call_target="tpu_custom_call", output_to_operand_aliasing={{0}: (1, {}), {1}: (2, {})} | custom-call | flops 16000000000 | bytes 16000000 | tf_op jit(solution)/shard_map/attn_fwd/pallas_call | solution.py:207
  124.9 11.5 %attn_fwd.7 = (bf16[2,1088,1024]{2,1,0:T(8,128)(2,1)}, f32[2,8,2,1088]{3,2,1,0:T(2,128)}) custom-call(bf16[3,2,1088,512]{3,2,1,0:T(8,128)(2,1)} %get-tuple-element.198.x_ref, bf16[2,1088,1024]{2,1,0:T(8,128)(2,1)} %get-tuple-element.196.rest_0_, f32[2,8,2,1088]{3,2,1,0:T(2,128)} %get-tuple-element.199.rest_1_), custom_call_target="tpu_custom_call", output_to_operand_aliasing={{0}: (1, {}), {1}: (2, {})} | custom-call | flops 16000000000 | bytes 16000000 | tf_op jit(solution)/shard_map/attn_fwd/pallas_call | solution.py:207
  137.8 69.8 %up_and_down.1 = (bf16[2,1088,1024]{2,1,0:T(8,128)(2,1)}, bf16[2,1088,4096]{2,1,0:T(8,128)(2,1)}, bf16[2,1088,4096]{2,1,0:T(8,128)(2,1)}, bf16[2,1088,1024]{2,1,...) custom-call(s32[8]{0:T(128)} %stack.51.starts_ref, ...), custom_call_target="tpu_custom_call" | custom-call | flops 80000000000 | bytes 80000000 | tf_op jit(solution)/shard_map/up_and_down/pallas_call | solution.py:355
  207.6 15.3 %grad_blocks.10 = bf16[2,1,1024,1024]{3,2,1,0:T(8,128)(2,1)} custom-call(s32[2]{0:T(128)} %pad_add_fusion.3.order_ref, bf16[2176,4096]{1,0:T(8,128)(2,1)} %bitcast.246, bf16[2176,1024]{1,0:T(8,128)(2,1)} %bitcast.250), custom_call_target="tpu_custom_call" | custom-call | flops 8999999488 | bytes 9000000 | tf_op jit(solution)/shard_map/grad_blocks/pallas_call | solution.py:582
  230.5 16.5 %grad_blocks.11 = (bf16[1,1024,1024]{2,1,0:T(8,128)(2,1)}, bf16[1,1024,1024]{2,1,0:T(8,128)(2,1)}) custom-call(s32[2]{0:T(128)} %get-tuple-element.360.order_ref, bf16[2176,4096]{1,0:T(8,128)(2,1)} %bitcast.247, bf16[2176,1024]{1,0:T(8,128)(2,1)} %bitcast.251, bf16[2,1,1024,1024]{3,2,1,0:T(8,128)(2,1)} %collective-permute-done.10.rest_1_), custom_call_target="tpu_custom_call" | custom-call | flops 8999999488 | bytes 9000000 | tf_op jit(solution)/shard_map/grad_blocks/pallas_call | solution.py:582
  247.6 29.3 %back_to_hidden.1.du_ref = bf16[2,1088,4096]{2,1,0:T(8,128)(2,1)} custom-call(s32[2]{0:T(128)} %get-tuple-element.359.starts_ref, bf16[2,1088,1024]{2,1,0:T(8,128)(2,1)} %get-tuple-element.209.dm_ref, bf16[2,1088,4096]{2,1,0:T(8,128)(2,1)} %get-tuple-element.210.slope_ref, bf16[2048,1024]{1,0:T(8,128)(2,1)} %convert_element_type.833.rest_6_.rest_0_, ...), custom_call_target="tpu_custom_call" | custom-call | flops 24999999488 | bytes 25000000 | tf_op jit(solution)/shard_map/back_to_hidden/pallas_call | solution.py:395
  276.9 19.8 %grad_blocks.12 = bf16[2,4,256,1024]{3,2,1,0:T(8,128)(2,1)} custom-call(s32[2]{0:T(128)} %pad_add_fusion.3.order_ref, bf16[2176,1024]{1,0:T(8,128)(2,1)} %bitcast.248, bf16[2176,4096]{1,0:T(8,128)(2,1)} %bitcast.244), custom_call_target="tpu_custom_call" | custom-call | flops 8999999488 | bytes 9000000 | tf_op jit(solution)/shard_map/grad_blocks/pallas_call | solution.py:582
  307.7 20.4 %grad_blocks.13 = (bf16[4,256,1024]{2,1,0:T(8,128)(2,1)}, bf16[4,256,1024]{2,1,0:T(8,128)(2,1)}) custom-call(s32[2]{0:T(128)} %get-tuple-element.360.order_ref, bf16[2176,1024]{1,0:T(8,128)(2,1)} %bitcast.249, bf16[2176,4096]{1,0:T(8,128)(2,1)} %bitcast.245, bf16[2,4,256,1024]{3,2,1,0:T(8,128)(2,1)} %collective-permute-done.12.rest_1_), custom_call_target="tpu_custom_call" | custom-call | flops 8999999488 | bytes 9000000 | tf_op jit(solution)/shard_map/grad_blocks/pallas_call | solution.py:582
  329.6 43.5 %back_to_mixture.1 = (bf16[2,1088,1024]{2,1,0:T(8,128)(2,1)}, bf16[2,1088,1024]{2,1,0:T(8,128)(2,1)}, f32[2,1088,1024]{2,1,0:T(8,128)}, f32[2,8,1024]{2,1,0:T(8,128)}) custom-call(s32[6]{0:T(128)} %stack.61.starts_ref, s32[2]{0:T(128)} %compare_convert_fusion.1.live_ref, bf16[2,1088,4096]{2,1,0:T(8,128)(2,1)} %back_to_hidden.1.du_ref, ...), custom_call_target="tpu_custom_call" | custom-call | flops 40000000000 | bytes 40000000 | tf_op jit(solution)/shard_map/back_to_mixture/pallas_call | solution.py:450
  383.1 19.5 %attn_bwd.4.refs_in_0_ = bf16[3,2,1088,256]{3,2,1,0:T(8,128)(2,1)} custom-call(bf16[3,2,1088,512]{3,2,1,0:T(8,128)(2,1)} %get-tuple-element.190.x_ref, bf16[2,1088,1024]{2,1,0:T(8,128)(2,1)} %get-tuple-element.200.o_ref, bf16[2,1088,1024]{2,1,0:T(8,128)(2,1)} %get-tuple-element.260.do_ref, f32[2,8,2,1088]{3,2,1,0:T(2,128)} %get-tuple-element.227.l_ref), custom_call_target="tpu_custom_call" | custom-call | flops 12000000000 | bytes 12000000 | tf_op jit(solution)/shard_map/attn_bwd/pallas_call | solution.py:277
  421.1 19.6 %attn_bwd.5.refs_in_1_ = bf16[3,2,1088,256]{3,2,1,0:T(8,128)(2,1)} custom-call(bf16[3,2,1088,512]{3,2,1,0:T(8,128)(2,1)} %get-tuple-element.190.x_ref, bf16[2,1088,1024]{2,1,0:T(8,128)(2,1)} %get-tuple-element.200.o_ref, bf16[2,1088,1024]{2,1,0:T(8,128)(2,1)} %get-tuple-element.260.do_ref, f32[2,8,2,1088]{3,2,1,0:T(2,128)} %get-tuple-element.227.l_ref), custom_call_target="tpu_custom_call" | custom-call | flops 12000000000 | bytes 12000000 | tf_op jit(solution)/shard_map/attn_bwd/pallas_call | solution.py:277
  449.6 10.7 %grad_blocks.16 = bf16[2,3,256,512]{3,2,1,0:T(8,128)(2,1)} custom-call(s32[2]{0:T(128)} %pad_add_fusion.3.order_ref, bf16[2176,1024]{1,0:T(8,128)(2,1)} %bitcast.183, bf16[3,2176,256]{2,1,0:T(8,128)(2,1)} %bitcast.191, bf16[3,2176,256]{2,1,0:T(8,128)(2,1)} %bitcast.193), custom_call_target="tpu_custom_call" | custom-call | flops 3000000000 | bytes 3000000 | tf_op jit(solution)/shard_map/grad_blocks/pallas_call | solution.py:582
  462.6 19.4 %attn_bwd.6.refs_in_2_ = bf16[3,2,1088,256]{3,2,1,0:T(8,128)(2,1)} custom-call(bf16[3,2,1088,512]{3,2,1,0:T(8,128)(2,1)} %get-tuple-element.198.x_ref, bf16[2,1088,1024]{2,1,0:T(8,128)(2,1)} %get-tuple-element.200.o_ref, bf16[2,1088,1024]{2,1,0:T(8,128)(2,1)} %get-tuple-element.260.do_ref, f32[2,8,2,1088]{3,2,1,0:T(2,128)} %get-tuple-element.227.l_ref), custom_call_target="tpu_custom_call" | custom-call | flops 12000000000 | bytes 12000000 | tf_op jit(solution)/shard_map/attn_bwd/pallas_call | solution.py:277
  490.7 11.0 %grad_blocks.17 = (bf16[3,256,512]{2,1,0:T(8,128)(2,1)}, bf16[3,256,512]{2,1,0:T(8,128)(2,1)}) custom-call(s32[2]{0:T(128)} %get-tuple-element.360.order_ref, bf16[2176,1024]{1,0:T(8,128)(2,1)} %bitcast.184, bf16[3,2176,256]{2,1,0:T(8,128)(2,1)} %bitcast.192, bf16[3,2176,256]{2,1,0:T(8,128)(2,1)} %bitcast.194, bf16[2,3,256,512]{3,2,1,0:T(8,128)(2,1)} %copy-done.6), custom_call_target="tpu_custom_call" | custom-call | flops 3000000000 | bytes 3000000 | tf_op jit(solution)/shard_map/grad_blocks/pallas_call | solution.py:582
  503.6 19.4 %attn_bwd.7.refs_in_3_ = bf16[3,2,1088,256]{3,2,1,0:T(8,128)(2,1)} custom-call(bf16[3,2,1088,512]{3,2,1,0:T(8,128)(2,1)} %get-tuple-element.198.x_ref, bf16[2,1088,1024]{2,1,0:T(8,128)(2,1)} %get-tuple-element.200.o_ref, bf16[2,1088,1024]{2,1,0:T(8,128)(2,1)} %get-tuple-element.260.do_ref, f32[2,8,2,1088]{3,2,1,0:T(2,128)} %get-tuple-element.227.l_ref), custom_call_target="tpu_custom_call" | custom-call | flops 12000000000 | bytes 12000000 | tf_op jit(solution)/shard_map/attn_bwd/pallas_call | solution.py:277
  526.3 10.8 %grad_blocks.18 = bf16[2,3,256,512]{3,2,1,0:T(8,128)(2,1)} custom-call(s32[2]{0:T(128)} %pad_add_fusion.3.order_ref, bf16[2176,1024]{1,0:T(8,128)(2,1)} %bitcast.185, bf16[3,2176,256]{2,1,0:T(8,128)(2,1)} %bitcast.195, bf16[3,2176,256]{2,1,0:T(8,128)(2,1)} %bitcast.197), custom_call_target="tpu_custom_call" | custom-call | flops 3000000000 | bytes 3000000 | tf_op jit(solution)/shard_map/grad_blocks/pallas_call | solution.py:582
  559.5 11.0 %grad_blocks.19 = (bf16[3,256,512]{2,1,0:T(8,128)(2,1)}, bf16[3,256,512]{2,1,0:T(8,128)(2,1)}) custom-call(s32[2]{0:T(128)} %get-tuple-element.360.order_ref, bf16[2176,1024]{1,0:T(8,128)(2,1)} %bitcast.186, bf16[3,2176,256]{2,1,0:T(8,128)(2,1)} %bitcast.196, bf16[3,2176,256]{2,1,0:T(8,128)(2,1)} %bitcast.198, bf16[2,3,256,512]{3,2,1,0:T(8,128)(2,1)} %copy-done.5), custom_call_target="tpu_custom_call" | custom-call | flops 3000000000 | bytes 3000000 | tf_op jit(solution)/shard_map/grad_blocks/pallas_call | solution.py:582
  574.0 17.9 %project_back.2 = (f32[1,1088,1024]{2,1,0:T(8,128)}, f32[1,8,1024]{2,1,0:T(8,128)}) custom-call(s32[6]{0:T(128)} %stack.61.starts_ref, bf16[3,2,1088,256]{3,2,1,0:T(8,128)(2,1)} %attn_bwd.4.refs_in_0_, bf16[3,2,1088,256]{3,2,1,0:T(8,128)(2,1)} %attn_bwd.5.refs_in_1_, bf16[3,2,1088,256]{3,2,1,0:T(8,128)(2,1)} %attn_bwd.6.refs_in_2_, ...), custom_call_target="tpu_custom_call" | custom-call | flops 15000000512 | bytes 15000000 | tf_op jit(solution)/shard_map/project_back/pallas_call | solution.py:513
  596.6 17.7 %project_back.3 = (f32[1,1088,1024]{2,1,0:T(8,128)}, f32[1,8,1024]{2,1,0:T(8,128)}) custom-call(s32[6]{0:T(128)} %stack.61.starts_ref, bf16[3,2,1088,256]{3,2,1,0:T(8,128)(2,1)} %attn_bwd.4.refs_in_0_, bf16[3,2,1088,256]{3,2,1,0:T(8,128)(2,1)} %attn_bwd.5.refs_in_1_, bf16[3,2,1088,256]{3,2,1,0:T(8,128)(2,1)} %attn_bwd.6.refs_in_2_, ...), custom_call_target="tpu_custom_call" | custom-call | flops 15000000512 | bytes 15000000 | tf_op jit(solution)/shard_map/project_back/pallas_call | solution.py:513
  662.7 9.2 %pad_maximum_fusion = f32[2,1088,1024]{2,1,0:T(8,128)} fusion(f32[1,1088,1024]{2,1,0:T(8,128)} %get-tuple-element.291, f32[1,1088,1024]{2,1,0:T(8,128)} %get-tuple-element.284), kind=kLoop, calls=%fused_computation | loop fusion | flops 2228224 | bytes 17825792 | tf_op jit(solution)/shard_map/concatenate | solution.py:971
  (251 shorter events, 221.3 us)
Async XLA Ops:
  7.2 129.3 %all-gather.6.cloned.1.call-start = ((), (), s32[]{:S(2)}) async-start(), calls=%async_computation | async-start | bytes 4456448 | tf_op jit(solution)/shard_map/all_gather | solution.py:693
  37.2 29.9 %collective-permute-start.2 = (bf16[3,256,512]{2,1,0:T(8,128)(2,1)S(1)}, bf16[3,256,512]{2,1,0:T(8,128)(2,1)}, u32[]{:S(2)}, u32[]{:S(2)}) collective-permute-start(bf16[3,256,512]{2,1,0:T(8,128)(2,1)S(1)} %copy-done.10), channel_id=1, source_target_pairs={{0,1},{1,0},{2,3},{3,2},{4,5},{5,4},{6,7},{7,6},{8,9},{9,8},{10,11... | collective-permute-start | bytes 2359304 | tf_op jit(solution)/shard_map/ppermute | solution.py:605
  55.0 563.2 %all-gather.8.cloned.1.call-start = ((), (), s32[]{:S(2)}) async-start(), calls=%async_computation.1 | async-start | bytes 4456448 | tf_op jit(solution)/shard_map/all_gather | solution.py:837
  74.3 47.6 %collective-permute-start.8 = (bf16[256,4096]{1,0:T(8,128)(2,1)S(1)}, bf16[256,4096]{1,0:T(8,128)(2,1)}, u32[]{:S(2)}, u32[]{:S(2)}) collective-permute-start(bf16[256,4096]{1,0:T(8,128)(2,1)S(1)} %constant_dynamic-slice_fusion.2), channel_id=1, source_target_pairs={{0,1},{1,0},{2,3},{3,2},{4,5},{5,4},{6,7},{7,6},{8,9},{9,8},{10,11... | collective-permute-start | bytes 6291464 | tf_op jit(solution)/shard_map/ppermute | solution.py:605
  247.0 49.6 %collective-permute-start.11 = (bf16[1,1024,1024]{2,1,0:T(8,128)(2,1)}, bf16[1,1024,1024]{2,1,0:T(8,128)(2,1)}, u32[]{:S(2)}, u32[]{:S(2)}) collective-permute-start(bf16[1,1024,1024]{2,1,0:T(8,128)(2,1)} %get-tuple-element.208), channel_id=1, source_target_pairs={{0,1},{1,0},{2,3},{3,2},{4,5},{5,4},{6,7},{7,6},{8,9},{9,8},{10,11... | collective-permute-start | bytes 6291464 | tf_op jit(solution)/shard_map/ppermute | solution.py:605
  300.9 72.2 %collective-permute-start.13 = (bf16[1,512,1024]{2,1,0:T(8,128)(2,1)}, bf16[1,512,1024]{2,1,0:T(8,128)(2,1)S(1)}, u32[]{:S(2)}, u32[]{:S(2)}) collective-permute-start(bf16[1,512,1024]{2,1,0:T(8,128)(2,1)} %get-tuple-element.216), channel_id=1, source_target_pairs={{0,4},{2,6},{4,0},{6,2},{8,12},{10,14},{12,8},{14,10},{16,20},{18,... | collective-permute-start | bytes 3145736 | tf_op jit(solution)/shard_map/ppermute | solution.py:605
  328.1 74.6 %collective-permute-start.14 = (bf16[4,256,1024]{2,1,0:T(8,128)(2,1)}, bf16[4,256,1024]{2,1,0:T(8,128)(2,1)}, u32[]{:S(2)}, u32[]{:S(2)}) collective-permute-start(bf16[4,256,1024]{2,1,0:T(8,128)(2,1)} %get-tuple-element.218), channel_id=1, source_target_pairs={{0,1},{1,0},{2,3},{3,2},{4,5},{5,4},{6,7},{7,6},{8,9},{9,8},{10,11... | collective-permute-start | bytes 6291464 | tf_op jit(solution)/shard_map/ppermute | solution.py:605
  374.4 28.3 %collective-permute-start.15 = (bf16[1,256,1024]{2,1,0:T(8,128)(2,1)}, bf16[1,256,1024]{2,1,0:T(8,128)(2,1)}, u32[]{:S(2)}, u32[]{:S(2)}) collective-permute-start(bf16[1,256,1024]{2,1,0:T(8,128)(2,1)} %get-tuple-element.340), channel_id=1, source_target_pairs={{0,8},{2,10},{4,12},{6,14},{8,0},{10,2},{12,4},{14,6},{16,24},{18,... | collective-permute-start | bytes 1572872 | tf_op jit(solution)/shard_map/ppermute | solution.py:605
  408.8 31.9 %collective-permute-start.18 = (bf16[1,128,1024]{2,1,0:T(8,128)(2,1)}, bf16[1,128,1024]{2,1,0:T(8,128)(2,1)S(1)}, u32[]{:S(2)}, u32[]{:S(2)}) collective-permute-start(bf16[1,128,1024]{2,1,0:T(8,128)(2,1)} %fusion.8), channel_id=1, source_target_pairs={{0,16},{2,18},{4,20},{6,22},{8,24},{10,26},{12,28},{14,30},{16,0},... | collective-permute-start | bytes 786440 | tf_op jit(solution)/shard_map/ppermute | solution.py:605
  418.8 21.9 %collective-permute-start.19 = (bf16[1,256,1024]{2,1,0:T(8,128)(2,1)}, bf16[1,256,1024]{2,1,0:T(8,128)(2,1)S(1)}, u32[]{:S(2)}, u32[]{:S(2)}) collective-permute-start(bf16[1,256,1024]{2,1,0:T(8,128)(2,1)} %get-tuple-element.235), channel_id=1, source_target_pairs={{0,1},{1,0},{2,3},{3,2},{4,5},{5,4},{6,7},{7,6},{8,9},{9,8},{10,11... | collective-permute-start | bytes 1572872 | tf_op jit(solution)/shard_map/ppermute | solution.py:605
  419.6 25.2 %collective-permute-start.17 = (bf16[4,128,1024]{2,1,0:T(8,128)(2,1)}, bf16[4,128,1024]{2,1,0:T(8,128)(2,1)S(1)}, u32[]{:S(2)}, u32[]{:S(2)}) collective-permute-start(bf16[4,128,1024]{2,1,0:T(8,128)(2,1)} %get-tuple-element.231), channel_id=1, source_target_pairs={{0,4},{2,6},{4,0},{6,2},{8,12},{10,14},{12,8},{14,10},{16,20},{18,... | collective-permute-start | bytes 3145736 | tf_op jit(solution)/shard_map/ppermute | solution.py:605
  448.0 232.6 %all-gather.10.cloned.1.call-start = ((), (), s32[]{:S(2)}) async-start(), calls=%async_computation.2 | async-start | bytes 4456448 | tf_op jit(solution)/shard_map/all_gather | solution.py:837
  460.4 26.5 %collective-permute-start.23 = (bf16[2,3,256,512]{3,2,1,0:T(8,128)(2,1)}, bf16[2,3,256,512]{3,2,1,0:T(8,128)(2,1)S(1)}, u32[]{:S(2)}, u32[]{:S(2)}) collective-permute-start(bf16[2,3,256,512]{3,2,1,0:T(8,128)(2,1)} %grad_blocks.16), channel_id=1, source_target_pairs={{0,2},{2,0},{4,6},{6,4},{8,10},{10,8},{12,14},{14,12},{16,18},{18,... | collective-permute-start | bytes 4718600 | tf_op jit(solution)/shard_map/ppermute | solution.py:605
  460.5 26.4 %collective-permute-start.21 = (bf16[4,64,1024]{2,1,0:T(8,128)(2,1)}, bf16[4,64,1024]{2,1,0:T(8,128)(2,1)S(1)}, u32[]{:S(2)}, u32[]{:S(2)}) collective-permute-start(bf16[4,64,1024]{2,1,0:T(8,128)(2,1)} %get-tuple-element.242), channel_id=1, source_target_pairs={{0,8},{2,10},{4,12},{6,14},{8,0},{10,2},{12,4},{14,6},{16,24},{18,... | collective-permute-start | bytes 1572872 | tf_op jit(solution)/shard_map/ppermute | solution.py:605
  461.0 25.8 %collective-permute-start.22 = (bf16[1,64,1024]{2,1,0:T(8,128)(2,1)S(1)}, bf16[1,64,1024]{2,1,0:T(8,128)(2,1)S(1)}, u32[]{:S(2)}, u32[]{:S(2)}) collective-permute-start(bf16[1,64,1024]{2,1,0:T(8,128)(2,1)S(1)} %get-tuple-element.248), channel_id=1, source_target_pairs={{0,8},{2,10},{4,12},{6,14},{8,0},{10,2},{12,4},{14,6},{16,24},{18,... | collective-permute-start | bytes 393224 | tf_op jit(solution)/shard_map/ppermute | solution.py:605
  487.8 35.3 %collective-permute-start.25 = (bf16[4,32,1024]{2,1,0:T(8,128)(2,1)}, bf16[4,32,1024]{2,1,0:T(8,128)(2,1)S(1)}, u32[]{:S(2)}, u32[]{:S(2)}) collective-permute-start(bf16[4,32,1024]{2,1,0:T(8,128)(2,1)} %fusion.11), channel_id=1, source_target_pairs={{0,16},{2,18},{4,20},{6,22},{8,24},{10,26},{12,28},{14,30},{16,0},... | collective-permute-start | bytes 786440 | tf_op jit(solution)/shard_map/ppermute | solution.py:605
  502.0 21.1 %collective-permute-start.27 = (bf16[1,32,1024]{2,1,0:T(8,128)(2,1)S(1)}, bf16[1,32,1024]{2,1,0:T(8,128)(2,1)S(1)}, u32[]{:S(2)}, u32[]{:S(2)}) collective-permute-start(bf16[1,32,1024]{2,1,0:T(8,128)(2,1)S(1)} %fusion.19), channel_id=1, source_target_pairs={{0,16},{2,18},{4,20},{6,22},{8,24},{10,26},{12,28},{14,30},{16,0},... | collective-permute-start | bytes 196616 | tf_op jit(solution)/shard_map/ppermute | solution.py:605
  502.0 21.1 %collective-permute-start.26 = (bf16[3,256,512]{2,1,0:T(8,128)(2,1)}, bf16[3,256,512]{2,1,0:T(8,128)(2,1)S(1)}, u32[]{:S(2)}, u32[]{:S(2)}) collective-permute-start(bf16[3,256,512]{2,1,0:T(8,128)(2,1)} %get-tuple-element.258), channel_id=1, source_target_pairs={{0,1},{1,0},{2,3},{3,2},{4,5},{5,4},{6,7},{7,6},{8,9},{9,8},{10,11... | collective-permute-start | bytes 2359304 | tf_op jit(solution)/shard_map/ppermute | solution.py:605
  537.2 19.8 %collective-permute-start.29 = (bf16[2,3,256,512]{3,2,1,0:T(8,128)(2,1)}, bf16[2,3,256,512]{3,2,1,0:T(8,128)(2,1)S(1)}, u32[]{:S(2)}, u32[]{:S(2)}) collective-permute-start(bf16[2,3,256,512]{3,2,1,0:T(8,128)(2,1)} %grad_blocks.18), channel_id=1, source_target_pairs={{0,2},{2,0},{4,6},{6,4},{8,10},{10,8},{12,14},{14,12},{16,18},{18,... | collective-permute-start | bytes 4718600 | tf_op jit(solution)/shard_map/ppermute | solution.py:605
  559.5 33.2 %collective-permute-start.35 = (bf16[1,256,1024]{2,1,0:T(8,128)(2,1)S(1)}, bf16[1,256,1024]{2,1,0:T(8,128)(2,1)}, u32[]{:S(2)}, u32[]{:S(2)}) collective-permute-start(bf16[1,256,1024]{2,1,0:T(8,128)(2,1)S(1)} %maximum_select_fusion.2.refs_0_), channel_id=1, source_target_pairs={{0,2},{2,0},{4,6},{6,4},{8,10},{10,8},{12,14},{14,12},{16,18},{18,... | collective-permute-start | bytes 1572872 | tf_op jit(solution)/shard_map/ppermute | solution.py:605
  570.5 22.2 %collective-permute-start.34 = (bf16[3,32,512]{2,1,0:T(8,128)(2,1)S(1)}, bf16[3,32,512]{2,1,0:T(8,128)(2,1)S(1)}, u32[]{:S(2)}, u32[]{:S(2)}) collective-permute-start(bf16[3,32,512]{2,1,0:T(8,128)(2,1)S(1)} %fusion.20), channel_id=1, source_target_pairs={{0,16},{2,18},{4,20},{6,22},{8,24},{10,26},{12,28},{14,30},{16,0},... | collective-permute-start | bytes 294920 | tf_op jit(solution)/shard_map/ppermute | solution.py:605
  573.8 19.9 %collective-permute-start.33 = (bf16[3,256,512]{2,1,0:T(8,128)(2,1)}, bf16[3,256,512]{2,1,0:T(8,128)(2,1)S(1)}, u32[]{:S(2)}, u32[]{:S(2)}) collective-permute-start(bf16[3,256,512]{2,1,0:T(8,128)(2,1)} %get-tuple-element.281), channel_id=1, source_target_pairs={{0,1},{1,0},{2,3},{3,2},{4,5},{5,4},{6,7},{7,6},{8,9},{9,8},{10,11... | collective-permute-start | bytes 2359304 | tf_op jit(solution)/shard_map/ppermute | solution.py:605
  593.9 21.4 %collective-permute-start.37 = (bf16[3,32,512]{2,1,0:T(8,128)(2,1)S(1)}, bf16[3,32,512]{2,1,0:T(8,128)(2,1)S(1)}, u32[]{:S(2)}, u32[]{:S(2)}) collective-permute-start(bf16[3,32,512]{2,1,0:T(8,128)(2,1)S(1)} %fusion.17), channel_id=1, source_target_pairs={{0,16},{2,18},{4,20},{6,22},{8,24},{10,26},{12,28},{14,30},{16,0},... | collective-permute-start | bytes 294920 | tf_op jit(solution)/shard_map/ppermute | solution.py:605
  594.4 21.0 %collective-permute-start.36 = (bf16[3,128,512]{2,1,0:T(8,128)(2,1)S(1)}, bf16[3,128,512]{2,1,0:T(8,128)(2,1)S(1)}, u32[]{:S(2)}, u32[]{:S(2)}) collective-permute-start(bf16[3,128,512]{2,1,0:T(8,128)(2,1)S(1)} %get-tuple-element.288), channel_id=1, source_target_pairs={{0,4},{2,6},{4,0},{6,2},{8,12},{10,14},{12,8},{14,10},{16,20},{18,... | collective-permute-start | bytes 1179656 | tf_op jit(solution)/shard_map/ppermute | solution.py:605
  (59 other events, 651.6 us)
Sparse Core Ops, SparseCore 0:
  55.1 51.0 all-gather.5
  448.1 63.4 all-gather.7
  541.2 56.3 all-gather.9

commit v2 on v1

--- a/solution.py
+++ b/solution.py
@@ -23,10 +23,6 @@
     return pltpu.CompilerParams(vmem_limit_bytes=VMEM_BYTES)
 
 
-def cost(micros):
-    return pl.CostEstimate(flops=int(micros * 1e9), bytes_accessed=int(micros * 1e6), transcendentals=0)
-
-
 def row_block(length, most):
     return max(b for b in range(16, most + 1, 16) if length % b == 0)
 
@@ -35,6 +31,11 @@
     centered = rows - jnp.mean(rows, axis=-1, keepdims=True)
     inv_std = lax.rsqrt(jnp.mean(centered * centered, axis=-1, keepdims=True) + EPSILON)
     return centered * inv_std, inv_std
+
+
+def halves(rows):
+    middle = rows // 32 * 16
+    return [slice(0, middle), slice(middle, rows)] if middle else [slice(0, rows)]
 
 
 def norm_back(gradient, unit, inv_std, gain):
@@ -97,55 +98,57 @@
         getattr(copy, method)()
 
 
-def project_in(tokens, added, gain, weight):
+def norm_in(tokens, added, gain):
     slots, length, width = tokens.shape
+    block = row_block(length, 544)
+
+    def kernel(x_ref, e_ref, g_ref, a_ref):
+        a_ref[0] = (normed(x_ref[0] + e_ref[0])[0] * g_ref[...]).astype(jnp.bfloat16)
+
+    rows = pl.BlockSpec((1, block, width), lambda s, i: (s, i, 0))
+    return pl.pallas_call(
+        kernel,
+        grid=(slots, length // block),
+        in_specs=[rows, pl.BlockSpec((1, 1, width), lambda s, i: (s, 0, 0)), pl.BlockSpec((1, width), lambda s, i: (0, 0))],
+        out_specs=rows,
+        out_shape=jax.ShapeDtypeStruct(tokens.shape, jnp.bfloat16),
+        compiler_params=params(),
+        name="norm_in",
+    )(tokens, added, gain)
+
+
+def project_in(a1, weight):
+    slots, length, width = a1.shape
     part = weight[1][2]
     block = row_block(length, 544)
     held = Weights([weight])
     n_held = len(held.refs)
 
-    def kernel(starts_ref, x_ref, e_ref, g_ref, *rest):
-        refs, (a_ref, out_ref), scratch = rest[:n_held], rest[n_held : n_held + 2], rest[n_held + 2 :]
-        first = (pl.program_id(0) == 0) & (pl.program_id(1) == 0)
-        copies = held.copies(starts_ref, refs, scratch)[0]
-
-        @pl.when(first)
+    def kernel(starts_ref, a_ref, *rest):
+        refs, out_ref, scratch = rest[:n_held], rest[n_held], rest[n_held + 1 :]
+
+        @pl.when((pl.program_id(0) == 0) & (pl.program_id(1) == 0))
         def _():
+            copies = held.copies(starts_ref, refs, scratch)[0]
             run_all(copies, "start")
-
-        a = (normed(x_ref[0] + e_ref[0])[0] * g_ref[...]).astype(jnp.bfloat16)
-        a_ref[0] = a
-
-        @pl.when(first)
-        def _():
             run_all(copies, "wait")
 
         for i in range(3):
-            out_ref[i, 0] = dot(a, scratch[0][i], 1, 0).astype(jnp.bfloat16)
-
-    rows = pl.BlockSpec((1, block, width), lambda s, i, _: (s, i, 0))
+            out_ref[i, 0] = dot(a_ref[0], scratch[0][i], 1, 0).astype(jnp.bfloat16)
+
     return pl.pallas_call(
         kernel,
         grid_spec=pltpu.PrefetchScalarGridSpec(
             num_scalar_prefetch=1,
             grid=(slots, length // block),
-            in_specs=[
-                rows,
-                pl.BlockSpec((1, 1, width), lambda s, i, _: (s, 0, 0)),
-                pl.BlockSpec((1, width), lambda s, i, _: (0, 0)),
-            ]
-            + held.in_specs,
-            out_specs=[rows, pl.BlockSpec((3, 1, block, part), lambda s, i, _: (0, s, i, 0))],
+            in_specs=[pl.BlockSpec((1, block, width), lambda s, i, _: (s, i, 0))] + held.in_specs,
+            out_specs=pl.BlockSpec((3, 1, block, part), lambda s, i, _: (0, s, i, 0)),
             scratch_shapes=held.scratch,
         ),
-        out_shape=[
-            jax.ShapeDtypeStruct(tokens.shape, jnp.bfloat16),
-            jax.ShapeDtypeStruct((3, slots, length, part), jnp.bfloat16),
-        ],
+        out_shape=jax.ShapeDtypeStruct((3, slots, length, part), jnp.bfloat16),
         compiler_params=params(),
-        cost_estimate=cost(14),
         name="project_in",
-    )(held.starts, tokens, added, gain, *held.refs)
+    )(held.starts, a1, *held.refs)
 
 
 def causal(scores, keys_first):
@@ -219,7 +222,6 @@
         ],
         input_output_aliases={1 + i: i for i in range(n_before)},
         compiler_params=params(),
-        cost_estimate=cost(8 * count),
         name="attn_fwd",
     )(qkv, *(before or ()))
 
@@ -282,7 +284,6 @@
         out_shape=jax.ShapeDtypeStruct((3, slots, length, count * LANES), jnp.bfloat16),
         scratch_shapes=[pltpu.VMEM((LANES, length), jnp.float32)],
         compiler_params=params(),
-        cost_estimate=cost(6 * count),
         name="attn_bwd",
     )(qkv, mixture, grad_mix, log_totals)
 
@@ -305,8 +306,9 @@
 
     def kernel(starts_ref, live_ref, o_ref, x_ref, c_ref, e_ref, g_ref, *rest):
         refs = rest[:n_held]
-        a_ref, f_ref, slope_ref, dm_ref, z_ref, h_ref, out_ref, sum_ref = rest[n_held : n_held + 8]
+        a_ref, f_ref, du_ref, dm_ref, z_ref, h_ref, out_ref, sum_ref = rest[n_held : n_held + 8]
         wp, wu, wd = rest[n_held + 8 : n_held + 11]
+        slope_ref = rest[n_held + 12]
 
         @pl.when((pl.program_id(0) == 0) & (pl.program_id(1) == 0))
         def _():
@@ -321,31 +323,57 @@
             sum_ref[...] = jnp.zeros_like(sum_ref)
 
         alive = live_ref[pl.program_id(0)].astype(jnp.float32)
-        z = dot(o_ref[0], wp[...], 1, 0)
-        z_ref[0] = z
-        h1 = x_ref[0] + e_ref[0] + normed(z)[0] * g_ref[1:2]
-        h_ref[0] = h1
-        a = (normed(h1)[0] * g_ref[2:3]).astype(jnp.bfloat16)
-        a_ref[0] = a
-        m = []
-
-        def activate(cols, u):
+        parts = halves(block)
+        cols = [slice(j, j + chunk) for j in range(0, hidden, chunk)]
+        h1, a, m, dm = {}, {}, {}, {}
+        zs = [dot(o_ref[0, r, :], wp[...], 1, 0) for r in parts]
+
+        def enter(n):
+            r = parts[n]
+            z_ref[0, r, :] = zs[n]
+            h1[n] = x_ref[0, r, :] + e_ref[0] + normed(zs[n])[0] * g_ref[1:2]
+            h_ref[0, r, :] = h1[n]
+            a[n] = (normed(h1[n])[0] * g_ref[2:3]).astype(jnp.bfloat16)
+            a_ref[0, r, :] = a[n]
+
+        def leave(n):
+            r = parts[n]
+            unit_m, inv_m = normed(m[n])
+            out_ref[0, r, :] = alive * (h1[n] + unit_m * g_ref[3:4])
+            dy = alive * c_ref[0, r, :]
+            dm[n] = norm_back(dy, unit_m, inv_m, g_ref[3:4]).astype(jnp.bfloat16)
+            dm_ref[0, r, :] = dm[n]
+            sum_ref[0, 0:1] += jnp.sum(dy * unit_m, axis=0, keepdims=True)
+
+        def raised(job):
+            n, c = job
+            u = dot(a[n], wu[:, c], 1, 0)
+            if c is cols[1 % len(cols)] and n + 1 < len(parts):
+                enter(n + 1)
+            return u
+
+        def activate(job, u):
+            n, c = job
             f, slope = gelu_parts(u)
-            f_ref[0, :, cols] = f.astype(jnp.bfloat16)
-            slope_ref[0, :, cols] = slope.astype(jnp.bfloat16)
+            f_ref[0, parts[n], c] = f.astype(jnp.bfloat16)
+            slope_ref[parts[n], c] = slope.astype(jnp.bfloat16)
             return f.astype(jnp.bfloat16)
 
-        def lower(cols, f):
-            more = dot(f, wd[cols, :], 1, 0)
-            m[:] = [m[0] + more] if m else [more]
-
-        cols = [slice(j, j + chunk) for j in range(0, hidden, chunk)]
-        staged(cols, lambda c: dot(a, wu[:, c], 1, 0), activate, lower)
-        unit_m, inv_m = normed(m[0])
-        out_ref[0] = alive * (h1 + unit_m * g_ref[3:4])
-        dy = alive * c_ref[0]
-        dm_ref[0] = norm_back(dy, unit_m, inv_m, g_ref[3:4]).astype(jnp.bfloat16)
-        sum_ref[0, 0:1] += jnp.sum(dy * unit_m, axis=0, keepdims=True)
+        def lower(job, f):
+            n, c = job
+            more = dot(f, wd[c, :], 1, 0)
+            m[n] = m[n] + more if n in m else more
+            if c is cols[-1]:
+                leave(n)
+
+        enter(0)
+        staged([(n, c) for n in range(len(parts)) for c in cols], raised, activate, lower)
+        dm = jnp.concatenate([dm[n] for n in range(len(parts))], axis=0)
+
+        def lift(cols, df):
+            du_ref[0, :, cols] = (df * slope_ref[:, cols].astype(jnp.float32)).astype(jnp.bfloat16)
+
+        staged(cols, lambda c: dot(dm, wd[c, :], 1, 1), lift, lambda c, _: None)
 
     rows, per_slot, whole = token_specs(tokens.shape, block)
     wide = pl.BlockSpec((1, block, hidden), lambda s, i, *_: (s, i, 0))
@@ -359,53 +387,12 @@
             grid=(slots, length // block),
             in_specs=[rows, rows, rows, per_slot(1), whole(gains)] + held.in_specs,
             out_specs=[rows, wide, wide, rows, rows, rows, rows, per_slot(8)],
-            scratch_shapes=held.scratch,
+            scratch_shapes=held.scratch + [pltpu.VMEM((block, hidden), jnp.bfloat16)],
         ),
         out_shape=[low, low_wide, low_wide, low, full, full, full, jax.ShapeDtypeStruct((slots, 8, width), jnp.float32)],
         compiler_params=params(),
-        cost_estimate=cost(80),
         name="up_and_down",
     )(held.starts, live, mixture, tokens, cotangent, added, gains, *held.refs)
-
-
-def back_to_hidden(dm, slope, w_down):
-    slots, length, width = dm.shape
-    hidden = slope.shape[-1]
-    block = row_block(length, 544)
-    chunk = min(512, hidden)
-    held = Weights([w_down])
-    n_held = len(held.refs)
-
-    def kernel(starts_ref, dm_ref, slope_ref, *rest):
-        refs, du_ref, scratch = rest[:n_held], rest[n_held], rest[n_held + 1 :]
-
-        @pl.when((pl.program_id(0) == 0) & (pl.program_id(1) == 0))
-        def _():
-            copies = held.copies(starts_ref, refs, scratch)[0]
-            run_all(copies, "start")
-            run_all(copies, "wait")
-
-        dm_block = dm_ref[0]
-        for j in range(0, hidden, chunk):
-            df = dot(dm_block, scratch[0][j : j + chunk, :], 1, 1)
-            du_ref[0, :, j : j + chunk] = (df * slope_ref[0, :, j : j + chunk].astype(jnp.float32)).astype(jnp.bfloat16)
-
-    rows, _, _ = token_specs(dm.shape, block)
-    wide = pl.BlockSpec((1, block, hidden), lambda s, i, *_: (s, i, 0))
-    return pl.pallas_call(
-        kernel,
-        grid_spec=pltpu.PrefetchScalarGridSpec(
-            num_scalar_prefetch=1,
-            grid=(slots, length // block),
-            in_specs=[rows, wide] + held.in_specs,
-            out_specs=wide,
-            scratch_shapes=held.scratch,
-        ),
-        out_shape=jax.ShapeDtypeStruct(slope.shape, jnp.bfloat16),
-        compiler_params=params(),
-        cost_estimate=cost(25),
-        name="back_to_hidden",
-    )(held.starts, dm, slope, *held.refs)
 
 
 def back_to_mixture(live, du, h1, z, cotangent, gains, w_proj, w_up):
@@ -463,23 +450,26 @@
             jax.ShapeDtypeStruct((slots, 8, width), jnp.float32),
         ],
         compiler_params=params(),
-        cost_estimate=cost(40),
         name="back_to_mixture",
     )(held.starts, live, du, h1, z, cotangent, gains, *held.refs)
 
 
-def project_back(slot, groups, tokens, grad_middle, added, gain, weights):
-    _, length, width = tokens.shape
-    block = row_block(length, 272)
+def project_back(slot, part_of, groups, tokens, grad_middle, added, gain, weights, before=None):
+    slots, length, width = tokens.shape
+    block = row_block(length // part_of[1], 272)
     held = Weights(weights)
     per_weight = len(groups) // len(weights)
     n_held = len(held.refs)
+    n_before = 0 if before is None else 2
 
     n_groups, part = len(groups), groups[0].shape[-1]
+    steps = length // part_of[1] // block
+    skip = part_of[0] * steps
 
     def kernel(starts_ref, *refs_in):
         d_refs, (x_ref, h_ref, e_ref, g_ref), rest = refs_in[:n_groups], refs_in[n_groups : n_groups + 4], refs_in[n_groups + 4 :]
-        refs, (out_ref, sum_ref), scratch = rest[:n_held], rest[n_held : n_held + 2], rest[n_held + 2 :]
+        refs, rest = rest[:n_held], rest[n_held + n_before :]
+        (out_ref, sum_ref), scratch = rest[:2], rest[2:]
         first = pl.program_id(0) == 0
         copies = sum(held.copies(starts_ref, refs, scratch), [])
 
@@ -509,34 +499,41 @@
         sum_ref[0, 0:1] += jnp.sum(da * unit, axis=0, keepdims=True)
         sum_ref[0, 1:2] += jnp.sum(dh, axis=0, keepdims=True)
 
-    rows = pl.BlockSpec((1, block, width), lambda i, _: (slot, i, 0))
+    rows = pl.BlockSpec((1, block, width), lambda i, _: (slot, skip + i, 0))
     return pl.pallas_call(
         kernel,
         grid_spec=pltpu.PrefetchScalarGridSpec(
             num_scalar_prefetch=1,
-            grid=(length // block,),
-            in_specs=[pl.BlockSpec((3, 1, block, part), lambda i, _: (0, slot, i, 0))] * n_groups
+            grid=(steps,),
+            in_specs=[pl.BlockSpec((3, 1, block, part), lambda i, _: (0, slot, skip + i, 0))] * n_groups
             + [
                 rows,
                 rows,
                 pl.BlockSpec((1, 1, width), lambda i, _: (slot, 0, 0)),
                 pl.BlockSpec((1, width), lambda i, _: (0, 0)),
             ]
-            + held.in_specs,
+            + held.in_specs
+            + [pl.BlockSpec(memory_space=pl.ANY)] * n_before,
             out_specs=[
-                pl.BlockSpec((1, block, width), lambda i, _: (0, i, 0)),
-                pl.BlockSpec((1, 8, width), lambda i, _: (0, 0, 0)),
+                rows,
+                pl.BlockSpec((1, 8, width), lambda i, _: (slot * part_of[1] + part_of[0], 0, 0)),
             ],
             scratch_shapes=held.scratch,
         ),
         out_shape=[
-            jax.ShapeDtypeStruct((1,) + tokens.shape[1:], jnp.float32),
-            jax.ShapeDtypeStruct((1, 8, width), jnp.float32),
+            jax.ShapeDtypeStruct(tokens.shape, jnp.float32),
+            jax.ShapeDtypeStruct((slots * part_of[1], 8, width), jnp.float32),
         ],
+        input_output_aliases={5 + n_groups + n_held + i: i for i in range(n_before)},
         compiler_params=params(),
-        cost_estimate=cost(15),
         name="project_back",
-    )(held.starts, *groups, tokens, grad_middle, added, gain, *held.refs)
+    )(held.starts, *groups, tokens, grad_middle, added, gain, *held.refs, *(before or ()))
+
+
+def columns_of(refs):
+    if len(refs[0].shape) == 3:
+        return jnp.concatenate([ref[0] for ref in refs], axis=1)
+    return refs[0][...]
 
 
 def grad_blocks(order, left, right, received=None):
@@ -553,12 +550,11 @@
         right_specs = [pl.BlockSpec((rows, slab), lambda r, k, j, order: (0, j))]
         right = [right]
     n_right = len(right)
+    if depth <= 512:
+        return narrow_grad_blocks(order, left, right, right_specs, (count, depth, slab), received)
 
     def kernel(order_ref, a_ref, *rest):
-        if stacked:
-            right_block = jnp.concatenate([ref[0] for ref in rest[:n_right]], axis=1)
-        else:
-            right_block = rest[0][...]
+        right_block = columns_of(rest[:n_right])
         outs = rest[n_right:]
         total = dot(a_ref[...], right_block, 0, 0)
         if received is None:
@@ -591,9 +587,41 @@
         ),
         out_shape=[jax.ShapeDtypeStruct(shape, jnp.bfloat16)] * 2 if more else jax.ShapeDtypeStruct((2,) + shape, jnp.bfloat16),
         compiler_params=params(),
-        cost_estimate=cost(rows * left.shape[1] * slab * count // 10**9),
         name="grad_blocks",
     )(order, left, *right, *more)
+
+
+def narrow_grad_blocks(order, left, right, right_specs, shape, received):
+    count, depth, slab = shape
+    rows, n_right = left.shape[0], len(right)
+
+    def kernel(order_ref, a0_ref, a1_ref, *rest):
+        right_block = columns_of(rest[:n_right])
+        outs = rest[n_right:]
+        for r, a_ref in enumerate((a0_ref, a1_ref)):
+            total = dot(a_ref[...], right_block, 0, 0)
+            if received is None:
+                outs[0][r, 0] = total.astype(jnp.bfloat16)
+            else:
+                outs[1 + r][0] = (total + outs[0][r, 0].astype(jnp.float32)).astype(jnp.bfloat16)
+
+    by_step = lambda spec: pl.BlockSpec(spec.block_shape, lambda j, order: spec.index_map(0, 0, j, order))
+    both = pl.BlockSpec((2, 1, depth, slab), lambda j, order: (0, j, 0, 0))
+    one = pl.BlockSpec((1, depth, slab), lambda j, order: (j, 0, 0))
+    left_spec = lambda r: pl.BlockSpec((rows, depth), lambda j, order: (0, order[r]), pipeline_mode=pl.Buffered(1))
+    more = [] if received is None else [received]
+    return pl.pallas_call(
+        kernel,
+        grid_spec=pltpu.PrefetchScalarGridSpec(
+            num_scalar_prefetch=1,
+            grid=(count,),
+            in_specs=[left_spec(0), left_spec(1)] + [by_step(spec) for spec in right_specs] + [both] * len(more),
+            out_specs=[one, one] if more else both,
+        ),
+        out_shape=[jax.ShapeDtypeStruct(shape, jnp.bfloat16)] * 2 if more else jax.ShapeDtypeStruct((2,) + shape, jnp.bfloat16),
+        compiler_params=params(),
+        name="grad_blocks",
+    )(order, left, left, *right, *more)
 
 
 def after(value, *earlier):
@@ -770,7 +798,6 @@
         ),
         out_shape=jax.ShapeDtypeStruct((2 * rows, count * n_pieces * wide), jnp.float32),
         compiler_params=params(),
-        cost_estimate=cost(4),
         name="assemble",
     )(bit_of("dp", 0).astype(jnp.int32).reshape(1), *[v for piece in pieces for v in piece])
 
@@ -867,7 +894,7 @@
             return self.total
         if self.spread:
             return in_rows(after(self.whole, *earlier))
-        return assemble([(self.kept, self.received)])
+        return assemble([(after(self.kept, *earlier), self.received)])
 
 
 def in_order(mine, other, bit):
@@ -893,49 +920,44 @@
     get_proj = Gather(after(w_proj, *t).astype(jnp.bfloat16))
     get_up = Gather(after(w_up, *t).astype(jnp.bfloat16))
     t = (get_down.sent, get_proj.sent, get_up.sent)
-    t = slot(t, [small, get_qkv[0]], [get_qkv[0], get_down, get_qkv[1]])
-    t = slot(t, [get_qkv[0]])
+    t = slot(t, [small])
     small = small.whole.astype(jnp.float32)
     g = small[: gains.shape[0]]
     embed = small[gains.shape[0] :]
     onehot = (group_ids[:, None] == jnp.arange(table.shape[0])[None, :]).astype(jnp.float32)
     added = jnp.sum(onehot[:, :, None] * embed[None], axis=1)[:, None, :]
     live = (jnp.arange(slots) < counts[0]).astype(jnp.int32)
+    a1 = norm_in(after(tokens, *t), added, g[0:1])
+    t = slot((a1,), [get_qkv[0]], [get_qkv[0], get_qkv[1]])
+    t = slot(t, [get_qkv[0]])
 
     qkv = []
-    a1, group = project_in(after(tokens, *t), added, g[0:1], get_qkv[0].parts())
+    group = project_in(after(a1, *t), get_qkv[0].parts())
     qkv.append(group)
-    t = slot((group,), [get_down], [get_down, get_proj])
+    t = slot((group,), [get_qkv[1]], [get_qkv[1], get_down, get_up])
     attended = attn_fwd(after(group, *t), 0, half, 0, width)
-    t = slot((attended[0],), [get_qkv[1], get_proj], [get_qkv[1], get_proj, get_up])
+    t = slot((attended[0],), [get_qkv[1], get_down], [get_down, get_proj])
     attended = attn_fwd(after(group, *t), half, group_pairs - half, 0, width, attended)
-    t = slot((attended[0],), [get_qkv[1], get_proj])
-    _, group = project_in(after(tokens, *t), added, g[0:1], get_qkv[1].parts())
+    t = (attended[0],)
+    group = project_in(after(a1, *t), get_qkv[1].parts())
     qkv.append(group)
-    attended = attn_fwd(group, 0, half, group_pairs, width, attended)
-    t = slot((attended[0],), [get_up], [get_up])
-    attended = attn_fwd(after(group, *t), half, group_pairs - half, group_pairs, width, attended)
-    mixture, log_totals = attended
-    t = slot((mixture,), [get_up])
+    mixture, log_totals = attn_fwd(group, 0, group_pairs, group_pairs, width, attended)
+    t = slot((mixture,), [get_up, get_proj], [get_up, get_proj])
+    t = slot(t, [get_up, get_proj])
     p_qkv = [w.parts() for w in get_qkv]
     p_proj, p_up, p_down = get_proj.parts(), get_up.parts(), get_down.parts()
-    a3, f, slope, dm, z, h1, output, sums_out = up_and_down(
+    a3, f, du, dm, z, h1, output, sums_out = up_and_down(
         live, after(mixture, *t), tokens, cotangent, added, g, p_proj, p_up, p_down
     )
 
     down = GradSum(flat(f), flat(dm), spread=True)
-    t = down.part((dm,))
-    t = slot(t, [], [down])
-    t = slot(t, [down])
-    t = slot(down.part(t), [], [down])
-    du = back_to_hidden(after(dm, *t), slope, p_down)
     up = GradSum(flat(a3), flat(du), spread=True)
-    t = up.part((du,))
-    t = slot(t, [down], [down, up])
-    t = slot(t, [up])
-    t = slot(up.part(t), [], [up])
+    t = slot(down.part((dm,)), [], [down])
+    t = slot(up.part(t), [down], [up])
+    t = slot(down.part(t), [up], [down])
+    t = up.part(t)
     dz, do, dh1, sums_mid = back_to_mixture(live, after(du, *t), h1, z, cotangent, g, p_proj, p_up)
-    t = slot((dz,), [down], [down])
+    t = slot((dz,), [down], [down, up])
     proj = GradSum(flat(mixture), flat(dz))
     t = slot(proj.part(t), [], [proj])
     chunks = []
@@ -946,45 +968,40 @@
         return (chunks[-1],)
 
     t = attend(0, t)
-    t = slot(t, [up, down, proj], [up, down])
+    t = slot(t, [down, proj], [down])
     t = slot(proj.part(t), [], [proj])
     t = attend(1, t)
     t = slot(t, [up, down, proj], [up, down, proj])
     first = GradSum(flat(a1), [flat(d) for d in chunks])
     t = slot(first.part(t), [proj], [first, proj])
     t = attend(2, t)
-    t = slot(t, [up, proj, first], [up, proj])
+    t = slot(t, [up, down, first, proj], [up, down, proj])
     t = slot(first.part(t), [proj], [first, proj])
     t = attend(3, t)
     t = slot(t, [up, first, proj], [up, first, proj])
     last = GradSum(flat(a1), [flat(d) for d in chunks[2:]])
     t = slot(last.part(t), [proj], [last, proj])
-    t = slot(t, [last, first, proj], [first, proj])
-    t = slot(last.part(t), [first], [last, first])
-
-    backs = []
-    for i in range(slots):
-        backs.append(project_back(i, chunks, tokens, after(dh1, *t), added, g[0:1], p_qkv))
-        t = (backs[-1][0],)
-        if i == 0:
-            t = slot(t, [last, first, proj], [last, first])
-    grad_tokens, more = (jnp.concatenate(v, axis=0) for v in zip(*backs))
+    grad_down = down.result(*t)
+    t = slot((grad_down,), [last])
+    t = slot(last.part(t), [up, first, proj], [up, last, first, proj])
+    back = project_back(0, (0, 1), chunks, tokens, after(dh1, *t), added, g[0:1], p_qkv)
+    t = slot((back[0],), [last, first, proj], [last, first])
+    back = project_back(1, (0, 1), chunks, tokens, after(dh1, *t), added, g[0:1], p_qkv, back)
+    grad_tokens, more = back
     grad_embed = jnp.sum(onehot[:, :, None] * more[:, None, 1, :], axis=0)
     grad_gains = jnp.concatenate([more[:, 0:1], sums_mid[:, 0:2], sums_out[:, 0:1]], axis=1).sum(axis=0)
     little = SmallSum(jnp.concatenate([grad_gains, grad_embed], axis=0))
-    t = slot(t + (little.sent,) if paired() else t, [last, first], [last, first, little])
-    grad_down = down.result(*t)
-    t = slot((grad_down,), [last, first, little], [last, first, little])
-    grad_proj = proj.result()
+    t = slot((more, little.sent) if paired() else (more,), [last, first], [last, first, little])
+    grad_proj = proj.result(*t)
     t = slot((grad_proj,), [last, first, little], [last, first, little])
+    grad_up = up.result(*t)
+    t = (grad_up,)
+    waiting = [last, first, little]
     while paired() and last.state != "done":
-        moving = [e for e in (last, first) if e.state != "done"] + ([little] if little.bits else [])
-        ending = [e for e in (last, first) if e.state != "done"] + ([little] if little.received is not None else [])
-        t = slot(t, ending, [])
-        moving = [e for e in (last, first) if e.state != "done"] + ([little] if little.bits else [])
-        little.received = None
-        if moving:
-            t = slot(t, [], moving)
+        t = slot(t, waiting)
+        waiting = [e for e in (last, first) if e.state != "done"] + ([little] if little.bits else [])
+        if waiting:
+            t = slot(t, [], waiting)
     if paired():
         grad_qkv = assemble([(e.kept, e.received) for e in (first, last)])
     else:
@@ -996,7 +1013,7 @@
         grad_tokens,
         grad_qkv,
         grad_proj,
-        up.result(*t),
+        grad_up,
         grad_down,
         small_sum[: gains.shape[0]],
         small_sum[gains.shape[0] :],

time: 701 us -> 649 us (0.926)
  Pallas kernels: 485 us -> 453 us
  waiting for transfers between devices: 80.8 us -> 60 us
    pallas_call x10 -> x2, Pallas kernels: 130 us -> 31.8 us  [grad_blocks(): pl.pallas_call(kernel, grid_spec=pltpu.PrefetchScalarGridSpec(num_scalar_...]
    pallas_call x1 -> x9, Pallas kernels: 29.3 us -> 86.9 us  [the longest x8 79.6 us: narrow_grad_blocks(): pl.pallas_call(kernel, grid_spec=pltpu.PrefetchScalarGridSpec(num_scalar_...]
    ppermute x52, waiting for transfers between devices: 80.7 us -> 56.3 us  [swap(): return lax.ppermute(value, axis, [(i, i ^ 1 << bit) for i in range(size)])]
    pallas_call x1, Pallas kernels: 69.8 us -> 84.2 us  [up_and_down(): pl.pallas_call(kernel, grid_spec=pltpu.PrefetchScalarGridSpec(num_scalar_...]
    concatenate x1 -> x0, other arithmetic: 9.18 us -> none  [local(): grad_tokens, more = (jnp.concatenate(v, axis=0) for v in zip(*backs))]
    pallas_call x4 -> x3, Pallas kernels: 46 us -> 44.1 us  [attn_fwd(): pl.pallas_call(kernel, grid=(slots, count), in_specs=[pl.BlockSpec((3, 1,...]
  transfers between devices with their start and end apart: 55 -> 55, of which waited for: 19 -> 16; matrix products, arithmetic and copies ran while one was open for 6% -> 4% of each run, Pallas kernels for 54% -> 54%
where the time goes in v2:
time: 649 us; the launch traced here: 642 us
  Pallas kernels  453 us (70%)
  waiting for transfers between devices  60 us (9%)
  starting transfers between devices  54.7 us (8%)
  other arithmetic  43.2 us (7%)
  between operations  15.7 us (2%)
  local copies, waits for them, and re-layouts  15.4 us (2%)
    pallas_call x1, Pallas kernels, up_and_down(): pl.pallas_call(kernel, grid_spec=pltpu.PrefetchScalarGridSpec(num_scalar_...  84.2 us
    pallas_call x8, Pallas kernels, narrow_grad_blocks(): pl.pallas_call(kernel, grid_spec=pltpu.PrefetchScalarGridSpec(num_scalar_...  79.6 us
    pallas_call x4, Pallas kernels, attn_bwd(): pl.pallas_call(attn_bwd_kernel, grid=(slots, count), in_specs=[triple, si...  78.2 us
    ppermute x52, waiting for transfers between devices, swap(): return lax.ppermute(value, axis, [(i, i ^ 1 << bit) for i in range(size)])  56.3 us
    ppermute x52, starting transfers between devices, swap(): return lax.ppermute(value, axis, [(i, i ^ 1 << bit) for i in range(size)])  53.8 us
    pallas_call x3, Pallas kernels, attn_fwd(): pl.pallas_call(kernel, grid=(slots, count), in_specs=[pl.BlockSpec((3, 1,...  44.1 us
    pallas_call x1, Pallas kernels, back_to_mixture(): pl.pallas_call(kernel, grid_spec=pltpu.PrefetchScalarGridSpec(num_scalar_...  44 us
    pallas_call x2, Pallas kernels, project_back(): pl.pallas_call(kernel, grid_spec=pltpu.PrefetchScalarGridSpec(num_scalar_...  36.3 us
  transfers between devices with their start and end apart: 55, of which 16 were waited for; matrix products, arithmetic and copies ran while one was open for 4% of the time, Pallas kernels for 54%

profile of v2, /device:TPU:0, one launch (start us, length us, event | category | flops | bytes accessed | tf_op | source)
XLA Modules:
  0.0 641.8 jit_solution(4430040519005658324)
XLA Ops:
  43.5 12.8 %project_in.2.x_ref = bf16[3,2,1088,512]{3,2,1,0:T(8,128)(2,1)} custom-call(s32[3]{0:T(128)} %pad_add_fusion.starts_ref, bf16[2,1088,1024]{2,1,0:T(8,128)(2,1)} %norm_in.1.a_ref, bf16[512,3072]{1,0:T(8,128)(2,1)} %copy-done, bf16[3,256,512]{2,1,0:T(8,128)(2,1)} %copy-done.4, bf16[3,256,512]{2,1,0:T(8,128)(2,1)} %copy-done.5), custom_call_target="tpu_custom_call" | custom-call | tf_op jit(solution)/shard_map/project_in/pallas_call | solution.py:139
  61.9 11.4 %attn_fwd.3 = (bf16[2,1088,1024]{2,1,0:T(8,128)(2,1)}, f32[2,8,2,1088]{3,2,1,0:T(2,128)}) custom-call(bf16[3,2,1088,512]{3,2,1,0:T(8,128)(2,1)} %project_in.2.x_ref), custom_call_target="tpu_custom_call" | custom-call | tf_op jit(solution)/shard_map/attn_fwd/pallas_call | solution.py:210
  76.7 11.4 %attn_fwd.4 = (bf16[2,1088,1024]{2,1,0:T(8,128)(2,1)}, f32[2,8,2,1088]{3,2,1,0:T(2,128)}) custom-call(bf16[3,2,1088,512]{3,2,1,0:T(8,128)(2,1)} %project_in.2.x_ref, bf16[2,1088,1024]{2,1,0:T(8,128)(2,1)} %get-tuple-element.182.rest_0_, f32[2,8,2,1088]{3,2,1,0:T(2,128)} %get-tuple-element.187.rest_1_), custom_call_target="tpu_custom_call", output_to_operand_aliasing={{0}: (1, {}), {1}: (2, {})} | custom-call | tf_op jit(solution)/shard_map/attn_fwd/pallas_call | solution.py:210
  88.1 12.8 %project_in.3.x_ref = bf16[3,2,1088,512]{3,2,1,0:T(8,128)(2,1)} custom-call(s32[3]{0:T(128)} %pad_add_fusion.starts_ref, bf16[2,1088,1024]{2,1,0:T(8,128)(2,1)} %norm_in.1.a_ref, bf16[512,3072]{1,0:T(8,128)(2,1)} %copy-done, bf16[3,256,512]{2,1,0:T(8,128)(2,1)} %copy-done.6, bf16[3,256,512]{2,1,0:T(8,128)(2,1)} %copy-done.7), custom_call_target="tpu_custom_call" | custom-call | tf_op jit(solution)/shard_map/project_in/pallas_call | solution.py:139
  100.9 21.3 %attn_fwd.5 = (bf16[2,1088,1024]{2,1,0:T(8,128)(2,1)}, f32[2,8,2,1088]{3,2,1,0:T(2,128)}) custom-call(bf16[3,2,1088,512]{3,2,1,0:T(8,128)(2,1)} %project_in.3.x_ref, bf16[2,1088,1024]{2,1,0:T(8,128)(2,1)} %get-tuple-element.188.rest_0_, f32[2,8,2,1088]{3,2,1,0:T(2,128)} %get-tuple-element.191.rest_1_), custom_call_target="tpu_custom_call", output_to_operand_aliasing={{0}: (1, {}), {1}: (2, {})} | custom-call | tf_op jit(solution)/shard_map/attn_fwd/pallas_call | solution.py:210
  122.2 11.7 %collective-permute-done.7.rest_1_.rest_4_ = bf16[256,1024]{1,0:T(8,128)(2,1)S(1)} collective-permute-done((bf16[256,1024]{1,0:T(8,128)(2,1)}, bf16[256,1024]{1,0:T(8,128)(2,1)S(1)}, u32[]{:S(2)}, u32[]{:S(2)}) %collective-permute-start.7) | collective-permute-done | bytes 524320 | tf_op jit(solution)/shard_map/ppermute | solution.py:633
  139.3 84.2 %up_and_down.1 = (bf16[2,1088,1024]{2,1,0:T(8,128)(2,1)}, bf16[2,1088,4096]{2,1,0:T(8,128)(2,1)}, bf16[2,1088,4096]{2,1,0:T(8,128)(2,1)}, bf16[2,1088,1024]{2,1,...) custom-call(s32[8]{0:T(128)} %stack.49.starts_ref, ...), custom_call_target="tpu_custom_call" | custom-call | tf_op jit(solution)/shard_map/up_and_down/pallas_call | solution.py:383
  223.4 15.3 %grad_blocks.10 = bf16[2,1,1024,1024]{3,2,1,0:T(8,128)(2,1)} custom-call(s32[2]{0:T(128)} %get-tuple-element.357.order_ref, bf16[2176,4096]{1,0:T(8,128)(2,1)} %bitcast.205, bf16[2176,1024]{1,0:T(8,128)(2,1)} %bitcast.214), custom_call_target="tpu_custom_call" | custom-call | tf_op jit(solution)/shard_map/grad_blocks/pallas_call | solution.py:578
  239.1 15.4 %grad_blocks.11 = bf16[2,4,256,1024]{3,2,1,0:T(8,128)(2,1)} custom-call(s32[2]{0:T(128)} %get-tuple-element.357.order_ref, bf16[2176,1024]{1,0:T(8,128)(2,1)} %bitcast.207, bf16[2176,1024]{1,0:T(8,128)(2,1)} %bitcast.208, bf16[2176,4096]{1,0:T(8,128)(2,1)} %bitcast.195), custom_call_target="tpu_custom_call" | custom-call | tf_op jit(solution)/shard_map/grad_blocks/pallas_call | solution.py:613
  254.7 16.5 %grad_blocks.12 = (bf16[1,1024,1024]{2,1,0:T(8,128)(2,1)}, bf16[1,1024,1024]{2,1,0:T(8,128)(2,1)}) custom-call(s32[2]{0:T(128)} %get-tuple-element.356.order_ref, bf16[2176,4096]{1,0:T(8,128)(2,1)} %bitcast.206, bf16[2176,1024]{1,0:T(8,128)(2,1)} %bitcast.215, bf16[2,1,1024,1024]{3,2,1,0:T(8,128)(2,1)} %collective-permute-done.10.rest_1_), custom_call_target="tpu_custom_call" | custom-call | tf_op jit(solution)/shard_map/grad_blocks/pallas_call | solution.py:578
  272.1 15.7 %grad_blocks.13 = (bf16[4,256,1024]{2,1,0:T(8,128)(2,1)}, bf16[4,256,1024]{2,1,0:T(8,128)(2,1)}) custom-call(s32[2]{0:T(128)} %get-tuple-element.356.order_ref, bf16[2176,1024]{1,0:T(8,128)(2,1)} %bitcast.209, bf16[2176,1024]{1,0:T(8,128)(2,1)} %bitcast.210, bf16[2176,4096]{1,0:T(8,128)(2,1)} %bitcast.196, ...), custom_call_target="tpu_custom_call" | custom-call | tf_op jit(solution)/shard_map/grad_blocks/pallas_call | solution.py:613
  287.8 44.0 %back_to_mixture.1 = (bf16[2,1088,1024]{2,1,0:T(8,128)(2,1)}, bf16[2,1088,1024]{2,1,0:T(8,128)(2,1)}, f32[2,1088,1024]{2,1,0:T(8,128)}, f32[2,8,1024]{2,1,0:T(8,128)}) custom-call(s32[6]{0:T(128)} %stack.59.starts_ref, s32[2]{0:T(128)} %compare_convert_fusion.1.live_ref, bf16[2,1088,4096]{2,1,0:T(8,128)(2,1)} %get-tuple-element.212.du_ref, ...), custom_call_target="tpu_custom_call" | custom-call | tf_op jit(solution)/shard_map/back_to_mixture/pallas_call | solution.py:437
  345.8 19.5 %attn_bwd.4.refs_in_0_ = bf16[3,2,1088,256]{3,2,1,0:T(8,128)(2,1)} custom-call(bf16[3,2,1088,512]{3,2,1,0:T(8,128)(2,1)} %project_in.2.x_ref, bf16[2,1088,1024]{2,1,0:T(8,128)(2,1)} %get-tuple-element.192.o_ref, bf16[2,1088,1024]{2,1,0:T(8,128)(2,1)} %get-tuple-element.254.do_ref, f32[2,8,2,1088]{3,2,1,0:T(2,128)} %get-tuple-element.223.l_ref), custom_call_target="tpu_custom_call" | custom-call | tf_op jit(solution)/shard_map/attn_bwd/pallas_call | solution.py:279
  380.9 19.8 %attn_bwd.5.refs_in_1_ = bf16[3,2,1088,256]{3,2,1,0:T(8,128)(2,1)} custom-call(bf16[3,2,1088,512]{3,2,1,0:T(8,128)(2,1)} %project_in.2.x_ref, bf16[2,1088,1024]{2,1,0:T(8,128)(2,1)} %get-tuple-element.192.o_ref, bf16[2,1088,1024]{2,1,0:T(8,128)(2,1)} %get-tuple-element.254.do_ref, f32[2,8,2,1088]{3,2,1,0:T(2,128)} %get-tuple-element.223.l_ref), custom_call_target="tpu_custom_call" | custom-call | tf_op jit(solution)/shard_map/attn_bwd/pallas_call | solution.py:279
  408.1 8.4 %grad_blocks.16 = bf16[2,3,256,512]{3,2,1,0:T(8,128)(2,1)} custom-call(s32[2]{0:T(128)} %get-tuple-element.357.order_ref, bf16[2176,1024]{1,0:T(8,128)(2,1)} %bitcast.187, bf16[2176,1024]{1,0:T(8,128)(2,1)} %bitcast.188, bf16[3,2176,256]{2,1,0:T(8,128)(2,1)} %bitcast.197, bf16[3,2176,256]{2,1,0:T(8,128)(2,1)} %bitcast.199), custom_call_target="tpu_custom_call" | custom-call | tf_op jit(solution)/shard_map/grad_blocks/pallas_call | solution.py:613
  420.7 19.5 %attn_bwd.6.refs_in_2_ = bf16[3,2,1088,256]{3,2,1,0:T(8,128)(2,1)} custom-call(bf16[3,2,1088,512]{3,2,1,0:T(8,128)(2,1)} %project_in.3.x_ref, bf16[2,1088,1024]{2,1,0:T(8,128)(2,1)} %get-tuple-element.192.o_ref, bf16[2,1088,1024]{2,1,0:T(8,128)(2,1)} %get-tuple-element.254.do_ref, f32[2,8,2,1088]{3,2,1,0:T(2,128)} %get-tuple-element.223.l_ref), custom_call_target="tpu_custom_call" | custom-call | tf_op jit(solution)/shard_map/attn_bwd/pallas_call | solution.py:279
  451.1 8.6 %grad_blocks.17 = (bf16[3,256,512]{2,1,0:T(8,128)(2,1)}, bf16[3,256,512]{2,1,0:T(8,128)(2,1)}) custom-call(s32[2]{0:T(128)} %get-tuple-element.356.order_ref, bf16[2176,1024]{1,0:T(8,128)(2,1)} %bitcast.189, bf16[2176,1024]{1,0:T(8,128)(2,1)} %bitcast.190, bf16[3,2176,256]{2,1,0:T(8,128)(2,1)} %bitcast.198, bf16[3,2176,256]{2,1,0:T(8,128)(2,1)} %bitcast.200, ...), custom_call_target="tpu_custom_call" | custom-call | tf_op jit(solution)/shard_map/grad_blocks/pallas_call | solution.py:613
  462.9 19.5 %attn_bwd.7.refs_in_3_ = bf16[3,2,1088,256]{3,2,1,0:T(8,128)(2,1)} custom-call(bf16[3,2,1088,512]{3,2,1,0:T(8,128)(2,1)} %project_in.3.x_ref, bf16[2,1088,1024]{2,1,0:T(8,128)(2,1)} %get-tuple-element.192.o_ref, bf16[2,1088,1024]{2,1,0:T(8,128)(2,1)} %get-tuple-element.254.do_ref, f32[2,8,2,1088]{3,2,1,0:T(2,128)} %get-tuple-element.223.l_ref), custom_call_target="tpu_custom_call" | custom-call | tf_op jit(solution)/shard_map/attn_bwd/pallas_call | solution.py:279
  485.9 8.4 %grad_blocks.18 = bf16[2,3,256,512]{3,2,1,0:T(8,128)(2,1)} custom-call(s32[2]{0:T(128)} %get-tuple-element.357.order_ref, bf16[2176,1024]{1,0:T(8,128)(2,1)} %bitcast.191, bf16[2176,1024]{1,0:T(8,128)(2,1)} %bitcast.192, bf16[3,2176,256]{2,1,0:T(8,128)(2,1)} %bitcast.201, bf16[3,2176,256]{2,1,0:T(8,128)(2,1)} %bitcast.203), custom_call_target="tpu_custom_call" | custom-call | tf_op jit(solution)/shard_map/grad_blocks/pallas_call | solution.py:613
  509.9 8.6 %grad_blocks.19 = (bf16[3,256,512]{2,1,0:T(8,128)(2,1)}, bf16[3,256,512]{2,1,0:T(8,128)(2,1)}) custom-call(s32[2]{0:T(128)} %get-tuple-element.356.order_ref, bf16[2176,1024]{1,0:T(8,128)(2,1)} %bitcast.193, bf16[2176,1024]{1,0:T(8,128)(2,1)} %bitcast.194, bf16[3,2176,256]{2,1,0:T(8,128)(2,1)} %bitcast.202, bf16[3,2176,256]{2,1,0:T(8,128)(2,1)} %bitcast.204, ...), custom_call_target="tpu_custom_call" | custom-call | tf_op jit(solution)/shard_map/grad_blocks/pallas_call | solution.py:613
  526.8 18.3 %project_back.2 = (f32[2,1088,1024]{2,1,0:T(8,128)}, f32[2,8,1024]{2,1,0:T(8,128)}) custom-call(s32[6]{0:T(128)} %stack.59.starts_ref, bf16[3,2,1088,256]{3,2,1,0:T(8,128)(2,1)} %attn_bwd.4.refs_in_0_, bf16[3,2,1088,256]{3,2,1,0:T(8,128)(2,1)} %attn_bwd.5.refs_in_1_, bf16[3,2,1088,256]{3,2,1,0:T(8,128)(2,1)} %attn_bwd.6.refs_in_2_, ...), custom_call_target="tpu_custom_call" | custom-call | tf_op jit(solution)/shard_map/project_back/pallas_call | solution.py:503
  548.7 17.9 %project_back.3 = (f32[2,1088,1024]{2,1,0:T(8,128)}, f32[2,8,1024]{2,1,0:T(8,128)}) custom-call(s32[6]{0:T(128)} %stack.59.starts_ref, bf16[3,2,1088,256]{3,2,1,0:T(8,128)(2,1)} %attn_bwd.4.refs_in_0_, bf16[3,2,1088,256]{3,2,1,0:T(8,128)(2,1)} %attn_bwd.5.refs_in_1_, ...), custom_call_target="tpu_custom_call", output_to_operand_aliasing={{0}: (15, {}), {1}: (16, {})} | custom-call | tf_op jit(solution)/shard_map/project_back/pallas_call | solution.py:503
  585.4 7.4 %in_rows.3 = f32[512,4096]{1,0:T(8,128)} custom-call(bf16[16,4,32,1024]{3,2,1,0:T(8,128)(2,1)} %bitcast.216), custom_call_target="tpu_custom_call" | custom-call | tf_op jit(solution)/shard_map/in_rows/pallas_call | solution.py:817
  597.3 7.9 %collective-permute-done.45 = f32[12,512]{1,0:T(8,128)S(1)} collective-permute-done((f32[12,512]{1,0:T(8,128)S(1)}, f32[12,512]{1,0:T(8,128)S(1)}, u32[]{:S(2)}, u32[]{:S(2)}) %collective-permute-start.45) | collective-permute-done | bytes 24608 | tf_op jit(solution)/shard_map/ppermute | solution.py:633
  (268 shorter events, 190.0 us)
Async XLA Ops:
  7.2 131.8 %all-gather.6.cloned.1.call-start = ((), (), s32[]{:S(2)}) async-start(), calls=%async_computation | async-start | bytes 4456448 | tf_op jit(solution)/shard_map/all_gather | solution.py:721
  15.6 24.2 %collective-permute-start.1 = (bf16[3,256,512]{2,1,0:T(8,128)(2,1)}, bf16[3,256,512]{2,1,0:T(8,128)(2,1)S(1)}, u32[]{:S(2)}, u32[]{:S(2)}) collective-permute-start(bf16[3,256,512]{2,1,0:T(8,128)(2,1)} %get-tuple-element.168), channel_id=1, source_target_pairs={{0,1},{1,0},{2,3},{3,2},{4,5},{5,4},{6,7},{7,6},{8,9},{9,8},{10,11... | collective-permute-start | bytes 2359304 | tf_op jit(solution)/shard_map/ppermute | solution.py:633
  39.9 20.2 %collective-permute-start.3 = (bf16[3,256,512]{2,1,0:T(8,128)(2,1)S(1)}, bf16[3,256,512]{2,1,0:T(8,128)(2,1)S(1)}, u32[]{:S(2)}, u32[]{:S(2)}) collective-permute-start(bf16[3,256,512]{2,1,0:T(8,128)(2,1)S(1)} %copy-done.24), channel_id=1, source_target_pairs={{0,1},{1,0},{2,3},{3,2},{4,5},{5,4},{6,7},{7,6},{8,9},{9,8},{10,11... | collective-permute-start | bytes 2359304 | tf_op jit(solution)/shard_map/ppermute | solution.py:633
  74.0 429.5 %all-gather.8.cloned.1.call-start = ((), (), s32[]{:S(2)}) async-start(), calls=%async_computation.1 | async-start | bytes 4456448 | tf_op jit(solution)/shard_map/all_gather | solution.py:864
  74.6 59.3 %collective-permute-start.6 = (bf16[256,4096]{1,0:T(8,128)(2,1)}, bf16[256,4096]{1,0:T(8,128)(2,1)S(1)}, u32[]{:S(2)}, u32[]{:S(2)}) collective-permute-start(bf16[256,4096]{1,0:T(8,128)(2,1)} %constant_dynamic-slice_fusion.2), channel_id=1, source_target_pairs={{0,1},{1,0},{2,3},{3,2},{4,5},{5,4},{6,7},{7,6},{8,9},{9,8},{10,11... | collective-permute-start | bytes 6291464 | tf_op jit(solution)/shard_map/ppermute | solution.py:633
  74.9 58.9 %collective-permute-start.7 = (bf16[256,1024]{1,0:T(8,128)(2,1)}, bf16[256,1024]{1,0:T(8,128)(2,1)S(1)}, u32[]{:S(2)}, u32[]{:S(2)}) collective-permute-start(bf16[256,1024]{1,0:T(8,128)(2,1)} %constant_dynamic-slice_fusion.3), channel_id=1, source_target_pairs={{0,1},{1,0},{2,3},{3,2},{4,5},{5,4},{6,7},{7,6},{8,9},{9,8},{10,11... | collective-permute-start | bytes 1572872 | tf_op jit(solution)/shard_map/ppermute | solution.py:633
  271.1 60.7 %collective-permute-start.12 = (bf16[1,1024,1024]{2,1,0:T(8,128)(2,1)}, bf16[1,1024,1024]{2,1,0:T(8,128)(2,1)}, u32[]{:S(2)}, u32[]{:S(2)}) collective-permute-start(bf16[1,1024,1024]{2,1,0:T(8,128)(2,1)} %get-tuple-element.208), channel_id=1, source_target_pairs={{0,1},{1,0},{2,3},{3,2},{4,5},{5,4},{6,7},{7,6},{8,9},{9,8},{10,11... | collective-permute-start | bytes 6291464 | tf_op jit(solution)/shard_map/ppermute | solution.py:633
  335.3 65.4 %collective-permute-start.15 = (bf16[4,256,1024]{2,1,0:T(8,128)(2,1)}, bf16[4,256,1024]{2,1,0:T(8,128)(2,1)}, u32[]{:S(2)}, u32[]{:S(2)}) collective-permute-start(bf16[4,256,1024]{2,1,0:T(8,128)(2,1)} %get-tuple-element.220), channel_id=1, source_target_pairs={{0,1},{1,0},{2,3},{3,2},{4,5},{5,4},{6,7},{7,6},{8,9},{9,8},{10,11... | collective-permute-start | bytes 6291464 | tf_op jit(solution)/shard_map/ppermute | solution.py:633
  344.3 21.0 %collective-permute-start.14 = (bf16[2,1,256,1024]{3,2,1,0:T(8,128)(2,1)}, bf16[2,1,256,1024]{3,2,1,0:T(8,128)(2,1)S(1)}, u32[]{:S(2)}, u32[]{:S(2)}) collective-permute-start(bf16[2,1,256,1024]{3,2,1,0:T(8,128)(2,1)} %grad_blocks.14), channel_id=1, source_target_pairs={{0,2},{2,0},{4,6},{6,4},{8,10},{10,8},{12,14},{14,12},{16,18},{18,... | collective-permute-start | bytes 3145736 | tf_op jit(solution)/shard_map/ppermute | solution.py:633
  344.3 25.8 %collective-permute-start.13 = (bf16[1,512,1024]{2,1,0:T(8,128)(2,1)}, bf16[1,512,1024]{2,1,0:T(8,128)(2,1)S(1)}, u32[]{:S(2)}, u32[]{:S(2)}) collective-permute-start(bf16[1,512,1024]{2,1,0:T(8,128)(2,1)} %get-tuple-element.219), channel_id=1, source_target_pairs={{0,4},{2,6},{4,0},{6,2},{8,12},{10,14},{12,8},{14,10},{16,20},{18,... | collective-permute-start | bytes 3145736 | tf_op jit(solution)/shard_map/ppermute | solution.py:633
  378.7 21.9 %collective-permute-start.17 = (bf16[1,256,1024]{2,1,0:T(8,128)(2,1)}, bf16[1,256,1024]{2,1,0:T(8,128)(2,1)}, u32[]{:S(2)}, u32[]{:S(2)}) collective-permute-start(bf16[1,256,1024]{2,1,0:T(8,128)(2,1)} %get-tuple-element.227), channel_id=1, source_target_pairs={{0,1},{1,0},{2,3},{3,2},{4,5},{5,4},{6,7},{7,6},{8,9},{9,8},{10,11... | collective-permute-start | bytes 1572872 | tf_op jit(solution)/shard_map/ppermute | solution.py:633
  379.1 21.6 %collective-permute-start.16 = (bf16[1,256,1024]{2,1,0:T(8,128)(2,1)}, bf16[1,256,1024]{2,1,0:T(8,128)(2,1)S(1)}, u32[]{:S(2)}, u32[]{:S(2)}) collective-permute-start(bf16[1,256,1024]{2,1,0:T(8,128)(2,1)} %get-tuple-element.337), channel_id=1, source_target_pairs={{0,8},{2,10},{4,12},{6,14},{8,0},{10,2},{12,4},{14,6},{16,24},{18,... | collective-permute-start | bytes 1572872 | tf_op jit(solution)/shard_map/ppermute | solution.py:633
  417.2 25.9 %collective-permute-start.21 = (bf16[2,3,256,512]{3,2,1,0:T(8,128)(2,1)}, bf16[2,3,256,512]{3,2,1,0:T(8,128)(2,1)S(1)}, u32[]{:S(2)}, u32[]{:S(2)}) collective-permute-start(bf16[2,3,256,512]{3,2,1,0:T(8,128)(2,1)} %grad_blocks.16), channel_id=1, source_target_pairs={{0,2},{2,0},{4,6},{6,4},{8,10},{10,8},{12,14},{14,12},{16,18},{18,... | collective-permute-start | bytes 4718600 | tf_op jit(solution)/shard_map/ppermute | solution.py:633
  417.2 25.9 %collective-permute-start.19 = (bf16[4,128,1024]{2,1,0:T(8,128)(2,1)}, bf16[4,128,1024]{2,1,0:T(8,128)(2,1)}, u32[]{:S(2)}, u32[]{:S(2)}) collective-permute-start(bf16[4,128,1024]{2,1,0:T(8,128)(2,1)} %get-tuple-element.234), channel_id=1, source_target_pairs={{0,4},{2,6},{4,0},{6,2},{8,12},{10,14},{12,8},{14,10},{16,20},{18,... | collective-permute-start | bytes 3145736 | tf_op jit(solution)/shard_map/ppermute | solution.py:633
  417.7 22.6 %collective-permute-start.20 = (bf16[1,128,1024]{2,1,0:T(8,128)(2,1)S(1)}, bf16[1,128,1024]{2,1,0:T(8,128)(2,1)}, u32[]{:S(2)}, u32[]{:S(2)}) collective-permute-start(bf16[1,128,1024]{2,1,0:T(8,128)(2,1)S(1)} %fusion.8), channel_id=1, source_target_pairs={{0,16},{2,18},{4,20},{6,22},{8,24},{10,26},{12,28},{14,30},{16,0},... | collective-permute-start | bytes 786440 | tf_op jit(solution)/shard_map/ppermute | solution.py:633
  448.2 137.2 %all-gather.10.cloned.1.call-start = ((), (), s32[]{:S(2)}) async-start(), calls=%async_computation.2 | async-start | bytes 4456448 | tf_op jit(solution)/shard_map/all_gather | solution.py:864
  460.6 21.8 %collective-permute-start.25 = (bf16[3,256,512]{2,1,0:T(8,128)(2,1)}, bf16[3,256,512]{2,1,0:T(8,128)(2,1)S(1)}, u32[]{:S(2)}, u32[]{:S(2)}) collective-permute-start(bf16[3,256,512]{2,1,0:T(8,128)(2,1)} %get-tuple-element.252), channel_id=1, source_target_pairs={{0,1},{1,0},{2,3},{3,2},{4,5},{5,4},{6,7},{7,6},{8,9},{9,8},{10,11... | collective-permute-start | bytes 2359304 | tf_op jit(solution)/shard_map/ppermute | solution.py:633
  462.2 20.2 %collective-permute-start.24 = (bf16[4,64,1024]{2,1,0:T(8,128)(2,1)}, bf16[4,64,1024]{2,1,0:T(8,128)(2,1)S(1)}, u32[]{:S(2)}, u32[]{:S(2)}) collective-permute-start(bf16[4,64,1024]{2,1,0:T(8,128)(2,1)} %get-tuple-element.245), channel_id=1, source_target_pairs={{0,8},{2,10},{4,12},{6,14},{8,0},{10,2},{12,4},{14,6},{16,24},{18,... | collective-permute-start | bytes 1572872 | tf_op jit(solution)/shard_map/ppermute | solution.py:633
  496.0 22.5 %collective-permute-start.30 = (bf16[3,128,512]{2,1,0:T(8,128)(2,1)}, bf16[3,128,512]{2,1,0:T(8,128)(2,1)S(1)}, u32[]{:S(2)}, u32[]{:S(2)}) collective-permute-start(bf16[3,128,512]{2,1,0:T(8,128)(2,1)} %get-tuple-element.261), channel_id=1, source_target_pairs={{0,4},{2,6},{4,0},{6,2},{8,12},{10,14},{12,8},{14,10},{16,20},{18,... | collective-permute-start | bytes 1179656 | tf_op jit(solution)/shard_map/ppermute | solution.py:633
  497.4 21.1 %collective-permute-start.29 = (bf16[4,32,1024]{2,1,0:T(8,128)(2,1)}, bf16[4,32,1024]{2,1,0:T(8,128)(2,1)}, u32[]{:S(2)}, u32[]{:S(2)}) collective-permute-start(bf16[4,32,1024]{2,1,0:T(8,128)(2,1)} %fusion.11), channel_id=1, source_target_pairs={{0,16},{2,18},{4,20},{6,22},{8,24},{10,26},{12,28},{14,30},{16,0},... | collective-permute-start | bytes 786440 | tf_op jit(solution)/shard_map/ppermute | solution.py:633
  498.3 20.1 %collective-permute-start.31 = (bf16[1,128,1024]{2,1,0:T(8,128)(2,1)}, bf16[1,128,1024]{2,1,0:T(8,128)(2,1)}, u32[]{:S(2)}, u32[]{:S(2)}) collective-permute-start(bf16[1,128,1024]{2,1,0:T(8,128)(2,1)} %maximum_select_fusion.5), channel_id=1, source_target_pairs={{0,4},{2,6},{4,0},{6,2},{8,12},{10,14},{12,8},{14,10},{16,20},{18,... | collective-permute-start | bytes 786440 | tf_op jit(solution)/shard_map/ppermute | solution.py:633
  521.7 23.5 %collective-permute-start.32 = (bf16[3,256,512]{2,1,0:T(8,128)(2,1)}, bf16[3,256,512]{2,1,0:T(8,128)(2,1)S(1)}, u32[]{:S(2)}, u32[]{:S(2)}) collective-permute-start(bf16[3,256,512]{2,1,0:T(8,128)(2,1)} %get-tuple-element.274), channel_id=1, source_target_pairs={{0,1},{1,0},{2,3},{3,2},{4,5},{5,4},{6,7},{7,6},{8,9},{9,8},{10,11... | collective-permute-start | bytes 2359304 | tf_op jit(solution)/shard_map/ppermute | solution.py:633
  545.5 22.4 %collective-permute-start.35 = (bf16[3,128,512]{2,1,0:T(8,128)(2,1)S(1)}, bf16[3,128,512]{2,1,0:T(8,128)(2,1)S(1)}, u32[]{:S(2)}, u32[]{:S(2)}) collective-permute-start(bf16[3,128,512]{2,1,0:T(8,128)(2,1)S(1)} %get-tuple-element.282), channel_id=1, source_target_pairs={{0,4},{2,6},{4,0},{6,2},{8,12},{10,14},{12,8},{14,10},{16,20},{18,... | collective-permute-start | bytes 1179656 | tf_op jit(solution)/shard_map/ppermute | solution.py:633
  547.6 20.3 %collective-permute-start.36 = (bf16[3,32,512]{2,1,0:T(8,128)(2,1)S(1)}, bf16[3,32,512]{2,1,0:T(8,128)(2,1)S(1)}, u32[]{:S(2)}, u32[]{:S(2)}) collective-permute-start(bf16[3,32,512]{2,1,0:T(8,128)(2,1)S(1)} %fusion.20), channel_id=1, source_target_pairs={{0,16},{2,18},{4,20},{6,22},{8,24},{10,26},{12,28},{14,30},{16,0},... | collective-permute-start | bytes 294920 | tf_op jit(solution)/shard_map/ppermute | solution.py:633
  (70 other events, 738.0 us)
Sparse Core Ops, SparseCore 0:
  74.1 50.8 all-gather.5
  448.3 55.1 all-gather.7
  521.8 61.8 all-gather.9

commit v3 on v2

--- a/solution.py
+++ b/solution.py
@@ -177,21 +177,23 @@
         if far is not None:
             top = jnp.maximum(top, jnp.max(far, axis=1, keepdims=True))
         near = jnp.exp(near - top)
-        total = jnp.sum(near, axis=1, keepdims=True)
         if far is not None:
-            far = jnp.exp(far - top)
-            total = total + jnp.sum(far, axis=1, keepdims=True)
-            far = far.astype(jnp.bfloat16)
-        return near.astype(jnp.bfloat16), far, top, total
+            far = jnp.exp(far - top).astype(jnp.bfloat16)
+        return near.astype(jnp.bfloat16), far, top
+
+    def with_ones(a, b):
+        v = x_ref[2, 0, a:b, :]
+        return jnp.concatenate([v, jnp.ones_like(v)], axis=1)
 
     def mix(job, parts):
         lo, hi, h = job
-        near, far, top, total = parts
-        o = dot(near, x_ref[2, 0, lo:hi, :], 1, 0)
+        near, far, top = parts
+        o = dot(near, with_ones(lo, hi), 1, 0)
         if far is not None:
-            o = o + dot(far, x_ref[2, 0, 0:lo, :], 1, 0)
+            o = o + dot(far, with_ones(0, lo), 1, 0)
+        o, total = o[:, :LANES], o[:, LANES:]
         outs[h] = o / total
-        log_total = jnp.broadcast_to(top + jnp.log(total), (hi - lo, LANES))
+        log_total = top + jnp.log(total)
         l_ref[0, 0, h : h + 1, lo:hi] = jnp.transpose(log_total)[0:1, :]
         if h == 1:
             o_ref[0, lo:hi, :] = jnp.where(first, outs[0], outs[1]).astype(jnp.bfloat16)
@@ -516,13 +518,13 @@
             + [pl.BlockSpec(memory_space=pl.ANY)] * n_before,
             out_specs=[
                 rows,
-                pl.BlockSpec((1, 8, width), lambda i, _: (slot * part_of[1] + part_of[0], 0, 0)),
+                pl.BlockSpec((1, 8, width), lambda i, _: (slot * 2 + part_of[0], 0, 0)),
             ],
             scratch_shapes=held.scratch,
         ),
         out_shape=[
             jax.ShapeDtypeStruct(tokens.shape, jnp.float32),
-            jax.ShapeDtypeStruct((slots * part_of[1], 8, width), jnp.float32),
+            jax.ShapeDtypeStruct((slots * 2, 8, width), jnp.float32),
         ],
         input_output_aliases={5 + n_groups + n_held + i: i for i in range(n_before)},
         compiler_params=params(),
@@ -928,17 +930,15 @@
     added = jnp.sum(onehot[:, :, None] * embed[None], axis=1)[:, None, :]
     live = (jnp.arange(slots) < counts[0]).astype(jnp.int32)
     a1 = norm_in(after(tokens, *t), added, g[0:1])
-    t = slot((a1,), [get_qkv[0]], [get_qkv[0], get_qkv[1]])
+    t = slot((a1,), [get_qkv[0]], [get_qkv[0], get_qkv[1], get_down])
     t = slot(t, [get_qkv[0]])
 
     qkv = []
     group = project_in(after(a1, *t), get_qkv[0].parts())
     qkv.append(group)
-    t = slot((group,), [get_qkv[1]], [get_qkv[1], get_down, get_up])
-    attended = attn_fwd(after(group, *t), 0, half, 0, width)
-    t = slot((attended[0],), [get_qkv[1], get_down], [get_down, get_proj])
-    attended = attn_fwd(after(group, *t), half, group_pairs - half, 0, width, attended)
-    t = (attended[0],)
+    t = slot((group,), [get_qkv[1], get_down], [get_qkv[1], get_down, get_up, get_proj])
+    attended = attn_fwd(after(group, *t), 0, group_pairs, 0, width)
+    t = slot((attended[0],), [get_qkv[1]])
     group = project_in(after(a1, *t), get_qkv[1].parts())
     qkv.append(group)
     mixture, log_totals = attn_fwd(group, 0, group_pairs, group_pairs, width, attended)
@@ -986,8 +986,11 @@
     t = slot(last.part(t), [up, first, proj], [up, last, first, proj])
     back = project_back(0, (0, 1), chunks, tokens, after(dh1, *t), added, g[0:1], p_qkv)
     t = slot((back[0],), [last, first, proj], [last, first])
-    back = project_back(1, (0, 1), chunks, tokens, after(dh1, *t), added, g[0:1], p_qkv, back)
+    back = project_back(1, (0, 2), chunks, tokens, after(dh1, *t), added, g[0:1], p_qkv, back)
+    t = slot((back[0],), [last, first], [last, first])
+    back = project_back(1, (1, 2), chunks, tokens, after(dh1, *t), added, g[0:1], p_qkv, back)
     grad_tokens, more = back
+    more = jnp.stack([more[0], more[2] + more[3]])
     grad_embed = jnp.sum(onehot[:, :, None] * more[:, None, 1, :], axis=0)
     grad_gains = jnp.concatenate([more[:, 0:1], sums_mid[:, 0:2], sums_out[:, 0:1]], axis=1).sum(axis=0)
     little = SmallSum(jnp.concatenate([grad_gains, grad_embed], axis=0))

time: 649 us -> 635 us (0.978)
  waiting for transfers between devices: 60 us -> 48.4 us
    ppermute x52, waiting for transfers between devices: 56.3 us -> 45.7 us  [swap(): return lax.ppermute(value, axis, [(i, i ^ 1 << bit) for i in range(size)])]
    pallas_call x2 -> x3, Pallas kernels: 36.3 us -> 42.7 us  [project_back(): pl.pallas_call(kernel, grid_spec=pltpu.PrefetchScalarGridSpec(num_scalar_...]
    pallas_call x3 -> x2, Pallas kernels: 44.1 us -> 39.5 us  [attn_fwd(): pl.pallas_call(kernel, grid=(slots, count), in_specs=[pl.BlockSpec((3, 1,...]
  transfers between devices with their start and end apart: 55 -> 55, of which waited for: 16 -> 17; matrix products, arithmetic and copies ran while one was open for 4% -> 4% of each run, Pallas kernels for 54% -> 56%
where the time goes in v3:
time: 635 us; the launch traced here: 626 us
  Pallas kernels  455 us (72%)
  starting transfers between devices  48.6 us (8%)
  waiting for transfers between devices  48.4 us (8%)
  other arithmetic  44 us (7%)
  between operations  15.6 us (2%)
  local copies, waits for them, and re-layouts  14.6 us (2%)
    pallas_call x1, Pallas kernels, up_and_down(): pl.pallas_call(kernel, grid_spec=pltpu.PrefetchScalarGridSpec(num_scalar_...  84.2 us
    pallas_call x8, Pallas kernels, narrow_grad_blocks(): pl.pallas_call(kernel, grid_spec=pltpu.PrefetchScalarGridSpec(num_scalar_...  79.7 us
    pallas_call x4, Pallas kernels, attn_bwd(): pl.pallas_call(attn_bwd_kernel, grid=(slots, count), in_specs=[triple, si...  78.2 us
    ppermute x52, starting transfers between devices, swap(): return lax.ppermute(value, axis, [(i, i ^ 1 << bit) for i in range(size)])  48.3 us
    ppermute x52, waiting for transfers between devices, swap(): return lax.ppermute(value, axis, [(i, i ^ 1 << bit) for i in range(size)])  45.7 us
    pallas_call x1, Pallas kernels, back_to_mixture(): pl.pallas_call(kernel, grid_spec=pltpu.PrefetchScalarGridSpec(num_scalar_...  44 us
    pallas_call x3, Pallas kernels, project_back(): pl.pallas_call(kernel, grid_spec=pltpu.PrefetchScalarGridSpec(num_scalar_...  42.7 us
    pallas_call x2, Pallas kernels, attn_fwd(): pl.pallas_call(kernel, grid=(slots, count), in_specs=[pl.BlockSpec((3, 1,...  39.5 us
  transfers between devices with their start and end apart: 55, of which 17 were waited for; matrix products, arithmetic and copies ran while one was open for 4% of the time, Pallas kernels for 56%

profile of v3, /device:TPU:0, one launch (start us, length us, event | category | flops | bytes accessed | tf_op | source)
XLA Modules:
  0.0 626.2 jit_solution(16948352681642325771)
XLA Ops:
  43.6 12.8 %project_in.2.x_ref = bf16[3,2,1088,512]{3,2,1,0:T(8,128)(2,1)} custom-call(s32[3]{0:T(128)} %pad_add_fusion.starts_ref, bf16[2,1088,1024]{2,1,0:T(8,128)(2,1)} %norm_in.1.a_ref, bf16[512,3072]{1,0:T(8,128)(2,1)} %copy-done, bf16[3,256,512]{2,1,0:T(8,128)(2,1)} %copy-done.3, bf16[3,256,512]{2,1,0:T(8,128)(2,1)} %copy-done.4), custom_call_target="tpu_custom_call" | custom-call | tf_op jit(solution)/shard_map/project_in/pallas_call | solution.py:139
  56.4 9.5 %collective-permute-done.3 = bf16[128,1024]{1,0:T(8,128)(2,1)} collective-permute-done((bf16[128,1024]{1,0:T(8,128)(2,1)S(1)}, bf16[128,1024]{1,0:T(8,128)(2,1)}, u32[]{:S(2)}, u32[]{:S(2)}) %collective-permute-start.3) | collective-permute-done | bytes 262176 | tf_op jit(solution)/shard_map/ppermute | solution.py:635
  68.0 19.8 %attn_fwd.2 = (bf16[2,1088,1024]{2,1,0:T(8,128)(2,1)}, f32[2,8,2,1088]{3,2,1,0:T(2,128)}) custom-call(bf16[3,2,1088,512]{3,2,1,0:T(8,128)(2,1)} %project_in.2.x_ref), custom_call_target="tpu_custom_call" | custom-call | tf_op jit(solution)/shard_map/attn_fwd/pallas_call | solution.py:212
  88.7 12.8 %project_in.3.x_ref = bf16[3,2,1088,512]{3,2,1,0:T(8,128)(2,1)} custom-call(s32[3]{0:T(128)} %pad_add_fusion.starts_ref, bf16[2,1088,1024]{2,1,0:T(8,128)(2,1)} %norm_in.1.a_ref, bf16[512,3072]{1,0:T(8,128)(2,1)} %copy-done, bf16[3,256,512]{2,1,0:T(8,128)(2,1)} %copy-done.5, bf16[3,256,512]{2,1,0:T(8,128)(2,1)} %copy-done.6), custom_call_target="tpu_custom_call" | custom-call | tf_op jit(solution)/shard_map/project_in/pallas_call | solution.py:139
  101.5 19.8 %attn_fwd.3 = (bf16[2,1088,1024]{2,1,0:T(8,128)(2,1)}, f32[2,8,2,1088]{3,2,1,0:T(2,128)}) custom-call(bf16[3,2,1088,512]{3,2,1,0:T(8,128)(2,1)} %project_in.3.x_ref, bf16[2,1088,1024]{2,1,0:T(8,128)(2,1)} %get-tuple-element.185.rest_0_, f32[2,8,2,1088]{3,2,1,0:T(2,128)} %get-tuple-element.187.rest_1_), custom_call_target="tpu_custom_call", output_to_operand_aliasing={{0}: (1, {}), {1}: (2, {})} | custom-call | tf_op jit(solution)/shard_map/attn_fwd/pallas_call | solution.py:212
  131.2 84.2 %up_and_down.1 = (bf16[2,1088,1024]{2,1,0:T(8,128)(2,1)}, bf16[2,1088,4096]{2,1,0:T(8,128)(2,1)}, bf16[2,1088,4096]{2,1,0:T(8,128)(2,1)}, bf16[2,1088,1024]{2,1,...) custom-call(s32[8]{0:T(128)} %stack.51.starts_ref, ...), custom_call_target="tpu_custom_call" | custom-call | tf_op jit(solution)/shard_map/up_and_down/pallas_call | solution.py:385
  215.4 15.3 %grad_blocks.10 = bf16[2,1,1024,1024]{3,2,1,0:T(8,128)(2,1)} custom-call(s32[2]{0:T(128)} %get-tuple-element.359.order_ref, bf16[2176,4096]{1,0:T(8,128)(2,1)} %bitcast.205, bf16[2176,1024]{1,0:T(8,128)(2,1)} %bitcast.214), custom_call_target="tpu_custom_call" | custom-call | tf_op jit(solution)/shard_map/grad_blocks/pallas_call | solution.py:580
  230.9 15.4 %grad_blocks.11 = bf16[2,4,256,1024]{3,2,1,0:T(8,128)(2,1)} custom-call(s32[2]{0:T(128)} %get-tuple-element.359.order_ref, bf16[2176,1024]{1,0:T(8,128)(2,1)} %bitcast.207, bf16[2176,1024]{1,0:T(8,128)(2,1)} %bitcast.208, bf16[2176,4096]{1,0:T(8,128)(2,1)} %bitcast.195), custom_call_target="tpu_custom_call" | custom-call | tf_op jit(solution)/shard_map/grad_blocks/pallas_call | solution.py:615
  246.6 16.5 %grad_blocks.12 = (bf16[1,1024,1024]{2,1,0:T(8,128)(2,1)}, bf16[1,1024,1024]{2,1,0:T(8,128)(2,1)}) custom-call(s32[2]{0:T(128)} %get-tuple-element.358.order_ref, bf16[2176,4096]{1,0:T(8,128)(2,1)} %bitcast.206, bf16[2176,1024]{1,0:T(8,128)(2,1)} %bitcast.215, bf16[2,1,1024,1024]{3,2,1,0:T(8,128)(2,1)} %collective-permute-done.10.rest_1_), custom_call_target="tpu_custom_call" | custom-call | tf_op jit(solution)/shard_map/grad_blocks/pallas_call | solution.py:580
  265.4 15.7 %grad_blocks.13 = (bf16[4,256,1024]{2,1,0:T(8,128)(2,1)}, bf16[4,256,1024]{2,1,0:T(8,128)(2,1)}) custom-call(s32[2]{0:T(128)} %get-tuple-element.358.order_ref, bf16[2176,1024]{1,0:T(8,128)(2,1)} %bitcast.209, bf16[2176,1024]{1,0:T(8,128)(2,1)} %bitcast.210, bf16[2176,4096]{1,0:T(8,128)(2,1)} %bitcast.196, ...), custom_call_target="tpu_custom_call" | custom-call | tf_op jit(solution)/shard_map/grad_blocks/pallas_call | solution.py:615
  281.1 44.0 %back_to_mixture.1 = (bf16[2,1088,1024]{2,1,0:T(8,128)(2,1)}, bf16[2,1088,1024]{2,1,0:T(8,128)(2,1)}, f32[2,1088,1024]{2,1,0:T(8,128)}, f32[2,8,1024]{2,1,0:T(8,128)}) custom-call(s32[6]{0:T(128)} %stack.61.starts_ref, s32[2]{0:T(128)} %compare_convert_fusion.1.live_ref, bf16[2,1088,4096]{2,1,0:T(8,128)(2,1)} %get-tuple-element.208.du_ref, ...), custom_call_target="tpu_custom_call" | custom-call | tf_op jit(solution)/shard_map/back_to_mixture/pallas_call | solution.py:439
  337.9 19.5 %attn_bwd.4.refs_in_0_ = bf16[3,2,1088,256]{3,2,1,0:T(8,128)(2,1)} custom-call(bf16[3,2,1088,512]{3,2,1,0:T(8,128)(2,1)} %project_in.2.x_ref, bf16[2,1088,1024]{2,1,0:T(8,128)(2,1)} %get-tuple-element.188.o_ref, bf16[2,1088,1024]{2,1,0:T(8,128)(2,1)} %get-tuple-element.250.do_ref, f32[2,8,2,1088]{3,2,1,0:T(2,128)} %get-tuple-element.219.l_ref), custom_call_target="tpu_custom_call" | custom-call | tf_op jit(solution)/shard_map/attn_bwd/pallas_call | solution.py:281
  363.4 7.3 %grad_blocks.15 = (bf16[1,256,1024]{2,1,0:T(8,128)(2,1)}, bf16[1,256,1024]{2,1,0:T(8,128)(2,1)}) custom-call(s32[2]{0:T(128)} %get-tuple-element.358.order_ref, bf16[2176,1024]{1,0:T(8,128)(2,1)} %bitcast.193, bf16[2176,1024]{1,0:T(8,128)(2,1)} %bitcast.194, bf16[2176,1024]{1,0:T(8,128)(2,1)} %bitcast.213, bf16[2,1,256,1024]{3,2,1,0:T(8,128)(2,1)} %copy-done.20), custom_call_target="tpu_custom_call" | custom-call | tf_op jit(solution)/shard_map/grad_blocks/pallas_call | solution.py:615
  373.9 19.8 %attn_bwd.5.refs_in_1_ = bf16[3,2,1088,256]{3,2,1,0:T(8,128)(2,1)} custom-call(bf16[3,2,1088,512]{3,2,1,0:T(8,128)(2,1)} %project_in.2.x_ref, bf16[2,1088,1024]{2,1,0:T(8,128)(2,1)} %get-tuple-element.188.o_ref, bf16[2,1088,1024]{2,1,0:T(8,128)(2,1)} %get-tuple-element.250.do_ref, f32[2,8,2,1088]{3,2,1,0:T(2,128)} %get-tuple-element.219.l_ref), custom_call_target="tpu_custom_call" | custom-call | tf_op jit(solution)/shard_map/attn_bwd/pallas_call | solution.py:281
  401.1 8.4 %grad_blocks.16 = bf16[2,3,256,512]{3,2,1,0:T(8,128)(2,1)} custom-call(s32[2]{0:T(128)} %get-tuple-element.359.order_ref, bf16[2176,1024]{1,0:T(8,128)(2,1)} %bitcast.183, bf16[2176,1024]{1,0:T(8,128)(2,1)} %bitcast.184, bf16[3,2176,256]{2,1,0:T(8,128)(2,1)} %bitcast.197, bf16[3,2176,256]{2,1,0:T(8,128)(2,1)} %bitcast.199), custom_call_target="tpu_custom_call" | custom-call | tf_op jit(solution)/shard_map/grad_blocks/pallas_call | solution.py:615
  413.7 19.5 %attn_bwd.6.refs_in_2_ = bf16[3,2,1088,256]{3,2,1,0:T(8,128)(2,1)} custom-call(bf16[3,2,1088,512]{3,2,1,0:T(8,128)(2,1)} %project_in.3.x_ref, bf16[2,1088,1024]{2,1,0:T(8,128)(2,1)} %get-tuple-element.188.o_ref, bf16[2,1088,1024]{2,1,0:T(8,128)(2,1)} %get-tuple-element.250.do_ref, f32[2,8,2,1088]{3,2,1,0:T(2,128)} %get-tuple-element.219.l_ref), custom_call_target="tpu_custom_call" | custom-call | tf_op jit(solution)/shard_map/attn_bwd/pallas_call | solution.py:281
  444.1 8.7 %grad_blocks.17 = (bf16[3,256,512]{2,1,0:T(8,128)(2,1)}, bf16[3,256,512]{2,1,0:T(8,128)(2,1)}) custom-call(s32[2]{0:T(128)} %get-tuple-element.358.order_ref, bf16[2176,1024]{1,0:T(8,128)(2,1)} %bitcast.185, bf16[2176,1024]{1,0:T(8,128)(2,1)} %bitcast.186, bf16[3,2176,256]{2,1,0:T(8,128)(2,1)} %bitcast.198, bf16[3,2176,256]{2,1,0:T(8,128)(2,1)} %bitcast.200, ...), custom_call_target="tpu_custom_call" | custom-call | tf_op jit(solution)/shard_map/grad_blocks/pallas_call | solution.py:615
  455.0 19.5 %attn_bwd.7.refs_in_3_ = bf16[3,2,1088,256]{3,2,1,0:T(8,128)(2,1)} custom-call(bf16[3,2,1088,512]{3,2,1,0:T(8,128)(2,1)} %project_in.3.x_ref, bf16[2,1088,1024]{2,1,0:T(8,128)(2,1)} %get-tuple-element.188.o_ref, bf16[2,1088,1024]{2,1,0:T(8,128)(2,1)} %get-tuple-element.250.do_ref, f32[2,8,2,1088]{3,2,1,0:T(2,128)} %get-tuple-element.219.l_ref), custom_call_target="tpu_custom_call" | custom-call | tf_op jit(solution)/shard_map/attn_bwd/pallas_call | solution.py:281
  478.0 8.4 %grad_blocks.18 = bf16[2,3,256,512]{3,2,1,0:T(8,128)(2,1)} custom-call(s32[2]{0:T(128)} %get-tuple-element.359.order_ref, bf16[2176,1024]{1,0:T(8,128)(2,1)} %bitcast.187, bf16[2176,1024]{1,0:T(8,128)(2,1)} %bitcast.188, bf16[3,2176,256]{2,1,0:T(8,128)(2,1)} %bitcast.201, bf16[3,2176,256]{2,1,0:T(8,128)(2,1)} %bitcast.203), custom_call_target="tpu_custom_call" | custom-call | tf_op jit(solution)/shard_map/grad_blocks/pallas_call | solution.py:615
  500.9 8.6 %grad_blocks.19 = (bf16[3,256,512]{2,1,0:T(8,128)(2,1)}, bf16[3,256,512]{2,1,0:T(8,128)(2,1)}) custom-call(s32[2]{0:T(128)} %get-tuple-element.358.order_ref, bf16[2176,1024]{1,0:T(8,128)(2,1)} %bitcast.189, bf16[2176,1024]{1,0:T(8,128)(2,1)} %bitcast.190, bf16[3,2176,256]{2,1,0:T(8,128)(2,1)} %bitcast.202, bf16[3,2176,256]{2,1,0:T(8,128)(2,1)} %bitcast.204, ...), custom_call_target="tpu_custom_call" | custom-call | tf_op jit(solution)/shard_map/grad_blocks/pallas_call | solution.py:615
  515.5 18.3 %project_back.3 = (f32[2,1088,1024]{2,1,0:T(8,128)}, f32[4,8,1024]{2,1,0:T(8,128)}) custom-call(s32[6]{0:T(128)} %stack.61.starts_ref, bf16[3,2,1088,256]{3,2,1,0:T(8,128)(2,1)} %attn_bwd.4.refs_in_0_, bf16[3,2,1088,256]{3,2,1,0:T(8,128)(2,1)} %attn_bwd.5.refs_in_1_, bf16[3,2,1088,256]{3,2,1,0:T(8,128)(2,1)} %attn_bwd.6.refs_in_2_, ...), custom_call_target="tpu_custom_call" | custom-call | tf_op jit(solution)/shard_map/project_back/pallas_call | solution.py:505
  538.8 12.1 %project_back.4 = (f32[2,1088,1024]{2,1,0:T(8,128)}, f32[4,8,1024]{2,1,0:T(8,128)}) custom-call(s32[6]{0:T(128)} %stack.61.starts_ref, bf16[3,2,1088,256]{3,2,1,0:T(8,128)(2,1)} %attn_bwd.4.refs_in_0_, bf16[3,2,1088,256]{3,2,1,0:T(8,128)(2,1)} %attn_bwd.5.refs_in_1_, ...), custom_call_target="tpu_custom_call", output_to_operand_aliasing={{0}: (15, {}), {1}: (16, {})} | custom-call | tf_op jit(solution)/shard_map/project_back/pallas_call | solution.py:505
  553.5 12.4 %project_back.5 = (f32[2,1088,1024]{2,1,0:T(8,128)}, f32[4,8,1024]{2,1,0:T(8,128)}) custom-call(s32[6]{0:T(128)} %stack.61.starts_ref, bf16[3,2,1088,256]{3,2,1,0:T(8,128)(2,1)} %attn_bwd.4.refs_in_0_, bf16[3,2,1088,256]{3,2,1,0:T(8,128)(2,1)} %attn_bwd.5.refs_in_1_, ...), custom_call_target="tpu_custom_call", output_to_operand_aliasing={{0}: (15, {}), {1}: (16, {})} | custom-call | tf_op jit(solution)/shard_map/project_back/pallas_call | solution.py:505
  578.5 7.4 %in_rows.3 = f32[512,4096]{1,0:T(8,128)} custom-call(bf16[16,4,32,1024]{3,2,1,0:T(8,128)(2,1)} %bitcast.216), custom_call_target="tpu_custom_call" | custom-call | tf_op jit(solution)/shard_map/in_rows/pallas_call | solution.py:819
  (267 shorter events, 175.3 us)
Async XLA Ops:
  7.2 122.8 %all-gather.6.cloned.1.call-start = ((), (), s32[]{:S(2)}) async-start(), calls=%async_computation | async-start | bytes 4456448 | tf_op jit(solution)/shard_map/all_gather | solution.py:723
  15.6 24.2 %collective-permute-start.1 = (bf16[3,256,512]{2,1,0:T(8,128)(2,1)}, bf16[3,256,512]{2,1,0:T(8,128)(2,1)S(1)}, u32[]{:S(2)}, u32[]{:S(2)}) collective-permute-start(bf16[3,256,512]{2,1,0:T(8,128)(2,1)} %get-tuple-element.168), channel_id=1, source_target_pairs={{0,1},{1,0},{2,3},{3,2},{4,5},{5,4},{6,7},{7,6},{8,9},{9,8},{10,11... | collective-permute-start | bytes 2359304 | tf_op jit(solution)/shard_map/ppermute | solution.py:635
  39.9 25.9 %collective-permute-start.2 = (bf16[3,256,512]{2,1,0:T(8,128)(2,1)S(1)}, bf16[3,256,512]{2,1,0:T(8,128)(2,1)S(1)}, u32[]{:S(2)}, u32[]{:S(2)}) collective-permute-start(bf16[3,256,512]{2,1,0:T(8,128)(2,1)S(1)} %copy-done.23), channel_id=1, source_target_pairs={{0,1},{1,0},{2,3},{3,2},{4,5},{5,4},{6,7},{7,6},{8,9},{9,8},{10,11... | collective-permute-start | bytes 2359304 | tf_op jit(solution)/shard_map/ppermute | solution.py:635
  42.0 23.9 %collective-permute-start.3 = (bf16[128,1024]{1,0:T(8,128)(2,1)S(1)}, bf16[128,1024]{1,0:T(8,128)(2,1)}, u32[]{:S(2)}, u32[]{:S(2)}) collective-permute-start(bf16[128,1024]{1,0:T(8,128)(2,1)S(1)} %dynamic-slice_bitcast_fusion.3), channel_id=1, source_target_pairs={{0,1},{1,0},{2,3},{3,2},{4,5},{5,4},{6,7},{7,6},{8,9},{9,8},{10,11... | collective-permute-start | bytes 786440 | tf_op jit(solution)/shard_map/ppermute | solution.py:635
  65.9 428.6 %all-gather.8.cloned.1.call-start = ((), (), s32[]{:S(2)}) async-start(), calls=%async_computation.1 | async-start | bytes 4456448 | tf_op jit(solution)/shard_map/all_gather | solution.py:866
  65.9 58.9 %collective-permute-start.6 = (bf16[256,4096]{1,0:T(8,128)(2,1)}, bf16[256,4096]{1,0:T(8,128)(2,1)}, u32[]{:S(2)}, u32[]{:S(2)}) collective-permute-start(bf16[256,4096]{1,0:T(8,128)(2,1)} %constant_dynamic-slice_fusion.2), channel_id=1, source_target_pairs={{0,1},{1,0},{2,3},{3,2},{4,5},{5,4},{6,7},{7,6},{8,9},{9,8},{10,11... | collective-permute-start | bytes 6291464 | tf_op jit(solution)/shard_map/ppermute | solution.py:635
  67.7 20.0 %collective-permute-start.5 = (bf16[3,256,512]{2,1,0:T(8,128)(2,1)S(1)}, bf16[3,256,512]{2,1,0:T(8,128)(2,1)S(1)}, u32[]{:S(2)}, u32[]{:S(2)}) collective-permute-start(bf16[3,256,512]{2,1,0:T(8,128)(2,1)S(1)} %collective-permute-done.2.rest_1_.refs_in_12_), channel_id=1, source_target_pairs={{0,2},{2,0},{4,6},{6,4},{8,10},{10,8},{12,14},{14,12},{16,18},{18,... | collective-permute-start | bytes 2359304 | tf_op jit(solution)/shard_map/ppermute | solution.py:635
  67.7 57.0 %collective-permute-start.7 = (bf16[256,1024]{1,0:T(8,128)(2,1)}, bf16[256,1024]{1,0:T(8,128)(2,1)S(1)}, u32[]{:S(2)}, u32[]{:S(2)}) collective-permute-start(bf16[256,1024]{1,0:T(8,128)(2,1)} %constant_dynamic-slice_fusion.3), channel_id=1, source_target_pairs={{0,1},{1,0},{2,3},{3,2},{4,5},{5,4},{6,7},{7,6},{8,9},{9,8},{10,11... | collective-permute-start | bytes 1572872 | tf_op jit(solution)/shard_map/ppermute | solution.py:635
  263.1 62.0 %collective-permute-start.12 = (bf16[1,1024,1024]{2,1,0:T(8,128)(2,1)}, bf16[1,1024,1024]{2,1,0:T(8,128)(2,1)}, u32[]{:S(2)}, u32[]{:S(2)}) collective-permute-start(bf16[1,1024,1024]{2,1,0:T(8,128)(2,1)} %get-tuple-element.204), channel_id=1, source_target_pairs={{0,1},{1,0},{2,3},{3,2},{4,5},{5,4},{6,7},{7,6},{8,9},{9,8},{10,11... | collective-permute-start | bytes 6291464 | tf_op jit(solution)/shard_map/ppermute | solution.py:635
  328.6 65.1 %collective-permute-start.15 = (bf16[4,256,1024]{2,1,0:T(8,128)(2,1)}, bf16[4,256,1024]{2,1,0:T(8,128)(2,1)}, u32[]{:S(2)}, u32[]{:S(2)}) collective-permute-start(bf16[4,256,1024]{2,1,0:T(8,128)(2,1)} %get-tuple-element.216), channel_id=1, source_target_pairs={{0,1},{1,0},{2,3},{3,2},{4,5},{5,4},{6,7},{7,6},{8,9},{9,8},{10,11... | collective-permute-start | bytes 6291464 | tf_op jit(solution)/shard_map/ppermute | solution.py:635
  336.3 21.1 %collective-permute-start.14 = (bf16[2,1,256,1024]{3,2,1,0:T(8,128)(2,1)}, bf16[2,1,256,1024]{3,2,1,0:T(8,128)(2,1)S(1)}, u32[]{:S(2)}, u32[]{:S(2)}) collective-permute-start(bf16[2,1,256,1024]{3,2,1,0:T(8,128)(2,1)} %grad_blocks.14), channel_id=1, source_target_pairs={{0,2},{2,0},{4,6},{6,4},{8,10},{10,8},{12,14},{14,12},{16,18},{18,... | collective-permute-start | bytes 3145736 | tf_op jit(solution)/shard_map/ppermute | solution.py:635
  336.3 25.8 %collective-permute-start.13 = (bf16[1,512,1024]{2,1,0:T(8,128)(2,1)}, bf16[1,512,1024]{2,1,0:T(8,128)(2,1)S(1)}, u32[]{:S(2)}, u32[]{:S(2)}) collective-permute-start(bf16[1,512,1024]{2,1,0:T(8,128)(2,1)} %get-tuple-element.215), channel_id=1, source_target_pairs={{0,4},{2,6},{4,0},{6,2},{8,12},{10,14},{12,8},{14,10},{16,20},{18,... | collective-permute-start | bytes 3145736 | tf_op jit(solution)/shard_map/ppermute | solution.py:635
  370.7 23.0 %collective-permute-start.17 = (bf16[1,256,1024]{2,1,0:T(8,128)(2,1)}, bf16[1,256,1024]{2,1,0:T(8,128)(2,1)}, u32[]{:S(2)}, u32[]{:S(2)}) collective-permute-start(bf16[1,256,1024]{2,1,0:T(8,128)(2,1)} %get-tuple-element.223), channel_id=1, source_target_pairs={{0,1},{1,0},{2,3},{3,2},{4,5},{5,4},{6,7},{7,6},{8,9},{9,8},{10,11... | collective-permute-start | bytes 1572872 | tf_op jit(solution)/shard_map/ppermute | solution.py:635
  372.3 21.3 %collective-permute-start.16 = (bf16[1,256,1024]{2,1,0:T(8,128)(2,1)}, bf16[1,256,1024]{2,1,0:T(8,128)(2,1)S(1)}, u32[]{:S(2)}, u32[]{:S(2)}) collective-permute-start(bf16[1,256,1024]{2,1,0:T(8,128)(2,1)} %get-tuple-element.337), channel_id=1, source_target_pairs={{0,8},{2,10},{4,12},{6,14},{8,0},{10,2},{12,4},{14,6},{16,24},{18,... | collective-permute-start | bytes 1572872 | tf_op jit(solution)/shard_map/ppermute | solution.py:635
  410.2 25.9 %collective-permute-start.21 = (bf16[2,3,256,512]{3,2,1,0:T(8,128)(2,1)}, bf16[2,3,256,512]{3,2,1,0:T(8,128)(2,1)S(1)}, u32[]{:S(2)}, u32[]{:S(2)}) collective-permute-start(bf16[2,3,256,512]{3,2,1,0:T(8,128)(2,1)} %grad_blocks.16), channel_id=1, source_target_pairs={{0,2},{2,0},{4,6},{6,4},{8,10},{10,8},{12,14},{14,12},{16,18},{18,... | collective-permute-start | bytes 4718600 | tf_op jit(solution)/shard_map/ppermute | solution.py:635
  410.2 25.9 %collective-permute-start.19 = (bf16[4,128,1024]{2,1,0:T(8,128)(2,1)}, bf16[4,128,1024]{2,1,0:T(8,128)(2,1)}, u32[]{:S(2)}, u32[]{:S(2)}) collective-permute-start(bf16[4,128,1024]{2,1,0:T(8,128)(2,1)} %get-tuple-element.230), channel_id=1, source_target_pairs={{0,4},{2,6},{4,0},{6,2},{8,12},{10,14},{12,8},{14,10},{16,20},{18,... | collective-permute-start | bytes 3145736 | tf_op jit(solution)/shard_map/ppermute | solution.py:635
  410.7 22.6 %collective-permute-start.20 = (bf16[1,128,1024]{2,1,0:T(8,128)(2,1)S(1)}, bf16[1,128,1024]{2,1,0:T(8,128)(2,1)}, u32[]{:S(2)}, u32[]{:S(2)}) collective-permute-start(bf16[1,128,1024]{2,1,0:T(8,128)(2,1)S(1)} %fusion.8), channel_id=1, source_target_pairs={{0,16},{2,18},{4,20},{6,22},{8,24},{10,26},{12,28},{14,30},{16,0},... | collective-permute-start | bytes 786440 | tf_op jit(solution)/shard_map/ppermute | solution.py:635
  413.3 20.0 %collective-permute-start.22 = (bf16[1,64,1024]{2,1,0:T(8,128)(2,1)}, bf16[1,64,1024]{2,1,0:T(8,128)(2,1)}, u32[]{:S(2)}, u32[]{:S(2)}) collective-permute-start(bf16[1,64,1024]{2,1,0:T(8,128)(2,1)} %get-tuple-element.236), channel_id=1, source_target_pairs={{0,8},{2,10},{4,12},{6,14},{8,0},{10,2},{12,4},{14,6},{16,24},{18,... | collective-permute-start | bytes 393224 | tf_op jit(solution)/shard_map/ppermute | solution.py:635
  441.2 137.3 %all-gather.10.cloned.1.call-start = ((), (), s32[]{:S(2)}) async-start(), calls=%async_computation.2 | async-start | bytes 4456448 | tf_op jit(solution)/shard_map/all_gather | solution.py:866
  453.6 20.8 %collective-permute-start.25 = (bf16[3,256,512]{2,1,0:T(8,128)(2,1)}, bf16[3,256,512]{2,1,0:T(8,128)(2,1)S(1)}, u32[]{:S(2)}, u32[]{:S(2)}) collective-permute-start(bf16[3,256,512]{2,1,0:T(8,128)(2,1)} %get-tuple-element.248), channel_id=1, source_target_pairs={{0,1},{1,0},{2,3},{3,2},{4,5},{5,4},{6,7},{7,6},{8,9},{9,8},{10,11... | collective-permute-start | bytes 2359304 | tf_op jit(solution)/shard_map/ppermute | solution.py:635
  454.2 20.2 %collective-permute-start.24 = (bf16[4,64,1024]{2,1,0:T(8,128)(2,1)}, bf16[4,64,1024]{2,1,0:T(8,128)(2,1)S(1)}, u32[]{:S(2)}, u32[]{:S(2)}) collective-permute-start(bf16[4,64,1024]{2,1,0:T(8,128)(2,1)} %get-tuple-element.241), channel_id=1, source_target_pairs={{0,8},{2,10},{4,12},{6,14},{8,0},{10,2},{12,4},{14,6},{16,24},{18,... | collective-permute-start | bytes 1572872 | tf_op jit(solution)/shard_map/ppermute | solution.py:635
  454.7 19.8 %collective-permute-start.26 = (bf16[1,32,1024]{2,1,0:T(8,128)(2,1)S(1)}, bf16[1,32,1024]{2,1,0:T(8,128)(2,1)S(1)}, u32[]{:S(2)}, u32[]{:S(2)}) collective-permute-start(bf16[1,32,1024]{2,1,0:T(8,128)(2,1)S(1)} %fusion.19), channel_id=1, source_target_pairs={{0,16},{2,18},{4,20},{6,22},{8,24},{10,26},{12,28},{14,30},{16,0},... | collective-permute-start | bytes 196616 | tf_op jit(solution)/shard_map/ppermute | solution.py:635
  488.6 20.9 %collective-permute-start.30 = (bf16[3,128,512]{2,1,0:T(8,128)(2,1)}, bf16[3,128,512]{2,1,0:T(8,128)(2,1)S(1)}, u32[]{:S(2)}, u32[]{:S(2)}) collective-permute-start(bf16[3,128,512]{2,1,0:T(8,128)(2,1)} %get-tuple-element.257), channel_id=1, source_target_pairs={{0,4},{2,6},{4,0},{6,2},{8,12},{10,14},{12,8},{14,10},{16,20},{18,... | collective-permute-start | bytes 1179656 | tf_op jit(solution)/shard_map/ppermute | solution.py:635
  512.7 21.2 %collective-permute-start.32 = (bf16[3,256,512]{2,1,0:T(8,128)(2,1)}, bf16[3,256,512]{2,1,0:T(8,128)(2,1)S(1)}, u32[]{:S(2)}, u32[]{:S(2)}) collective-permute-start(bf16[3,256,512]{2,1,0:T(8,128)(2,1)} %get-tuple-element.270), channel_id=1, source_target_pairs={{0,1},{1,0},{2,3},{3,2},{4,5},{5,4},{6,7},{7,6},{8,9},{9,8},{10,11... | collective-permute-start | bytes 2359304 | tf_op jit(solution)/shard_map/ppermute | solution.py:635
  (69 other events, 724.8 us)
Sparse Core Ops, SparseCore 0:
  66.0 52.2 all-gather.5
  441.3 53.1 all-gather.7
  512.8 56.8 all-gather.9

commit v4 on v3

--- a/solution.py
+++ b/solution.py
@@ -255,7 +255,8 @@
         p = jnp.exp(both[0] - l_ref[0, 0, h : h + 1, a:b])
         if a == lo:
             p = jnp.where(causal(p, True), p, 0.0)
-        return p.astype(jnp.bfloat16), (p * (both[1] - deltas[h][:, a:b])).astype(jnp.bfloat16)
+        p = p.astype(jnp.bfloat16)
+        return p, p * (both[1] - deltas[h][:, a:b]).astype(jnp.bfloat16)
 
     def collect(job, parts):
         lo, hi, h, a, b = job

time: 635 us -> 635 us (level)
  transfers between devices with their start and end apart: 55 -> 55, of which waited for: 17 -> 18; matrix products, arithmetic and copies ran while one was open for 4% -> 4% of each run, Pallas kernels for 56% -> 56%
where the time goes in v4:
time: 635 us; the launch traced here: 626 us
  Pallas kernels  454 us (71%)
  starting transfers between devices  49 us (8%)
  waiting for transfers between devices  48.9 us (8%)
  other arithmetic  44 us (7%)
  between operations  15.6 us (2%)
  local copies, waits for them, and re-layouts  14.6 us (2%)
    pallas_call x1, Pallas kernels, up_and_down(): pl.pallas_call(kernel, grid_spec=pltpu.PrefetchScalarGridSpec(num_scalar_...  84.2 us
    pallas_call x8, Pallas kernels, narrow_grad_blocks(): pl.pallas_call(kernel, grid_spec=pltpu.PrefetchScalarGridSpec(num_scalar_...  79.7 us
    pallas_call x4, Pallas kernels, attn_bwd(): pl.pallas_call(attn_bwd_kernel, grid=(slots, count), in_specs=[triple, si...  77.3 us
    ppermute x52, starting transfers between devices, swap(): return lax.ppermute(value, axis, [(i, i ^ 1 << bit) for i in range(size)])  48.6 us
    ppermute x52, waiting for transfers between devices, swap(): return lax.ppermute(value, axis, [(i, i ^ 1 << bit) for i in range(size)])  46 us
    pallas_call x1, Pallas kernels, back_to_mixture(): pl.pallas_call(kernel, grid_spec=pltpu.PrefetchScalarGridSpec(num_scalar_...  44 us
    pallas_call x3, Pallas kernels, project_back(): pl.pallas_call(kernel, grid_spec=pltpu.PrefetchScalarGridSpec(num_scalar_...  42.7 us
    pallas_call x2, Pallas kernels, attn_fwd(): pl.pallas_call(kernel, grid=(slots, count), in_specs=[pl.BlockSpec((3, 1,...  39.5 us
  transfers between devices with their start and end apart: 55, of which 18 were waited for; matrix products, arithmetic and copies ran while one was open for 4% of the time, Pallas kernels for 56%

profile of v4, /device:TPU:0, one launch (start us, length us, event | category | flops | bytes accessed | tf_op | source)
XLA Modules:
  0.0 626.1 jit_solution(13637765816454807302)
XLA Ops:
  43.6 12.8 %project_in.2.x_ref = bf16[3,2,1088,512]{3,2,1,0:T(8,128)(2,1)} custom-call(s32[3]{0:T(128)} %pad_add_fusion.starts_ref, bf16[2,1088,1024]{2,1,0:T(8,128)(2,1)} %norm_in.1.a_ref, bf16[512,3072]{1,0:T(8,128)(2,1)} %copy-done, bf16[3,256,512]{2,1,0:T(8,128)(2,1)} %copy-done.3, bf16[3,256,512]{2,1,0:T(8,128)(2,1)} %copy-done.4), custom_call_target="tpu_custom_call" | custom-call | tf_op jit(solution)/shard_map/project_in/pallas_call | solution.py:139
  56.4 9.5 %collective-permute-done.3 = bf16[128,1024]{1,0:T(8,128)(2,1)} collective-permute-done((bf16[128,1024]{1,0:T(8,128)(2,1)S(1)}, bf16[128,1024]{1,0:T(8,128)(2,1)}, u32[]{:S(2)}, u32[]{:S(2)}) %collective-permute-start.3) | collective-permute-done | bytes 262176 | tf_op jit(solution)/shard_map/ppermute | solution.py:636
  68.0 19.8 %attn_fwd.2 = (bf16[2,1088,1024]{2,1,0:T(8,128)(2,1)}, f32[2,8,2,1088]{3,2,1,0:T(2,128)}) custom-call(bf16[3,2,1088,512]{3,2,1,0:T(8,128)(2,1)} %project_in.2.x_ref), custom_call_target="tpu_custom_call" | custom-call | tf_op jit(solution)/shard_map/attn_fwd/pallas_call | solution.py:212
  88.7 12.8 %project_in.3.x_ref = bf16[3,2,1088,512]{3,2,1,0:T(8,128)(2,1)} custom-call(s32[3]{0:T(128)} %pad_add_fusion.starts_ref, bf16[2,1088,1024]{2,1,0:T(8,128)(2,1)} %norm_in.1.a_ref, bf16[512,3072]{1,0:T(8,128)(2,1)} %copy-done, bf16[3,256,512]{2,1,0:T(8,128)(2,1)} %copy-done.5, bf16[3,256,512]{2,1,0:T(8,128)(2,1)} %copy-done.6), custom_call_target="tpu_custom_call" | custom-call | tf_op jit(solution)/shard_map/project_in/pallas_call | solution.py:139
  101.5 19.8 %attn_fwd.3 = (bf16[2,1088,1024]{2,1,0:T(8,128)(2,1)}, f32[2,8,2,1088]{3,2,1,0:T(2,128)}) custom-call(bf16[3,2,1088,512]{3,2,1,0:T(8,128)(2,1)} %project_in.3.x_ref, bf16[2,1088,1024]{2,1,0:T(8,128)(2,1)} %get-tuple-element.185.rest_0_, f32[2,8,2,1088]{3,2,1,0:T(2,128)} %get-tuple-element.187.rest_1_), custom_call_target="tpu_custom_call", output_to_operand_aliasing={{0}: (1, {}), {1}: (2, {})} | custom-call | tf_op jit(solution)/shard_map/attn_fwd/pallas_call | solution.py:212
  131.2 84.2 %up_and_down.1 = (bf16[2,1088,1024]{2,1,0:T(8,128)(2,1)}, bf16[2,1088,4096]{2,1,0:T(8,128)(2,1)}, bf16[2,1088,4096]{2,1,0:T(8,128)(2,1)}, bf16[2,1088,1024]{2,1,...) custom-call(s32[8]{0:T(128)} %stack.51.starts_ref, ...), custom_call_target="tpu_custom_call" | custom-call | tf_op jit(solution)/shard_map/up_and_down/pallas_call | solution.py:386
  215.4 15.3 %grad_blocks.10 = bf16[2,1,1024,1024]{3,2,1,0:T(8,128)(2,1)} custom-call(s32[2]{0:T(128)} %get-tuple-element.359.order_ref, bf16[2176,4096]{1,0:T(8,128)(2,1)} %bitcast.205, bf16[2176,1024]{1,0:T(8,128)(2,1)} %bitcast.214), custom_call_target="tpu_custom_call" | custom-call | tf_op jit(solution)/shard_map/grad_blocks/pallas_call | solution.py:581
  230.9 15.4 %grad_blocks.11 = bf16[2,4,256,1024]{3,2,1,0:T(8,128)(2,1)} custom-call(s32[2]{0:T(128)} %get-tuple-element.359.order_ref, bf16[2176,1024]{1,0:T(8,128)(2,1)} %bitcast.207, bf16[2176,1024]{1,0:T(8,128)(2,1)} %bitcast.208, bf16[2176,4096]{1,0:T(8,128)(2,1)} %bitcast.195), custom_call_target="tpu_custom_call" | custom-call | tf_op jit(solution)/shard_map/grad_blocks/pallas_call | solution.py:616
  246.6 16.5 %grad_blocks.12 = (bf16[1,1024,1024]{2,1,0:T(8,128)(2,1)}, bf16[1,1024,1024]{2,1,0:T(8,128)(2,1)}) custom-call(s32[2]{0:T(128)} %get-tuple-element.358.order_ref, bf16[2176,4096]{1,0:T(8,128)(2,1)} %bitcast.206, bf16[2176,1024]{1,0:T(8,128)(2,1)} %bitcast.215, bf16[2,1,1024,1024]{3,2,1,0:T(8,128)(2,1)} %collective-permute-done.10.rest_1_), custom_call_target="tpu_custom_call" | custom-call | tf_op jit(solution)/shard_map/grad_blocks/pallas_call | solution.py:581
  265.4 15.7 %grad_blocks.13 = (bf16[4,256,1024]{2,1,0:T(8,128)(2,1)}, bf16[4,256,1024]{2,1,0:T(8,128)(2,1)}) custom-call(s32[2]{0:T(128)} %get-tuple-element.358.order_ref, bf16[2176,1024]{1,0:T(8,128)(2,1)} %bitcast.209, bf16[2176,1024]{1,0:T(8,128)(2,1)} %bitcast.210, bf16[2176,4096]{1,0:T(8,128)(2,1)} %bitcast.196, ...), custom_call_target="tpu_custom_call" | custom-call | tf_op jit(solution)/shard_map/grad_blocks/pallas_call | solution.py:616
  281.1 44.0 %back_to_mixture.1 = (bf16[2,1088,1024]{2,1,0:T(8,128)(2,1)}, bf16[2,1088,1024]{2,1,0:T(8,128)(2,1)}, f32[2,1088,1024]{2,1,0:T(8,128)}, f32[2,8,1024]{2,1,0:T(8,128)}) custom-call(s32[6]{0:T(128)} %stack.61.starts_ref, s32[2]{0:T(128)} %compare_convert_fusion.1.live_ref, bf16[2,1088,4096]{2,1,0:T(8,128)(2,1)} %get-tuple-element.208.du_ref, ...), custom_call_target="tpu_custom_call" | custom-call | tf_op jit(solution)/shard_map/back_to_mixture/pallas_call | solution.py:440
  337.9 19.2 %attn_bwd.4.refs_in_0_ = bf16[3,2,1088,256]{3,2,1,0:T(8,128)(2,1)} custom-call(bf16[3,2,1088,512]{3,2,1,0:T(8,128)(2,1)} %project_in.2.x_ref, bf16[2,1088,1024]{2,1,0:T(8,128)(2,1)} %get-tuple-element.188.o_ref, bf16[2,1088,1024]{2,1,0:T(8,128)(2,1)} %get-tuple-element.250.do_ref, f32[2,8,2,1088]{3,2,1,0:T(2,128)} %get-tuple-element.219.l_ref), custom_call_target="tpu_custom_call" | custom-call | tf_op jit(solution)/shard_map/attn_bwd/pallas_call | solution.py:282
  363.4 7.3 %grad_blocks.15 = (bf16[1,256,1024]{2,1,0:T(8,128)(2,1)}, bf16[1,256,1024]{2,1,0:T(8,128)(2,1)}) custom-call(s32[2]{0:T(128)} %get-tuple-element.358.order_ref, bf16[2176,1024]{1,0:T(8,128)(2,1)} %bitcast.193, bf16[2176,1024]{1,0:T(8,128)(2,1)} %bitcast.194, bf16[2176,1024]{1,0:T(8,128)(2,1)} %bitcast.213, bf16[2,1,256,1024]{3,2,1,0:T(8,128)(2,1)} %copy-done.20), custom_call_target="tpu_custom_call" | custom-call | tf_op jit(solution)/shard_map/grad_blocks/pallas_call | solution.py:616
  373.9 19.6 %attn_bwd.5.refs_in_1_ = bf16[3,2,1088,256]{3,2,1,0:T(8,128)(2,1)} custom-call(bf16[3,2,1088,512]{3,2,1,0:T(8,128)(2,1)} %project_in.2.x_ref, bf16[2,1088,1024]{2,1,0:T(8,128)(2,1)} %get-tuple-element.188.o_ref, bf16[2,1088,1024]{2,1,0:T(8,128)(2,1)} %get-tuple-element.250.do_ref, f32[2,8,2,1088]{3,2,1,0:T(2,128)} %get-tuple-element.219.l_ref), custom_call_target="tpu_custom_call" | custom-call | tf_op jit(solution)/shard_map/attn_bwd/pallas_call | solution.py:282
  400.9 8.4 %grad_blocks.16 = bf16[2,3,256,512]{3,2,1,0:T(8,128)(2,1)} custom-call(s32[2]{0:T(128)} %get-tuple-element.359.order_ref, bf16[2176,1024]{1,0:T(8,128)(2,1)} %bitcast.183, bf16[2176,1024]{1,0:T(8,128)(2,1)} %bitcast.184, bf16[3,2176,256]{2,1,0:T(8,128)(2,1)} %bitcast.197, bf16[3,2176,256]{2,1,0:T(8,128)(2,1)} %bitcast.199), custom_call_target="tpu_custom_call" | custom-call | tf_op jit(solution)/shard_map/grad_blocks/pallas_call | solution.py:616
  413.6 19.2 %attn_bwd.6.refs_in_2_ = bf16[3,2,1088,256]{3,2,1,0:T(8,128)(2,1)} custom-call(bf16[3,2,1088,512]{3,2,1,0:T(8,128)(2,1)} %project_in.3.x_ref, bf16[2,1088,1024]{2,1,0:T(8,128)(2,1)} %get-tuple-element.188.o_ref, bf16[2,1088,1024]{2,1,0:T(8,128)(2,1)} %get-tuple-element.250.do_ref, f32[2,8,2,1088]{3,2,1,0:T(2,128)} %get-tuple-element.219.l_ref), custom_call_target="tpu_custom_call" | custom-call | tf_op jit(solution)/shard_map/attn_bwd/pallas_call | solution.py:282
  443.9 8.7 %grad_blocks.17 = (bf16[3,256,512]{2,1,0:T(8,128)(2,1)}, bf16[3,256,512]{2,1,0:T(8,128)(2,1)}) custom-call(s32[2]{0:T(128)} %get-tuple-element.358.order_ref, bf16[2176,1024]{1,0:T(8,128)(2,1)} %bitcast.185, bf16[2176,1024]{1,0:T(8,128)(2,1)} %bitcast.186, bf16[3,2176,256]{2,1,0:T(8,128)(2,1)} %bitcast.198, bf16[3,2176,256]{2,1,0:T(8,128)(2,1)} %bitcast.200, ...), custom_call_target="tpu_custom_call" | custom-call | tf_op jit(solution)/shard_map/grad_blocks/pallas_call | solution.py:616
  454.8 19.3 %attn_bwd.7.refs_in_3_ = bf16[3,2,1088,256]{3,2,1,0:T(8,128)(2,1)} custom-call(bf16[3,2,1088,512]{3,2,1,0:T(8,128)(2,1)} %project_in.3.x_ref, bf16[2,1088,1024]{2,1,0:T(8,128)(2,1)} %get-tuple-element.188.o_ref, bf16[2,1088,1024]{2,1,0:T(8,128)(2,1)} %get-tuple-element.250.do_ref, f32[2,8,2,1088]{3,2,1,0:T(2,128)} %get-tuple-element.219.l_ref), custom_call_target="tpu_custom_call" | custom-call | tf_op jit(solution)/shard_map/attn_bwd/pallas_call | solution.py:282
  477.6 8.4 %grad_blocks.18 = bf16[2,3,256,512]{3,2,1,0:T(8,128)(2,1)} custom-call(s32[2]{0:T(128)} %get-tuple-element.359.order_ref, bf16[2176,1024]{1,0:T(8,128)(2,1)} %bitcast.187, bf16[2176,1024]{1,0:T(8,128)(2,1)} %bitcast.188, bf16[3,2176,256]{2,1,0:T(8,128)(2,1)} %bitcast.201, bf16[3,2176,256]{2,1,0:T(8,128)(2,1)} %bitcast.203), custom_call_target="tpu_custom_call" | custom-call | tf_op jit(solution)/shard_map/grad_blocks/pallas_call | solution.py:616
  500.8 8.6 %grad_blocks.19 = (bf16[3,256,512]{2,1,0:T(8,128)(2,1)}, bf16[3,256,512]{2,1,0:T(8,128)(2,1)}) custom-call(s32[2]{0:T(128)} %get-tuple-element.358.order_ref, bf16[2176,1024]{1,0:T(8,128)(2,1)} %bitcast.189, bf16[2176,1024]{1,0:T(8,128)(2,1)} %bitcast.190, bf16[3,2176,256]{2,1,0:T(8,128)(2,1)} %bitcast.202, bf16[3,2176,256]{2,1,0:T(8,128)(2,1)} %bitcast.204, ...), custom_call_target="tpu_custom_call" | custom-call | tf_op jit(solution)/shard_map/grad_blocks/pallas_call | solution.py:616
  515.4 18.3 %project_back.3 = (f32[2,1088,1024]{2,1,0:T(8,128)}, f32[4,8,1024]{2,1,0:T(8,128)}) custom-call(s32[6]{0:T(128)} %stack.61.starts_ref, bf16[3,2,1088,256]{3,2,1,0:T(8,128)(2,1)} %attn_bwd.4.refs_in_0_, bf16[3,2,1088,256]{3,2,1,0:T(8,128)(2,1)} %attn_bwd.5.refs_in_1_, bf16[3,2,1088,256]{3,2,1,0:T(8,128)(2,1)} %attn_bwd.6.refs_in_2_, ...), custom_call_target="tpu_custom_call" | custom-call | tf_op jit(solution)/shard_map/project_back/pallas_call | solution.py:506
  538.6 12.1 %project_back.4 = (f32[2,1088,1024]{2,1,0:T(8,128)}, f32[4,8,1024]{2,1,0:T(8,128)}) custom-call(s32[6]{0:T(128)} %stack.61.starts_ref, bf16[3,2,1088,256]{3,2,1,0:T(8,128)(2,1)} %attn_bwd.4.refs_in_0_, bf16[3,2,1088,256]{3,2,1,0:T(8,128)(2,1)} %attn_bwd.5.refs_in_1_, ...), custom_call_target="tpu_custom_call", output_to_operand_aliasing={{0}: (15, {}), {1}: (16, {})} | custom-call | tf_op jit(solution)/shard_map/project_back/pallas_call | solution.py:506
  553.4 12.4 %project_back.5 = (f32[2,1088,1024]{2,1,0:T(8,128)}, f32[4,8,1024]{2,1,0:T(8,128)}) custom-call(s32[6]{0:T(128)} %stack.61.starts_ref, bf16[3,2,1088,256]{3,2,1,0:T(8,128)(2,1)} %attn_bwd.4.refs_in_0_, bf16[3,2,1088,256]{3,2,1,0:T(8,128)(2,1)} %attn_bwd.5.refs_in_1_, ...), custom_call_target="tpu_custom_call", output_to_operand_aliasing={{0}: (15, {}), {1}: (16, {})} | custom-call | tf_op jit(solution)/shard_map/project_back/pallas_call | solution.py:506
  578.4 7.4 %in_rows.3 = f32[512,4096]{1,0:T(8,128)} custom-call(bf16[16,4,32,1024]{3,2,1,0:T(8,128)(2,1)} %bitcast.216), custom_call_target="tpu_custom_call" | custom-call | tf_op jit(solution)/shard_map/in_rows/pallas_call | solution.py:820
  (267 shorter events, 176.1 us)
Async XLA Ops:
  7.2 122.8 %all-gather.6.cloned.1.call-start = ((), (), s32[]{:S(2)}) async-start(), calls=%async_computation | async-start | bytes 4456448 | tf_op jit(solution)/shard_map/all_gather | solution.py:724
  15.6 24.2 %collective-permute-start.1 = (bf16[3,256,512]{2,1,0:T(8,128)(2,1)}, bf16[3,256,512]{2,1,0:T(8,128)(2,1)S(1)}, u32[]{:S(2)}, u32[]{:S(2)}) collective-permute-start(bf16[3,256,512]{2,1,0:T(8,128)(2,1)} %get-tuple-element.168), channel_id=1, source_target_pairs={{0,1},{1,0},{2,3},{3,2},{4,5},{5,4},{6,7},{7,6},{8,9},{9,8},{10,11... | collective-permute-start | bytes 2359304 | tf_op jit(solution)/shard_map/ppermute | solution.py:636
  39.9 25.9 %collective-permute-start.2 = (bf16[3,256,512]{2,1,0:T(8,128)(2,1)S(1)}, bf16[3,256,512]{2,1,0:T(8,128)(2,1)S(1)}, u32[]{:S(2)}, u32[]{:S(2)}) collective-permute-start(bf16[3,256,512]{2,1,0:T(8,128)(2,1)S(1)} %copy-done.23), channel_id=1, source_target_pairs={{0,1},{1,0},{2,3},{3,2},{4,5},{5,4},{6,7},{7,6},{8,9},{9,8},{10,11... | collective-permute-start | bytes 2359304 | tf_op jit(solution)/shard_map/ppermute | solution.py:636
  42.0 23.9 %collective-permute-start.3 = (bf16[128,1024]{1,0:T(8,128)(2,1)S(1)}, bf16[128,1024]{1,0:T(8,128)(2,1)}, u32[]{:S(2)}, u32[]{:S(2)}) collective-permute-start(bf16[128,1024]{1,0:T(8,128)(2,1)S(1)} %dynamic-slice_bitcast_fusion.3), channel_id=1, source_target_pairs={{0,1},{1,0},{2,3},{3,2},{4,5},{5,4},{6,7},{7,6},{8,9},{9,8},{10,11... | collective-permute-start | bytes 786440 | tf_op jit(solution)/shard_map/ppermute | solution.py:636
  65.9 428.5 %all-gather.8.cloned.1.call-start = ((), (), s32[]{:S(2)}) async-start(), calls=%async_computation.1 | async-start | bytes 4456448 | tf_op jit(solution)/shard_map/all_gather | solution.py:867
  65.9 58.9 %collective-permute-start.6 = (bf16[256,4096]{1,0:T(8,128)(2,1)}, bf16[256,4096]{1,0:T(8,128)(2,1)}, u32[]{:S(2)}, u32[]{:S(2)}) collective-permute-start(bf16[256,4096]{1,0:T(8,128)(2,1)} %constant_dynamic-slice_fusion.2), channel_id=1, source_target_pairs={{0,1},{1,0},{2,3},{3,2},{4,5},{5,4},{6,7},{7,6},{8,9},{9,8},{10,11... | collective-permute-start | bytes 6291464 | tf_op jit(solution)/shard_map/ppermute | solution.py:636
  67.7 20.0 %collective-permute-start.5 = (bf16[3,256,512]{2,1,0:T(8,128)(2,1)S(1)}, bf16[3,256,512]{2,1,0:T(8,128)(2,1)S(1)}, u32[]{:S(2)}, u32[]{:S(2)}) collective-permute-start(bf16[3,256,512]{2,1,0:T(8,128)(2,1)S(1)} %collective-permute-done.2.rest_1_.refs_in_12_), channel_id=1, source_target_pairs={{0,2},{2,0},{4,6},{6,4},{8,10},{10,8},{12,14},{14,12},{16,18},{18,... | collective-permute-start | bytes 2359304 | tf_op jit(solution)/shard_map/ppermute | solution.py:636
  67.7 57.0 %collective-permute-start.7 = (bf16[256,1024]{1,0:T(8,128)(2,1)}, bf16[256,1024]{1,0:T(8,128)(2,1)S(1)}, u32[]{:S(2)}, u32[]{:S(2)}) collective-permute-start(bf16[256,1024]{1,0:T(8,128)(2,1)} %constant_dynamic-slice_fusion.3), channel_id=1, source_target_pairs={{0,1},{1,0},{2,3},{3,2},{4,5},{5,4},{6,7},{7,6},{8,9},{9,8},{10,11... | collective-permute-start | bytes 1572872 | tf_op jit(solution)/shard_map/ppermute | solution.py:636
  263.1 62.0 %collective-permute-start.12 = (bf16[1,1024,1024]{2,1,0:T(8,128)(2,1)}, bf16[1,1024,1024]{2,1,0:T(8,128)(2,1)}, u32[]{:S(2)}, u32[]{:S(2)}) collective-permute-start(bf16[1,1024,1024]{2,1,0:T(8,128)(2,1)} %get-tuple-element.204), channel_id=1, source_target_pairs={{0,1},{1,0},{2,3},{3,2},{4,5},{5,4},{6,7},{7,6},{8,9},{9,8},{10,11... | collective-permute-start | bytes 6291464 | tf_op jit(solution)/shard_map/ppermute | solution.py:636
  328.6 64.9 %collective-permute-start.15 = (bf16[4,256,1024]{2,1,0:T(8,128)(2,1)}, bf16[4,256,1024]{2,1,0:T(8,128)(2,1)}, u32[]{:S(2)}, u32[]{:S(2)}) collective-permute-start(bf16[4,256,1024]{2,1,0:T(8,128)(2,1)} %get-tuple-element.216), channel_id=1, source_target_pairs={{0,1},{1,0},{2,3},{3,2},{4,5},{5,4},{6,7},{7,6},{8,9},{9,8},{10,11... | collective-permute-start | bytes 6291464 | tf_op jit(solution)/shard_map/ppermute | solution.py:636
  336.3 20.8 %collective-permute-start.14 = (bf16[2,1,256,1024]{3,2,1,0:T(8,128)(2,1)}, bf16[2,1,256,1024]{3,2,1,0:T(8,128)(2,1)S(1)}, u32[]{:S(2)}, u32[]{:S(2)}) collective-permute-start(bf16[2,1,256,1024]{3,2,1,0:T(8,128)(2,1)} %grad_blocks.14), channel_id=1, source_target_pairs={{0,2},{2,0},{4,6},{6,4},{8,10},{10,8},{12,14},{14,12},{16,18},{18,... | collective-permute-start | bytes 3145736 | tf_op jit(solution)/shard_map/ppermute | solution.py:636
  336.3 25.8 %collective-permute-start.13 = (bf16[1,512,1024]{2,1,0:T(8,128)(2,1)}, bf16[1,512,1024]{2,1,0:T(8,128)(2,1)S(1)}, u32[]{:S(2)}, u32[]{:S(2)}) collective-permute-start(bf16[1,512,1024]{2,1,0:T(8,128)(2,1)} %get-tuple-element.215), channel_id=1, source_target_pairs={{0,4},{2,6},{4,0},{6,2},{8,12},{10,14},{12,8},{14,10},{16,20},{18,... | collective-permute-start | bytes 3145736 | tf_op jit(solution)/shard_map/ppermute | solution.py:636
  370.7 22.8 %collective-permute-start.17 = (bf16[1,256,1024]{2,1,0:T(8,128)(2,1)}, bf16[1,256,1024]{2,1,0:T(8,128)(2,1)}, u32[]{:S(2)}, u32[]{:S(2)}) collective-permute-start(bf16[1,256,1024]{2,1,0:T(8,128)(2,1)} %get-tuple-element.223), channel_id=1, source_target_pairs={{0,1},{1,0},{2,3},{3,2},{4,5},{5,4},{6,7},{7,6},{8,9},{9,8},{10,11... | collective-permute-start | bytes 1572872 | tf_op jit(solution)/shard_map/ppermute | solution.py:636
  372.3 21.2 %collective-permute-start.16 = (bf16[1,256,1024]{2,1,0:T(8,128)(2,1)}, bf16[1,256,1024]{2,1,0:T(8,128)(2,1)S(1)}, u32[]{:S(2)}, u32[]{:S(2)}) collective-permute-start(bf16[1,256,1024]{2,1,0:T(8,128)(2,1)} %get-tuple-element.337), channel_id=1, source_target_pairs={{0,8},{2,10},{4,12},{6,14},{8,0},{10,2},{12,4},{14,6},{16,24},{18,... | collective-permute-start | bytes 1572872 | tf_op jit(solution)/shard_map/ppermute | solution.py:636
  410.0 25.9 %collective-permute-start.21 = (bf16[2,3,256,512]{3,2,1,0:T(8,128)(2,1)}, bf16[2,3,256,512]{3,2,1,0:T(8,128)(2,1)S(1)}, u32[]{:S(2)}, u32[]{:S(2)}) collective-permute-start(bf16[2,3,256,512]{3,2,1,0:T(8,128)(2,1)} %grad_blocks.16), channel_id=1, source_target_pairs={{0,2},{2,0},{4,6},{6,4},{8,10},{10,8},{12,14},{14,12},{16,18},{18,... | collective-permute-start | bytes 4718600 | tf_op jit(solution)/shard_map/ppermute | solution.py:636
  410.0 25.9 %collective-permute-start.19 = (bf16[4,128,1024]{2,1,0:T(8,128)(2,1)}, bf16[4,128,1024]{2,1,0:T(8,128)(2,1)}, u32[]{:S(2)}, u32[]{:S(2)}) collective-permute-start(bf16[4,128,1024]{2,1,0:T(8,128)(2,1)} %get-tuple-element.230), channel_id=1, source_target_pairs={{0,4},{2,6},{4,0},{6,2},{8,12},{10,14},{12,8},{14,10},{16,20},{18,... | collective-permute-start | bytes 3145736 | tf_op jit(solution)/shard_map/ppermute | solution.py:636
  410.5 22.2 %collective-permute-start.20 = (bf16[1,128,1024]{2,1,0:T(8,128)(2,1)S(1)}, bf16[1,128,1024]{2,1,0:T(8,128)(2,1)}, u32[]{:S(2)}, u32[]{:S(2)}) collective-permute-start(bf16[1,128,1024]{2,1,0:T(8,128)(2,1)S(1)} %fusion.8), channel_id=1, source_target_pairs={{0,16},{2,18},{4,20},{6,22},{8,24},{10,26},{12,28},{14,30},{16,0},... | collective-permute-start | bytes 786440 | tf_op jit(solution)/shard_map/ppermute | solution.py:636
  413.1 19.7 %collective-permute-start.22 = (bf16[1,64,1024]{2,1,0:T(8,128)(2,1)}, bf16[1,64,1024]{2,1,0:T(8,128)(2,1)}, u32[]{:S(2)}, u32[]{:S(2)}) collective-permute-start(bf16[1,64,1024]{2,1,0:T(8,128)(2,1)} %get-tuple-element.236), channel_id=1, source_target_pairs={{0,8},{2,10},{4,12},{6,14},{8,0},{10,2},{12,4},{14,6},{16,24},{18,... | collective-permute-start | bytes 393224 | tf_op jit(solution)/shard_map/ppermute | solution.py:636
  441.0 137.3 %all-gather.10.cloned.1.call-start = ((), (), s32[]{:S(2)}) async-start(), calls=%async_computation.2 | async-start | bytes 4456448 | tf_op jit(solution)/shard_map/all_gather | solution.py:867
  453.5 20.7 %collective-permute-start.25 = (bf16[3,256,512]{2,1,0:T(8,128)(2,1)}, bf16[3,256,512]{2,1,0:T(8,128)(2,1)S(1)}, u32[]{:S(2)}, u32[]{:S(2)}) collective-permute-start(bf16[3,256,512]{2,1,0:T(8,128)(2,1)} %get-tuple-element.248), channel_id=1, source_target_pairs={{0,1},{1,0},{2,3},{3,2},{4,5},{5,4},{6,7},{7,6},{8,9},{9,8},{10,11... | collective-permute-start | bytes 2359304 | tf_op jit(solution)/shard_map/ppermute | solution.py:636
  454.1 20.1 %collective-permute-start.24 = (bf16[4,64,1024]{2,1,0:T(8,128)(2,1)}, bf16[4,64,1024]{2,1,0:T(8,128)(2,1)S(1)}, u32[]{:S(2)}, u32[]{:S(2)}) collective-permute-start(bf16[4,64,1024]{2,1,0:T(8,128)(2,1)} %get-tuple-element.241), channel_id=1, source_target_pairs={{0,8},{2,10},{4,12},{6,14},{8,0},{10,2},{12,4},{14,6},{16,24},{18,... | collective-permute-start | bytes 1572872 | tf_op jit(solution)/shard_map/ppermute | solution.py:636
  488.4 21.0 %collective-permute-start.30 = (bf16[3,128,512]{2,1,0:T(8,128)(2,1)}, bf16[3,128,512]{2,1,0:T(8,128)(2,1)S(1)}, u32[]{:S(2)}, u32[]{:S(2)}) collective-permute-start(bf16[3,128,512]{2,1,0:T(8,128)(2,1)} %get-tuple-element.257), channel_id=1, source_target_pairs={{0,4},{2,6},{4,0},{6,2},{8,12},{10,14},{12,8},{14,10},{16,20},{18,... | collective-permute-start | bytes 1179656 | tf_op jit(solution)/shard_map/ppermute | solution.py:636
  512.5 21.1 %collective-permute-start.32 = (bf16[3,256,512]{2,1,0:T(8,128)(2,1)}, bf16[3,256,512]{2,1,0:T(8,128)(2,1)S(1)}, u32[]{:S(2)}, u32[]{:S(2)}) collective-permute-start(bf16[3,256,512]{2,1,0:T(8,128)(2,1)} %get-tuple-element.270), channel_id=1, source_target_pairs={{0,1},{1,0},{2,3},{3,2},{4,5},{5,4},{6,7},{7,6},{8,9},{9,8},{10,11... | collective-permute-start | bytes 2359304 | tf_op jit(solution)/shard_map/ppermute | solution.py:636
  514.0 19.6 %collective-permute-start.34 = (bf16[1,256,1024]{2,1,0:T(8,128)(2,1)S(1)}, bf16[1,256,1024]{2,1,0:T(8,128)(2,1)S(1)}, u32[]{:S(2)}, u32[]{:S(2)}) collective-permute-start(bf16[1,256,1024]{2,1,0:T(8,128)(2,1)S(1)} %maximum_select_fusion.2.refs_0_), channel_id=1, source_target_pairs={{0,2},{2,0},{4,6},{6,4},{8,10},{10,8},{12,14},{14,12},{16,18},{18,... | collective-permute-start | bytes 1572872 | tf_op jit(solution)/shard_map/ppermute | solution.py:636
  (69 other events, 725.7 us)
Sparse Core Ops, SparseCore 0:
  66.0 52.2 all-gather.5
  441.1 53.1 all-gather.7
  512.6 56.8 all-gather.9
